TPU v7x, 32 devices: a whole 2x2x4 slice. The times are simulated.
32 devices in a mesh: row: 8 (over y, x, core), col: 4 (over z).
Axes of the slice: x: 2, y: 2, z: 4, core: 2. Of those that a mesh axis runs over, the one named last changes fastest.
Arguments:
- fields: float32 [4, 16, 64, 512], P(None, 'row', None, 'col'), may hold values from -6 to 6
- diffusivity: float32 [4], replicated, may hold values from 0.05 to 0.3
- records: float32 [6, 262144], P(None, ('row', 'col')), may hold values from -6 to 6
- response_time: float32 [262144], P(('row', 'col')), may hold values from 0.5 to 4
- cell_index: int32 [262144], P(('row', 'col')), may hold values from 0 to 16383
- counts: int32 [32], P(('row', 'col')), may hold values from 4096 to 8192, as said below
- destination: int32 [262144], P(('row', 'col')), may hold values from 0 to 4, as said below
- slot: int32 [262144], P(('row', 'col')), may hold values from 0 to 255, as said below
Outputs:
- tendency: float32 [4, 16, 64, 512], P(None, 'row', None, 'col')
- kept: float32 [6, 262144], P(None, ('row', 'col'))
- arrivals: float32 [4, 6, 8192], P(None, None, ('row', 'col'))
Inputs may be any that keep to these rules, and one draw needn't show every extreme that they name: `counts`: both wall rows of pencils are full. `destination`: only live particles leave; none leaves row index 0 downward or row index 7 upward. For each pencil and direction the leaving particles' slots are distinct; pencil 0 sends exactly 256 particles toward col index + 1; slot is 0 for particles that stay.
All inputs are finite; a program needn't handle non-finite values.
Results may differ from a plain program's by a relative error of at most 0.00009.
Values sent between devices are 32-bit elements; how exact they have to be, the bound alone decides.
No kernel may reach another device: no remote copies, remote signals or barrier semaphores. Data moves between devices by JAX's collectives and lax.ppermute only.
A program may use at most 192 MiB of HBM per device.

v0:
```python
import math

import jax
import jax.numpy as jnp
from jax import lax
from jax.sharding import PartitionSpec as P

PART_DEV = 8192
MIG = 256


time_step = 0.2
coupling = 0.5
stretch = 1.5


def shifted(value, axis, steps):
    count = lax.axis_size(axis)
    first, last = (max(0, -steps), min(count, count - steps))
    return lax.ppermute(value, axis, [(source, source + steps) for source in range(first, last)])


def from_behind(block, axis, distance):
    devices = range(lax.axis_size(axis))
    route = [((i - distance) % len(devices), i) for i in devices]
    return lax.ppermute(block, axis, route)


def periodic_compact(points):
    index = jnp.arange(points, dtype=jnp.int32)
    offset = (index[None, :] - index[:, None]) % points
    lhs = jnp.where(offset == 0, 1.0, 0.0) + jnp.where(
        (offset == 1) | (offset == points - 1), 1.0 / 3.0, 0.0
    )
    rhs = jnp.where(offset == 1, 7.0 / 9.0, 0.0) - jnp.where(offset == points - 1, 7.0 / 9.0, 0.0)
    rhs = (
        rhs
        + jnp.where(offset == 2, 1.0 / 36.0, 0.0)
        - jnp.where(offset == points - 2, 1.0 / 36.0, 0.0)
    )
    factor = jnp.linalg.cholesky(lhs.astype(jnp.float32))
    return jax.scipy.linalg.cho_solve((factor, True), rhs.astype(jnp.float32))


def wall_compact(points):
    index = jnp.arange(points, dtype=jnp.int32)
    first = index == 0
    final = index == points - 1
    near = (index == 1) | (index == points - 2)
    lower = jnp.where(first, 0.0, jnp.where(final, 2.0, jnp.where(near, 0.25, 1.0 / 3.0))).astype(
        jnp.float32
    )
    upper = jnp.where(final, 0.0, jnp.where(first, 2.0, jnp.where(near, 0.25, 1.0 / 3.0))).astype(
        jnp.float32
    )
    middle = jnp.ones((points,), jnp.float32)
    offset = index[None, :] - index[:, None]
    inner = jnp.where(offset == 1, 7.0 / 9.0, 0.0) - jnp.where(offset == -1, 7.0 / 9.0, 0.0)
    inner = (
        inner + jnp.where(offset == 2, 1.0 / 36.0, 0.0) - jnp.where(offset == -2, 1.0 / 36.0, 0.0)
    )
    padde_rows = jnp.where(offset == 1, 0.75, 0.0) - jnp.where(offset == -1, 0.75, 0.0)
    top_row = (
        jnp.where(offset == 0, -2.5, 0.0)
        + jnp.where(offset == 1, 2.0, 0.0)
        + jnp.where(offset == 2, 0.5, 0.0)
    )
    end_row = (
        jnp.where(offset == 0, 2.5, 0.0)
        - jnp.where(offset == -1, 2.0, 0.0)
        - jnp.where(offset == -2, 0.5, 0.0)
    )
    rhs = jnp.where(
        first[:, None],
        top_row,
        jnp.where(final[:, None], end_row, jnp.where(near[:, None], padde_rows, inner)),
    )
    solved = lax.linalg.tridiagonal_solve(lower, middle, upper, rhs.astype(jnp.float32))
    coord = -1.0 + 2.0 * index.astype(jnp.float32) / (points - 1)
    slope = stretch * (1.0 - jnp.tanh(stretch * coord) ** 2) / math.tanh(stretch)
    return solved / slope[:, None]


def spectral_matrix(points):
    index = jnp.arange(points, dtype=jnp.int32)
    offset = index[:, None] - index[None, :]
    parity = (1 - 2 * (offset % 2)).astype(jnp.float32)
    angle = math.pi * offset.astype(jnp.float32) / points
    safe_angle = jnp.where(offset == 0, 1.0, angle)
    value = math.pi / points * parity * jnp.cos(safe_angle) / jnp.sin(safe_angle)
    return jnp.where(offset == 0, 0.0, value)


def spanwise_terms(pencil_data, viscous):
    highest = lax.Precision.HIGHEST
    deriv_z = spectral_matrix(pencil_data.shape[3])
    second_z = jnp.dot(deriv_z, deriv_z, precision=highest)
    along_z = jnp.einsum("ij,cabj->cabi", deriv_z, pencil_data, precision=highest)
    curve_z = jnp.einsum("ij,cabj->cabi", second_z, pencil_data, precision=highest)
    return -pencil_data[2] * along_z + viscous * curve_z


def on_device(fields, diffusivity, records, response_time, cell_index, counts, destination, slot):
    highest = lax.Precision.HIGHEST
    viscous = diffusivity[:, None, None, None]
    planes = fields.shape[2]
    deriv_x = periodic_compact(planes)
    second_x = jnp.dot(deriv_x, deriv_x, precision=highest)
    along_x = jnp.einsum("ij,cyjz->cyiz", deriv_x, fields, precision=highest)
    curve_x = jnp.einsum("ij,cyjz->cyiz", second_x, fields, precision=highest)
    partial_x = -fields[0] * along_x + viscous * curve_x
    local = jnp.arange(PART_DEV, dtype=jnp.int32)
    live = local < counts[0]
    flat_speed = fields[0:3].reshape(3, -1)
    fluid = jnp.take(flat_speed, cell_index, axis=1)
    drag = (fluid - records[3:6]) / response_time
    velocity = records[3:6] + time_step * drag
    moved_pos = records[0:3] + time_step * velocity
    moved = jnp.concatenate([moved_pos, velocity], axis=0)
    force = jnp.where(live[None, :], -coupling * drag, 0.0)
    deposit = (
        jnp.zeros_like(flat_speed)
        .at[:, cell_index]
        .add(force)
        .reshape(3, fields.shape[1], fields.shape[2], fields.shape[3])
    )
    partial_x = partial_x.at[0:3].add(deposit)
    normal_pencil = lax.all_to_all(fields, "row", split_axis=2, concat_axis=1, tiled=True)
    deriv_y = wall_compact(normal_pencil.shape[1])
    second_y = jnp.dot(deriv_y, deriv_y, precision=highest)
    along_y = jnp.einsum("ij,cjxz->cixz", deriv_y, normal_pencil, precision=highest)
    curve_y = jnp.einsum("ij,cjxz->cixz", second_y, normal_pencil, precision=highest)
    partial_y = -normal_pencil[1] * along_y + viscous * curve_y
    span_pencil = lax.all_to_all(normal_pencil, "col", split_axis=1, concat_axis=3, tiled=True)
    partial_z = spanwise_terms(span_pencil, viscous)
    partial_y = partial_y + lax.all_to_all(
        partial_z, "col", split_axis=3, concat_axis=1, tiled=True
    )
    tendency = partial_x + lax.all_to_all(partial_y, "row", split_axis=1, concat_axis=2, tiled=True)
    staying = live & (destination == 0)
    kept = jnp.where(staying[None, :], moved, 0.0)
    leaving = live & (destination > 0)
    target = jnp.where(leaving, (destination - 1) * MIG + slot, 4 * MIG)
    outgoing = (
        jnp.zeros((6, 4 * MIG + 1), jnp.float32)
        .at[:, target]
        .add(jnp.where(leaving[None, :], moved, 0.0))
    )
    outgoing = outgoing[:, : 4 * MIG].reshape(6, 4, MIG)
    received = []
    for direction, offset in ((0, 1), (1, -1)):
        received.append(shifted(outgoing[:, direction], "row", offset))
    for direction, offset in ((2, 1), (3, -1)):
        received.append(from_behind(outgoing[:, direction], "col", offset))
    arrivals = jnp.stack(received, axis=0)
    return (tendency, kept, arrivals)


def solution(mesh):
    return jax.shard_map(
        on_device,
        mesh=mesh,
        in_specs=(
            P(None, "row", None, "col"),
            P(),
            P(None, ("row", "col")),
            P(("row", "col")),
            P(("row", "col")),
            P(("row", "col")),
            P(("row", "col")),
            P(("row", "col")),
        ),
        out_specs=(
            P(None, "row", None, "col"),
            P(None, ("row", "col")),
            P(None, None, ("row", "col")),
        ),
        check_vma=False,
    )
```

profile of v0, /device:TPU:0, one launch (start us, length us, event | category | flops | bytes accessed | tf_op | source)
XLA Modules:
  0.0 283.9 jit_solution(7045374825839742556)
XLA Ops:
  0.6 1.8 copy.109
  2.5 5.2 %all-to-all-start = ((f32[4,2,64,128]{3,0,1,2:T(4,128)}), f32[4,2,64,128]{3,0,1,2:T(4,128)S(1)}, u32[]{:S(2)}, u32[]{:S(2)}) async-start(f32[4,2,64,128]{3,0,1,2:T(4,128)} %copy.109), calls=%async_computation | async-start | bytes 524288 | tf_op jit(solution)/shard_map/all_to_all | solution.py:128
  7.6 0.9 slice.750
  8.6 0.8 broadcast_clamp_fusion
  9.3 0.8 compare_and_fusion.2
  10.1 4.6 %copy.105 = f32[3,2,64,128]{0,3,2,1:T(8,128)} copy(f32[3,2,64,128]{3,2,1,0:T(8,128)S(1)} %slice.750) | data formatting | bytes 393216 | tf_op jit(solution)/shard_map/slice | solution.py:114
  14.8 31.2 %gather_fusion = f32[8192,3]{1,0:T(8,128)} fusion(f32[3,16384]{0,1:T(8,128)} %bitcast.151, s32[8192]{0:T(1024)S(1)} %get-tuple-element.76), kind=kCustom, calls=%fused_computation | custom fusion | bytes 229376 | tf_op jit(solution)/shard_map/jit(_take)/gather | solution.py:115
  45.9 2.8 %copy.106 = f32[8192,3]{0,1:T(4,128)S(1)} copy(f32[8192,3]{1,0:T(8,128)} %gather_fusion) | data formatting | bytes 196608 | tf_op jit(solution)/shard_map/jit(_take)/gather | solution.py:115
  49.5 0.1 multiply_add_fusion
  49.6 0.0 copy-start
  49.6 0.8 select_bitcast_fusion
  50.4 2.6 copy.119
  53.1 52.9 %scatter_custom_fusion.1 = f32[6,1025]{0,1:T(8,128)S(1)} fusion(s32[8192]{0:T(1024)S(1)} %compare_select_fusion, f32[8192,6]{1,0:T(8,128)} %copy.119, f32[]{:T(128)} %constant.167.clone.1), kind=kCustom, calls=%fused_computation.40 | custom fusion | flops 49152 | bytes 25112 | tf_op jit(solution)/shard_map/scatter-add | solution.py:147
  106.1 0.1 copy.136
  106.2 4.7 %collective-permute-start.3 = (f32[6,256]{1,0:T(8,128)S(1)}, f32[6,256]{1,0:T(8,128)S(1)}, u32[]{:S(2)}, u32[]{:S(2)}) collective-permute-start(f32[6,256]{1,0:T(8,128)S(1)} %bitcast.164), channel_id=1, source_target_pairs={{1,0},{2,1},{3,2},{0,3},{5,4},{6,5},{7,6},{4,7},{9,8},{10,9},{11,1... | collective-permute-start | bytes 18440 | tf_op jit(solution)/shard_map/ppermute | solution.py:26
  110.9 0.1 copy.135
  111.0 0.0 collective-permute-start.2
  111.0 0.1 copy.134
  111.1 1.3 collective-permute-start.1
  112.4 0.1 copy.133
  112.5 3.0 %collective-permute-start = (f32[6,256]{1,0:T(8,128)S(1)}, f32[6,256]{1,0:T(8,128)S(1)}, u32[]{:S(2)}, u32[]{:S(2)}) collective-permute-start(f32[6,256]{1,0:T(8,128)S(1)} %bitcast.167), channel_id=1, source_target_pairs={{0,4},{4,8},{8,12},{12,16},{16,20},{20,24},{24,28},{1,5},{5,9},{9,... | collective-permute-start | bytes 18440 | tf_op jit(solution)/shard_map/ppermute | solution.py:20
  115.6 5.8 %cholesky.15 = f32[64,64]{1,0:T(8,128)S(1)} custom-call(f32[64,64]{1,0:T(8,128)S(1)} %add_multiply_fusion), custom_call_target="Cholesky" | custom-call | tf_op jit(solution)/shard_map/jit(cholesky)/cholesky | solution.py:41
  121.5 0.6 compare_reduce_fusion
  122.2 0.7 fusion.35
  122.8 4.9 %custom-call.10 = f32[1,64,64]{1,2,0:T(8,128)S(1)} custom-call(f32[1,64,64]{2,1,0:T(8,128)S(1)} %fusion.35), custom_call_target="InvertDiagBlocksLowerTriangular" | custom-call | tf_op jit(solution)/shard_map/jit(_cho_solve)/triangular_solve | solution.py:42
  127.7 0.3 fusion.41
  128.0 0.2 fusion.39
  128.2 0.2 convolution_bitcast_fusion.3
  128.3 0.4 fusion.7
  128.7 0.7 fusion.122
  129.4 0.7 fusion.121
  147.7 0.1 select_bitcast_fusion.1
  147.8 0.4 fusion.6
  148.2 0.1 select_select_fusion.1
  148.2 8.8 %fusion.70 = (f32[1,16]{1,0:T(1,128)S(1)}, f32[1,16]{1,0:T(1,128)S(1)}, f32[1,16]{1,0:T(1,128)S(1)}, f32[1,16]{1,0:T(1,128)S(1)}, f32[1,16]{1,0:T(1,128)S(1)}, /...) fusion(f32[16,16]{1,0:T(8,128)S(1)} %select_select_fusion.1, ...), kind=kLoop, calls=%fused_computation.124 | loop fusion | flops 672 | bytes 1968 | tf_op jit(solution)/shard_map/eval_jaxpr/div | solution.py:78
  158.4 1.3 multiply_subtract_fusion
  159.7 0.1 copy.149
  159.8 0.8 copy.111
  160.6 5.1 %all-to-all-start.1 = ((f32[4,16,8,128]{3,2,0,1:T(8,128)}), f32[4,16,8,128]{3,2,0,1:T(8,128)S(1)}, u32[]{:S(2)}, u32[]{:S(2)}) async-start(f32[4,16,8,128]{3,2,0,1:T(8,128)} %copy.111), calls=%async_computation.1 | async-start | bytes 524288 | tf_op jit(solution)/shard_map/all_to_all | solution.py:134
  165.7 2.7 copy.107
  168.3 48.0 %scatter_custom_fusion = f32[3,16384]{0,1:T(8,128)} fusion(s32[8192]{0:T(1024)S(1)} %get-tuple-element.77, f32[8192,3]{1,0:T(8,128)} %copy.107, f32[]{:T(128)} %constant.167.clone.1), kind=kCustom, calls=%fused_computation.3 | custom fusion | flops 24576 | bytes 197120 | tf_op jit(solution)/shard_map/scatter-add | solution.py:124
  216.4 5.4 %copy.131 = f32[3,2,64,128]{3,2,1,0:T(8,128)S(1)} copy(f32[3,2,64,128]{0,3,2,1:T(8,128)} %bitcast.148) | data formatting | bytes 393216 | tf_op jit(solution)/shard_map/reshape.45
  221.8 0.1 concatenate.8
  221.8 0.2 convolution_bitcast_fusion.4
  222.0 6.0 %convolution_bitcast_fusion = f32[512,512,1,1]{1,0,3,2:T(8,128)S(1)} fusion(), kind=kOutput, calls=%fused_computation.8 | convolution fusion | flops 1616642048 | bytes 1048576 | tf_op jit(solution)/shard_map/dot_general | solution.py:97
  228.1 1.2 fusion.10
  229.3 5.5 %fusion.9 = f32[4,4,8,512]{3,2,1,0:T(8,128)S(1)} fusion(f32[4,4,8,512]{3,2,1,0:T(8,128)S(1)} %fusion.10, f32[4,4,8,4,128]{4,2,0,1,3:T(8,128)S(1)} %bitcast.157, f32[4,8,512]{2,1,0:T(8,128)S(1)} %copy_bitcast_fusion), kind=kOutput, calls=%fused_computation.21 | convolution fusion | flops 408813568 | bytes 851968 | tf_op jit(solution)/shard_map/ij,cabj->cabi/dot_general | solution.py:98
  234.8 3.2 %copy.115 = f32[4,4,8,512]{2,1,0,3:T(4,128)} copy(f32[4,4,8,512]{3,2,1,0:T(8,128)S(1)} %fusion.9) | data formatting | bytes 524288 | tf_op jit(solution)/shard_map/add | solution.py:100
  238.1 7.2 %reshape.160 = f32[4,1,16384]{2,1,0:T(1,128)} reshape(f32[512,4,4,8]{3,2,1,0:T(4,128)} %bitcast.149) | data formatting | bytes 524288
  245.2 5.1 %all-to-all-start.2 = ((f32[4,1,16384]{2,1,0:T(1,128)}), f32[4,1,16384]{2,1,0:T(1,128)S(1)}, u32[]{:S(2)}, u32[]{:S(2)}) async-start(f32[4,1,16384]{2,1,0:T(1,128)} %reshape.160), calls=%async_computation.2 | async-start | bytes 524288 | tf_op jit(solution)/shard_map/all_to_all | solution.py:136
  250.3 0.4 convolution_multiply_fusion.1
  250.8 8.6 %all-to-all-done.2 = f32[4,1,16384]{2,1,0:T(1,128)S(1)} async-done(((f32[4,1,16384]{2,1,0:T(1,128)}), f32[4,1,16384]{2,1,0:T(1,128)S(1)}, u32[]{:S(2)}, u32[]{:S(2)}) %all-to-all-start.2) | async-done | bytes 262176 | tf_op jit(solution)/shard_map/all_to_all | solution.py:136
  259.4 0.5 broadcast.928
  259.9 1.4 reduce.8
  261.3 7.0 %reshape.161 = f32[512,4,4,8]{3,2,1,0:T(4,128)} reshape(f32[4,16384]{1,0:T(4,128)S(1)} %reduce.8) | data formatting | bytes 524288
  268.2 3.5 %copy.116 = f32[4,4,8,4,128]{4,1,3,2,0:T(4,128)S(1)} copy(f32[4,4,8,4,128]{2,1,0,4,3:T(4,128)} %bitcast.150) | data formatting | bytes 524288 | tf_op jit(solution)/shard_map/all_to_all | solution.py:136
  271.7 0.4 fusion.4
  272.1 0.8 copy.117
  272.9 3.4 %all-to-all-start.3 = ((f32[4,16,8,128]{3,2,0,1:T(8,128)}), f32[4,16,8,128]{3,2,0,1:T(8,128)S(1)}, u32[]{:S(2)}, u32[]{:S(2)}) async-start(f32[4,16,8,128]{3,2,0,1:T(8,128)} %copy.117), calls=%async_computation.3 | async-start | bytes 524288 | tf_op jit(solution)/shard_map/all_to_all | solution.py:139
  276.4 0.0 collective-permute-done.3
  276.4 0.0 collective-permute-done.1
  276.4 0.6 copy.124
  277.0 6.2 %all-to-all-done.3 = f32[4,16,8,128]{3,2,0,1:T(8,128)S(1)} async-done(((f32[4,16,8,128]{3,2,0,1:T(8,128)}), f32[4,16,8,128]{3,2,0,1:T(8,128)S(1)}, u32[]{:S(2)}, u32[]{:S(2)}) %all-to-all-start.3) | async-done | bytes 262176 | tf_op jit(solution)/shard_map/all_to_all | solution.py:139
  283.2 0.7 bitcast_add_fusion
  (32 shorter events, 0.4 us)
Async XLA Ops:
  2.5 157.2 %all-to-all-start = ((f32[4,2,64,128]{3,0,1,2:T(4,128)}), f32[4,2,64,128]{3,0,1,2:T(4,128)S(1)}, u32[]{:S(2)}, u32[]{:S(2)}) async-start(f32[4,2,64,128]{3,0,1,2:T(4,128)} %copy.109), calls=%async_computation | async-start | bytes 524288 | tf_op jit(solution)/shard_map/all_to_all | solution.py:128
  14.7 34.7 %copy-start.2 = (s32[8192]{0:T(1024)S(1)}, s32[8192]{0:T(1024)}, u32[]{:S(2)}) copy-start(s32[8192]{0:T(1024)} %param.16) | copy-start | bytes 98308
  14.7 34.7 %copy-start.1 = (f32[6,8192]{1,0:T(8,128)S(1)}, f32[6,8192]{1,0:T(8,128)}, u32[]{:S(2)}) copy-start(f32[6,8192]{1,0:T(8,128)} %param.12) | copy-start | bytes 589828
  14.7 34.7 %copy-start.3 = (f32[8192]{0:T(1024)S(1)}, f32[8192]{0:T(1024)}, u32[]{:S(2)}) copy-start(f32[8192]{0:T(1024)} %param.13) | copy-start | bytes 98308
  45.9 7.2 %copy-start.4 = (s32[8192]{0:T(1024)S(1)}, s32[8192]{0:T(1024)}, u32[]{:S(2)}) copy-start(s32[8192]{0:T(1024)} %param.17) | copy-start | bytes 98308
  49.6 65.9 %copy-start = (f32[4,2,64,128]{3,2,1,0:T(8,128)S(1)}, f32[4,2,64,128]{3,2,1,0:T(8,128)}, u32[]{:S(2)}) copy-start(f32[4,2,64,128]{3,2,1,0:T(8,128)} %param.10) | copy-start | bytes 786436
  50.4 97.3 %copy-start.5 = (f32[4]{0:T(128)S(1)}, f32[4]{0:T(128)}, u32[]{:S(2)}) copy-start(f32[4]{0:T(128)} %param.11) | copy-start | bytes 52
  106.2 170.2 %collective-permute-start.3 = (f32[6,256]{1,0:T(8,128)S(1)}, f32[6,256]{1,0:T(8,128)S(1)}, u32[]{:S(2)}, u32[]{:S(2)}) collective-permute-start(f32[6,256]{1,0:T(8,128)S(1)} %bitcast.164), channel_id=1, source_target_pairs={{1,0},{2,1},{3,2},{0,3},{5,4},{6,5},{7,6},{4,7},{9,8},{10,9},{11,1... | collective-permute-start | bytes 18440 | tf_op jit(solution)/shard_map/ppermute | solution.py:26
  111.0 165.4 %collective-permute-start.2 = (f32[6,256]{1,0:T(8,128)S(1)}, f32[6,256]{1,0:T(8,128)S(1)}, u32[]{:S(2)}, u32[]{:S(2)}) collective-permute-start(f32[6,256]{1,0:T(8,128)S(1)} %bitcast.165), channel_id=1, source_target_pairs={{3,0},{0,1},{1,2},{2,3},{7,4},{4,5},{5,6},{6,7},{11,8},{8,9},{9,10... | collective-permute-start | bytes 18440 | tf_op jit(solution)/shard_map/ppermute | solution.py:26
  111.1 165.3 %collective-permute-start.1 = (f32[6,256]{1,0:T(8,128)S(1)}, f32[6,256]{1,0:T(8,128)S(1)}, u32[]{:S(2)}, u32[]{:S(2)}) collective-permute-start(f32[6,256]{1,0:T(8,128)S(1)} %bitcast.166), channel_id=1, source_target_pairs={{4,0},{8,4},{12,8},{16,12},{20,16},{24,20},{28,24},{5,1},{9,5},{13... | collective-permute-start | bytes 18440 | tf_op jit(solution)/shard_map/ppermute | solution.py:20
  112.5 163.9 %collective-permute-start = (f32[6,256]{1,0:T(8,128)S(1)}, f32[6,256]{1,0:T(8,128)S(1)}, u32[]{:S(2)}, u32[]{:S(2)}) collective-permute-start(f32[6,256]{1,0:T(8,128)S(1)} %bitcast.167), channel_id=1, source_target_pairs={{0,4},{4,8},{8,12},{12,16},{16,20},{20,24},{24,28},{1,5},{5,9},{9,... | collective-permute-start | bytes 18440 | tf_op jit(solution)/shard_map/ppermute | solution.py:20
  160.6 67.4 %all-to-all-start.1 = ((f32[4,16,8,128]{3,2,0,1:T(8,128)}), f32[4,16,8,128]{3,2,0,1:T(8,128)S(1)}, u32[]{:S(2)}, u32[]{:S(2)}) async-start(f32[4,16,8,128]{3,2,0,1:T(8,128)} %copy.111), calls=%async_computation.1 | async-start | bytes 524288 | tf_op jit(solution)/shard_map/all_to_all | solution.py:134
  245.2 14.2 %all-to-all-start.2 = ((f32[4,1,16384]{2,1,0:T(1,128)}), f32[4,1,16384]{2,1,0:T(1,128)S(1)}, u32[]{:S(2)}, u32[]{:S(2)}) async-start(f32[4,1,16384]{2,1,0:T(1,128)} %reshape.160), calls=%async_computation.2 | async-start | bytes 524288 | tf_op jit(solution)/shard_map/all_to_all | solution.py:136
  272.9 10.3 %all-to-all-start.3 = ((f32[4,16,8,128]{3,2,0,1:T(8,128)}), f32[4,16,8,128]{3,2,0,1:T(8,128)S(1)}, u32[]{:S(2)}, u32[]{:S(2)}) async-start(f32[4,16,8,128]{3,2,0,1:T(8,128)} %copy.117), calls=%async_computation.3 | async-start | bytes 524288 | tf_op jit(solution)/shard_map/all_to_all | solution.py:139
where the time goes:
time: 285 us; the launch traced here: 284 us
  other arithmetic  128 us (45%)
  local copies, waits for them, and re-layouts  77.6 us (27%)
  starting transfers between devices  27.8 us (10%)
  between operations  20.6 us (7%)
  matrix products  15 us (5%)
  waiting for transfers between devices  14.8 us (5%)
    scatter-add x1, other arithmetic, on_device(): outgoing = jnp.zeros((6, 4 * MIG + 1), jnp.float32).at[:, target].add(jnp...  52.9 us
    scatter-add x1, other arithmetic, on_device(): deposit = jnp.zeros_like(flat_speed).at[:, cell_index].add(force).reshape...  48 us
    gather x2, local copies, waits for them, and re-layouts, on_device(): fluid = jnp.take(flat_speed, cell_index, axis=1)  34 us
    unnamed x20, local copies, waits for them, and re-layouts  16.9 us
    div x1, other arithmetic, wall_compact(): lax.linalg.tridiagonal_solve(lower, middle, upper, rhs.astype(jnp.float32))  8.82 us
    all_to_all x1, waiting for transfers between devices, on_device(): lax.all_to_all(partial_z, 'col', split_axis=3, concat_axis=1, tiled=True)  8.61 us
    another operation x3, other arithmetic, periodic_compact(): factor = jnp.linalg.cholesky(lhs.astype(jnp.float32))  6.52 us
    all_to_all x1, waiting for transfers between devices, on_device(): lax.all_to_all(partial_y, 'row', split_axis=1, concat_axis=2, tiled=True)  6.18 us
  transfers between devices with their start and end apart: 8, of which 2 were waited for; matrix products, arithmetic and copies ran while one was open for 77% of the time, Pallas kernels for 0%

commit v1 on v0

v1 whole, which is shorter than its diff:
```python
import functools

import jax
import jax.numpy as jnp
import ml_dtypes
import numpy as np
from jax import lax
from jax.experimental import pallas as pl
from jax.experimental.pallas import tpu as pltpu
from jax.sharding import PartitionSpec as P

MIG = 256
LANES = 128
MIB = 1 << 20

time_step = 0.2
coupling = 0.5
stretch = 1.5


def periodic_compact(points):
    index = np.arange(points)
    offset = (index[None, :] - index[:, None]) % points
    lhs = (offset == 0) + ((offset == 1) | (offset == points - 1)) / 3.0
    rhs = 7.0 / 9.0 * ((offset == 1) * 1.0 - (offset == points - 1))
    rhs = rhs + ((offset == 2) * 1.0 - (offset == points - 2)) / 36.0
    return np.linalg.solve(lhs, rhs)


def wall_compact(points):
    lhs = np.eye(points)
    rhs = np.zeros((points, points))
    for row in range(points):
        if row == 0:
            lhs[0, 1] = 2.0
            rhs[0, :3] = (-2.5, 2.0, 0.5)
        elif row == points - 1:
            lhs[row, row - 1] = 2.0
            rhs[row, -3:] = (-0.5, -2.0, 2.5)
        elif row in (1, points - 2):
            lhs[row, [row - 1, row + 1]] = 0.25
            rhs[row, [row - 1, row + 1]] = (-0.75, 0.75)
        else:
            lhs[row, [row - 1, row + 1]] = 1.0 / 3.0
            rhs[row, [row - 2, row - 1, row + 1, row + 2]] = (-1 / 36, -7 / 9, 7 / 9, 1 / 36)
    coord = -1.0 + 2.0 * np.arange(points) / (points - 1)
    slope = stretch * (1.0 - np.tanh(stretch * coord) ** 2) / np.tanh(stretch)
    return np.linalg.solve(lhs, rhs) / slope[:, None]


def spectral_matrix(points):
    index = np.arange(points)
    offset = index[:, None] - index[None, :]
    parity = 1 - 2 * (offset % 2)
    angle = np.pi * np.where(offset == 0, 1, offset) / points
    return np.where(offset == 0, 0.0, np.pi / points * parity / np.tan(angle))


def two_terms(matrix):
    exact = np.asarray(matrix, np.float32)
    high = exact.astype(ml_dtypes.bfloat16)
    low = (exact - high.astype(np.float32)).astype(ml_dtypes.bfloat16)
    return high, low


def split(value, terms):
    pieces = []
    for _ in range(terms):
        piece = value.astype(jnp.bfloat16)
        pieces.append(piece)
        value = value - piece.astype(jnp.float32)
    return pieces


def dot(a, b):
    return lax.dot_general(a, b, (((1,), (0,)), ((), ())), preferred_element_type=jnp.float32)


def dot_transposed(a, b):
    return lax.dot_general(a, b, (((1,), (1,)), ((), ())), preferred_element_type=jnp.float32)


def one_hot(mask):
    return jnp.where(mask, 1.0, 0.0).astype(jnp.bfloat16)


def sublane_iota(rows, columns):
    return lax.broadcasted_iota(jnp.int32, (rows, columns), 0)


def params(mib):
    return pltpu.CompilerParams(vmem_limit_bytes=mib * MIB)


def cost(flops, nbytes):
    return pl.CostEstimate(flops=int(flops), bytes_accessed=int(nbytes), transcendentals=0)


def any_space(shape):
    return jax.ShapeDtypeStruct(tuple(shape), jnp.float32)


VMEM = pl.BlockSpec(memory_space=pltpu.VMEM)
SMEM = pl.BlockSpec(memory_space=pltpu.SMEM)


def advance_kernel(chunk, count_ref, fields_ref, records_ref, response_ref, cell_ref, destination_ref, slot_ref,
                   kept_ref, force_ref, outgoing_ref, table_ref, total_ref):
    planes, width, lanes = fields_ref.shape[1:]
    rows = planes * width
    particles = records_ref.shape[1]
    for component in range(3):
        plane = fields_ref[component].reshape(rows, lanes).T
        high, low = split(plane, 2)
        table_ref[component * lanes:(component + 1) * lanes, :rows] = high
        table_ref[component * lanes:(component + 1) * lanes, rows:] = low
    total_ref[...] = jnp.zeros_like(total_ref)
    groups = 4 * MIG // LANES

    def step(index, carry):
        start = pl.multiple_of(index * chunk, chunk)
        window = pl.ds(start, chunk)
        cell = cell_ref[:, window]
        row_hot = one_hot(sublane_iota(rows, chunk) == cell // lanes)
        found = dot(table_ref[...], jnp.concatenate([row_hot, row_hot], axis=0))
        at_lane = sublane_iota(lanes, chunk) == cell % lanes
        fluid = jnp.concatenate(
            [jnp.sum(jnp.where(at_lane, found[a * lanes:(a + 1) * lanes], 0.0), axis=0, keepdims=True) for a in range(3)],
            axis=0)
        records = records_ref[:, window]
        speed = records[3:6]
        drag = (fluid - speed) / response_ref[:, window]
        velocity = speed + time_step * drag
        moved = jnp.concatenate([records[0:3] + time_step * velocity, velocity], axis=0)
        live = start + lax.broadcasted_iota(jnp.int32, (1, chunk), 1) < count_ref[0]
        destination = destination_ref[:, window]
        kept_ref[:, window] = jnp.where(live & (destination == 0), moved, 0.0)
        force_ref[:, window] = jnp.where(live, -coupling * drag, 0.0)
        target = jnp.where(live & (destination > 0), (destination - 1) * MIG + slot_ref[:, window], -1)
        in_group = sublane_iota(groups, chunk) == target // LANES
        slot_hot = one_hot(sublane_iota(LANES, chunk) == target % LANES)
        pieces = []
        rest = moved
        for _ in range(3):
            piece = rest.astype(jnp.bfloat16).astype(jnp.float32)
            rest = rest - piece
            pieces += [jnp.where(in_group, piece[a:a + 1], 0.0) for a in range(6)]
        sent = jnp.concatenate(pieces, axis=0).astype(jnp.bfloat16)
        total_ref[...] += dot_transposed(sent, slot_hot)
        return carry

    lax.fori_loop(0, particles // chunk, step, 0)
    total = total_ref[...].reshape(3, 6, groups, LANES)
    outgoing_ref[...] = total[0] + total[1] + total[2]


def advance(counts, fields, records, response, cell, destination, slot):
    planes, width, lanes = fields.shape[1:]
    rows = planes * width
    particles = records.shape[1]
    chunk = min(1024 if rows <= 256 else 256, particles)
    groups = 4 * MIG // LANES
    return pl.pallas_call(
        functools.partial(advance_kernel, chunk),
        out_shape=(any_space((6, particles)), any_space((3, particles)), any_space((6, groups, LANES))),
        in_specs=[SMEM] + [VMEM] * 6,
        out_specs=(VMEM,) * 3,
        scratch_shapes=[pltpu.VMEM((3 * lanes, 2 * rows), jnp.bfloat16), pltpu.VMEM((18 * groups, LANES), jnp.float32)],
        compiler_params=params(32),
        cost_estimate=cost(2 * 3 * lanes * 2 * rows * particles, 4 * 20 * particles + fields.size * 4),
        name="advance",
    )(counts, fields, records, response, cell, destination, slot)


def along_x_kernel(chunk, viscous_ref, fields_ref, operator_ref, cell_ref, force_ref, out_ref, total_ref):
    parts, planes, width, lanes = fields_ref.shape
    rows = planes * width
    half = rows // 2
    particles = cell_ref.shape[1]
    total_ref[...] = jnp.zeros_like(total_ref)

    def step(index, carry):
        window = pl.ds(pl.multiple_of(index * chunk, chunk), chunk)
        cell = cell_ref[:, window]
        row = cell // lanes
        column = jnp.where(row >= half, lanes, 0) + cell % lanes
        at_row = sublane_iota(half, chunk) == row % half
        column_hot = one_hot(sublane_iota(2 * lanes, chunk) == column)
        pieces = []
        force = force_ref[:, window]
        for _ in range(2):
            piece = force.astype(jnp.bfloat16).astype(jnp.float32)
            force = force - piece
            pieces += [jnp.where(at_row, piece[a:a + 1], 0.0).astype(jnp.bfloat16) for a in range(3)]
        total_ref[...] += dot_transposed(jnp.concatenate(pieces, axis=0), column_hot)
        return carry

    lax.fori_loop(0, particles // chunk, step, 0)
    for component in range(parts):
        viscous = viscous_ref[component]
        for plane in range(planes):
            field = fields_ref[component, plane]
            high, low = split(field, 2)
            stacked = jnp.concatenate([high, low, high], axis=0)
            both = dot(operator_ref[...], stacked)
            value = -fields_ref[0, plane] * both[:width] + viscous * both[width:]
            if component < 3:
                for start in range(plane * width, (plane + 1) * width, min(width, half)):
                    part, first = divmod(start, half)
                    size = min(width, half)
                    columns = slice(part * lanes, (part + 1) * lanes)
                    base = component * half + first
                    deposit = (total_ref[base:base + size, columns]
                               + total_ref[3 * half + base:3 * half + base + size, columns])
                    inside = start - plane * width
                    out_ref[component, plane, inside:inside + size] = value[inside:inside + size] + deposit
            else:
                out_ref[component, plane] = value


def along_x(viscous, fields, cell, force):
    parts, planes, width, lanes = fields.shape
    half = planes * width // 2
    particles = cell.shape[1]
    chunk = min(1024 if half <= 128 else 256, particles)
    deriv = periodic_compact(width)
    high, low = two_terms(np.concatenate([deriv, deriv @ deriv], axis=0))
    operator = jnp.asarray(np.concatenate([high, high, low], axis=1))
    return pl.pallas_call(
        functools.partial(along_x_kernel, chunk),
        out_shape=any_space(fields.shape),
        in_specs=[SMEM] + [VMEM] * 4,
        out_specs=VMEM,
        scratch_shapes=[pltpu.VMEM((6 * half, 2 * lanes), jnp.float32)],
        compiler_params=params(40),
        cost_estimate=cost(2 * 6 * half * 2 * lanes * particles, fields.size * 8 + 16 * particles),
        name="along_x",
    )(viscous, fields, operator, cell, force)


def along_z_kernel(viscous_ref, high_ref, low_ref, *refs):
    count = len(refs) // 2
    blocks, results = refs[:count], refs[count:]
    parts, planes, width, lanes = blocks[0].shape
    rows = parts * planes * width
    pieces = [split(block[...].reshape(rows, lanes), 2) for block in blocks]

    def lines(term):
        return jnp.concatenate(
            [jnp.concatenate([pieces[(d - s) % count][term] for d in range(count)], axis=1) for s in range(count)], axis=0)

    high = lines(0)
    both = dot(high, high_ref[...]) + dot(lines(1), high_ref[...]) + dot(high, low_ref[...])
    for s in range(count):
        speed = blocks[(-s) % count][2]
        for component in range(parts):
            first = s * rows + component * planes * width
            part = both[first:first + planes * width]
            along = part[:, :lanes].reshape(planes, width, lanes)
            curve = part[:, lanes:].reshape(planes, width, lanes)
            results[s][component] = -speed * along + viscous_ref[component] * curve


def along_z(viscous, blocks):
    count = len(blocks)
    shape = blocks[0].shape
    lanes = shape[3]
    points = count * lanes
    deriv = spectral_matrix(points)
    second = deriv @ deriv
    weights = [
        np.concatenate([matrix[d * lanes:(d + 1) * lanes, :lanes].T for matrix in (deriv, second)], axis=1)
        for d in range(count)
    ]
    high, low = two_terms(np.concatenate(weights, axis=0))
    size = int(np.prod(shape))
    return pl.pallas_call(
        along_z_kernel,
        out_shape=tuple(any_space(shape) for _ in blocks),
        in_specs=[SMEM] + [VMEM] * (2 + count),
        out_specs=(VMEM,) * count,
        compiler_params=params(48),
        cost_estimate=cost(2 * 3 * size * count * points * 2, 8 * count * size),
        name="along_z",
    )(viscous, jnp.asarray(high), jnp.asarray(low), *blocks)


def along_y_kernel(viscous_ref, weight_ref, *refs):
    blocks, out_ref = refs[:-1], refs[-1]
    parts, planes, width, lanes = out_ref.shape
    for component in range(parts):
        viscous = viscous_ref[component]
        along = [jnp.zeros((width, lanes), jnp.float32) for _ in range(planes)]
        curve = [jnp.zeros((width, lanes), jnp.float32) for _ in range(planes)]
        for s, block in enumerate(blocks):
            for source in range(planes):
                value = block[component, source]
                for plane in range(planes):
                    base = ((s * planes + source) * planes + plane) * 2
                    along[plane] += weight_ref[base] * value
                    curve[plane] += weight_ref[base + 1] * value
        for plane in range(planes):
            out_ref[component, plane] = -blocks[0][1, plane] * along[plane] + viscous * curve[plane]


def along_y(viscous, blocks):
    count = len(blocks)
    planes = blocks[0].shape[1]
    deriv = wall_compact(count * planes)
    second = deriv @ deriv
    table = np.zeros((count, count, planes, planes, 2), np.float32)
    for me in range(count):
        for s in range(count):
            for source in range(planes):
                for plane in range(planes):
                    place = (me * planes + plane, (me ^ s) * planes + source)
                    table[me, s, source, plane] = deriv[place], second[place]
    weights = lax.dynamic_index_in_dim(jnp.asarray(table.reshape(count, -1)), lax.axis_index("row"), 0, keepdims=False)
    size = blocks[0].size
    return pl.pallas_call(
        along_y_kernel,
        out_shape=any_space(blocks[0].shape),
        in_specs=[SMEM, SMEM] + [VMEM] * count,
        out_specs=VMEM,
        compiler_params=params(32),
        cost_estimate=cost(4 * size * count * planes, 4 * size * (count + 1)),
        name="along_y",
    )(viscous, weights, *blocks)


def gathered_lines(fields):
    count = lax.axis_size("row")
    blocks = {0: fields}
    for s in range(2, count, 2):
        blocks[s] = lax.ppermute(fields, "row", [(i, i ^ s) for i in range(count)])
    for s in range(0, count, 2):
        blocks[s + 1] = lax.ppermute(blocks[s], "row", [(i, i ^ 1) for i in range(count)])
    return [blocks[s] for s in range(count)]


def pencil_along_y(viscous, fields):
    highest = lax.Precision.HIGHEST
    pencil = lax.all_to_all(fields, "row", split_axis=2, concat_axis=1, tiled=True)
    deriv = wall_compact(pencil.shape[1])
    operators = [jnp.asarray(matrix, jnp.float32) for matrix in (deriv, deriv @ deriv)]
    along, curve = (jnp.einsum("ij,cjxz->cixz", matrix, pencil, precision=highest) for matrix in operators)
    partial = -pencil[1] * along + viscous[:, None, None, None] * curve
    return lax.all_to_all(partial, "row", split_axis=1, concat_axis=2, tiled=True)


def total_kernel(place_ref, *refs):
    along_x_ref, along_y_ref = refs[:2]
    blocks, out_ref = refs[2:-1], refs[-1]
    count = len(blocks)
    width = blocks[0].shape[2]
    for s, block in enumerate(blocks):
        rows = pl.ds(pl.multiple_of(lax.rem(place_ref[0] + count - s, count) * width, width), width)
        out_ref[:, :, rows, :] = along_x_ref[:, :, rows, :] + along_y_ref[:, :, rows, :] + block[...]


def total(place, along_x_part, along_y_part, blocks):
    size = along_x_part.size
    return pl.pallas_call(
        total_kernel,
        out_shape=any_space(along_x_part.shape),
        in_specs=[SMEM] + [VMEM] * (2 + len(blocks)),
        out_specs=VMEM,
        compiler_params=params(32),
        cost_estimate=cost(3 * size, 16 * size),
        name="total",
    )(place, along_x_part, along_y_part, *blocks)


def exchange(blocks):
    count = lax.axis_size("col")
    received = list(blocks)
    for s in sorted(range(1, count), key=lambda s: -min(s, count - s)):
        received[s] = lax.ppermute(blocks[s], "col", [(i, (i + s) % count) for i in range(count)])
    return received


def on_device(fields, diffusivity, records, response_time, cell_index, counts, destination, slot):
    columns = lax.axis_size("col")
    place = lax.axis_index("col")
    width = fields.shape[2] // columns
    response = response_time.reshape(1, -1)
    cell = cell_index.reshape(1, -1)
    blocks = [
        lax.dynamic_slice_in_dim(fields, (place + s) % columns * width, width, axis=2) for s in range(columns)
    ]
    lines = exchange(blocks)
    kept, force, outgoing = advance(
        counts, fields, records, response, cell, destination.reshape(1, -1), slot.reshape(1, -1))
    outgoing = outgoing.reshape(6, 4, MIG)
    terms_z = exchange(along_z(diffusivity, lines))
    rows = lax.axis_size("row")
    if rows & (rows - 1) == 0 and rows * fields.size * 4 <= 16 * MIB:
        terms_y = along_y(diffusivity, gathered_lines(fields))
    else:
        terms_y = pencil_along_y(diffusivity, fields)
    terms_x = along_x(diffusivity, fields, cell, force)
    tendency = total(place.reshape(1), terms_x, terms_y, terms_z)
    steps = [(i, i + 1) for i in range(rows - 1)]
    ring = [(i, (i + 1) % columns) for i in range(columns)]
    arrivals = jnp.stack(
        [
            lax.ppermute(outgoing[:, 0], "row", steps),
            lax.ppermute(outgoing[:, 1], "row", [(b, a) for a, b in steps]),
            lax.ppermute(outgoing[:, 2], "col", ring),
            lax.ppermute(outgoing[:, 3], "col", [(b, a) for a, b in ring]),
        ],
        axis=0,
    )
    return (tendency, kept, arrivals)


def solution(mesh):
    return jax.shard_map(
        on_device,
        mesh=mesh,
        in_specs=(
            P(None, "row", None, "col"),
            P(),
            P(None, ("row", "col")),
            P(("row", "col")),
            P(("row", "col")),
            P(("row", "col")),
            P(("row", "col")),
            P(("row", "col")),
        ),
        out_specs=(
            P(None, "row", None, "col"),
            P(None, ("row", "col")),
            P(None, None, ("row", "col")),
        ),
        check_vma=False,
    )
```

time: 285 us -> 54.1 us (0.19)
  the two profiles are of different devices: /device:TPU:0 before, /device:TPU:13 now
where the time goes in v1:
time: 54.1 us; the launch traced here: 53.9 us
  starting transfers between devices  27.3 us (50%)
  Pallas kernels  13.5 us (25%)
  waiting for transfers between devices  9.15 us (17%)
  local copies, waits for them, and re-layouts  2.42 us (4%)
  between operations  1.5 us (3%)
    ppermute x6, starting transfers between devices, exchange(): lax.ppermute(blocks[s], 'col', [(i, (i + s) % count) for i in range(count)])  8.75 us
    ppermute x1, starting transfers between devices, on_device(): lax.ppermute(outgoing[:, 0], 'row', steps)  6.79 us
    pallas_call x1, Pallas kernels, advance(): pl.pallas_call(functools.partial(advance_kernel, chunk), out_shape=(any_s...  6.2 us
    ppermute x6, waiting for transfers between devices, exchange(): lax.ppermute(blocks[s], 'col', [(i, (i + s) % count) for i in range(count)])  5.08 us
    pallas_call x1, Pallas kernels, along_x(): pl.pallas_call(functools.partial(along_x_kernel, chunk), out_shape=any_sp...  4.22 us
    ppermute x4, starting transfers between devices, gathered_lines(): lax.ppermute(blocks[s], 'row', [(i, i ^ 1) for i in range(count)])  3.22 us
    ppermute x1, starting transfers between devices, on_device(): lax.ppermute(outgoing[:, 1], 'row', [(b, a) for a, b in steps])  2.86 us
    ppermute x3, starting transfers between devices, gathered_lines(): blocks[s] = lax.ppermute(fields, 'row', [(i, i ^ s) for i in range(count)])  2.71 us
  transfers between devices with their start and end apart: 17, of which 7 were waited for; matrix products, arithmetic and copies ran while one was open for 4% of the time, Pallas kernels for 24%

profile of v1, /device:TPU:13, one launch (start us, length us, event | category | flops | bytes accessed | tf_op | source)
XLA Modules:
  0.0 53.9 jit_solution(11321017788289186331)
XLA Ops:
  0.6 1.3 %collective-permute-start.1 = (f32[4,2,64,128]{3,2,1,0:T(8,128)}, f32[4,2,64,128]{3,2,1,0:T(8,128)S(1)}, u32[]{:S(2)}, u32[]{:S(2)}) collective-permute-start(f32[4,2,64,128]{3,2,1,0:T(8,128)} %refs_0_.1), channel_id=1, source_target_pairs={{0,8},{4,12},{8,0},{12,4},{16,24},{20,28},{24,16},{28,20},{1,9},{5... | collective-permute-start | bytes 786440 | tf_op jit(solution)/shard_map/ppermute | solution.py:335
  1.9 0.2 collective-permute-start.3
  2.1 1.2 %collective-permute-start.5 = (f32[4,2,64,128]{3,2,1,0:T(8,128)}, f32[4,2,64,128]{3,2,1,0:T(8,128)S(1)}, u32[]{:S(2)}, u32[]{:S(2)}) collective-permute-start(f32[4,2,64,128]{3,2,1,0:T(8,128)} %refs_0_.1), channel_id=1, source_target_pairs={{0,24},{4,28},{8,16},{12,20},{16,8},{20,12},{24,0},{28,4},{1,25},{... | collective-permute-start | bytes 786440 | tf_op jit(solution)/shard_map/ppermute | solution.py:335
  3.3 0.0 copy-start.6
  3.3 0.0 copy-start.5
  3.4 0.0 copy-start.4
  3.4 0.0 copy-start.3
  3.4 0.0 copy-start
  3.4 0.0 copy-start.2
  3.4 1.0 %constant_dynamic-slice_fusion = (f32[4,2,16,128]{3,2,1,0:T(8,128)S(1)}, f32[4,2,16,128]{3,2,1,0:T(8,128)S(1)}, f32[4,2,16,128]{3,2,1,0:T(8,128)S(1)}, f32[4,2,16,128]{3,2,1,0:T(8,128)S(1)}) fusion(f32[4,2,64,128]{3,2,1,0:T(8,128)} %refs_0_.1, s32[]{:T(128)S(6)} %select_n.43, s32[]{:T(128)S(6)} %select_n.39, s32[]{:T(128)S(6)} %select_n.37, s32[]{:T(128)S(6)} %select_n.41), kind=kLoop, calls=%fused_computation.5 | loop fusion | bytes 524304 | tf_op jit(solution)/shard_map/dynamic_slice | solution.py:389
  4.4 1.3 %collective-permute-start.7 = (f32[4,2,16,128]{3,2,1,0:T(8,128)S(1)}, f32[4,2,16,128]{3,2,1,0:T(8,128)S(1)}, u32[]{:S(2)}, u32[]{:S(2)}) collective-permute-start(f32[4,2,16,128]{3,2,1,0:T(8,128)S(1)} %get-tuple-element.21), channel_id=1, source_target_pairs={{0,1},{1,2},{2,3},{3,0},{4,5},{5,6},{6,7},{7,4},{8,9},{9,10},{10,1... | collective-permute-start | bytes 196616 | tf_op jit(solution)/shard_map/ppermute | solution.py:378
  6.4 0.0 copy-done.6
  6.4 0.0 copy-done.5
  6.4 0.0 copy-done.4
  6.5 0.0 copy-done.3
  6.5 0.0 copy-done
  6.5 0.0 copy-done.2
  6.5 6.2 %advance.1 = (f32[6,8192]{1,0:T(8,128)}, f32[3,8192]{1,0:T(4,128)S(1)}, f32[6,8,128]{2,1,0:T(8,128)S(1)}) custom-call(s32[1]{0:T(128)S(6)} %copy.36.count_ref, f32[4,2,64,128]{3,2,1,0:T(8,128)S(1)} %copy-done, f32[6,8192]{1,0:T(8,128)S(1)} %copy-done.2, f32[1,8192]{1,0:T(1,128)S(1)} %bitcast.23, s32[1,8192]{1,0:T(1,128)S(1)} %bitcast.26, ...), custom_call_target="tpu_custom_call" | custom-call | flops 1610612736 | bytes 917504 | tf_op jit(solution)/shard_map/advance/pallas_call | solution.py:163
  12.7 0.0 copy-start.9
  12.8 1.4 %collective-permute-start.15 = (f32[6,256]{1,0:T(8,128)S(1)}, f32[6,256]{1,0:T(8,128)S(1)}, u32[]{:S(2)}, u32[]{:S(2)}) collective-permute-start(f32[6,256]{1,0:T(8,128)S(1)} %bitcast.31), channel_id=1, source_target_pairs={{0,1},{1,2},{2,3},{3,0},{4,5},{5,6},{6,7},{7,4},{8,9},{9,10},{10,1... | collective-permute-start | bytes 18440 | tf_op jit(solution)/shard_map/ppermute | solution.py:409
  14.1 1.5 %collective-permute-done.15 = f32[6,256]{1,0:T(8,128)S(1)} collective-permute-done((f32[6,256]{1,0:T(8,128)S(1)}, f32[6,256]{1,0:T(8,128)S(1)}, u32[]{:S(2)}, u32[]{:S(2)}) %collective-permute-start.15) | collective-permute-done | bytes 6176 | tf_op jit(solution)/shard_map/ppermute | solution.py:409
  15.6 1.7 %collective-permute-start.16 = (f32[6,256]{1,0:T(8,128)S(1)}, f32[6,256]{1,0:T(8,128)S(1)}, u32[]{:S(2)}, u32[]{:S(2)}) collective-permute-start(f32[6,256]{1,0:T(8,128)S(1)} %bitcast.29), channel_id=1, source_target_pairs={{1,0},{2,1},{3,2},{0,3},{5,4},{6,5},{7,6},{4,7},{9,8},{10,9},{11,1... | collective-permute-start | bytes 18440 | tf_op jit(solution)/shard_map/ppermute | solution.py:410
  17.3 0.8 %collective-permute-done.16 = f32[6,256]{1,0:T(8,128)S(1)} collective-permute-done((f32[6,256]{1,0:T(8,128)S(1)}, f32[6,256]{1,0:T(8,128)S(1)}, u32[]{:S(2)}, u32[]{:S(2)}) %collective-permute-start.16) | collective-permute-done | bytes 6176 | tf_op jit(solution)/shard_map/ppermute | solution.py:410
  18.1 6.8 %collective-permute-start.13 = (f32[6,256]{1,0:T(8,128)S(1)}, f32[6,256]{1,0:T(8,128)S(1)}, u32[]{:S(2)}, u32[]{:S(2)}) collective-permute-start(f32[6,256]{1,0:T(8,128)S(1)} %bitcast.30), channel_id=1, source_target_pairs={{0,4},{4,8},{8,12},{12,16},{16,20},{20,24},{24,28},{1,5},{5,9},{9,... | collective-permute-start | bytes 18440 | tf_op jit(solution)/shard_map/ppermute | solution.py:407
  24.9 0.8 %collective-permute-done.13 = f32[6,256]{1,0:T(8,128)S(1)} collective-permute-done((f32[6,256]{1,0:T(8,128)S(1)}, f32[6,256]{1,0:T(8,128)S(1)}, u32[]{:S(2)}, u32[]{:S(2)}) %collective-permute-start.13) | collective-permute-done | bytes 6176 | tf_op jit(solution)/shard_map/ppermute | solution.py:407
  25.7 2.1 %collective-permute-start = (f32[4,2,64,128]{3,2,1,0:T(8,128)S(1)}, f32[4,2,64,128]{3,2,1,0:T(8,128)S(1)}, u32[]{:S(2)}, u32[]{:S(2)}) collective-permute-start(f32[4,2,64,128]{3,2,1,0:T(8,128)S(1)} %copy-done), channel_id=1, source_target_pairs={{0,4},{4,0},{8,12},{12,8},{16,20},{20,16},{24,28},{28,24},{1,5},{5... | collective-permute-start | bytes 786440 | tf_op jit(solution)/shard_map/ppermute | solution.py:337
  27.8 0.0 collective-permute-done.7.refs_1_
  27.8 0.0 copy-start.1
  27.8 2.8 %collective-permute-start.8 = (f32[4,2,16,128]{3,2,1,0:T(8,128)S(1)}, f32[4,2,16,128]{3,2,1,0:T(8,128)S(1)}, u32[]{:S(2)}, u32[]{:S(2)}) collective-permute-start(f32[4,2,16,128]{3,2,1,0:T(8,128)S(1)} %get-tuple-element.23), channel_id=1, source_target_pairs={{0,2},{1,3},{2,0},{3,1},{4,6},{5,7},{6,4},{7,5},{8,10},{9,11},{10,... | collective-permute-start | bytes 196616 | tf_op jit(solution)/shard_map/ppermute | solution.py:378
  30.5 0.0 collective-permute-done.1.refs_2_
  30.5 0.4 collective-permute-start.2
  30.9 0.0 copy-done.9
  30.9 0.0 copy-done.1
  30.9 0.0 copy-start.7
  30.9 0.0 copy-start.8
  30.9 4.2 %along_x.1.refs_0_ = f32[4,2,64,128]{3,2,1,0:T(8,128)S(1)} custom-call(f32[4]{0:T(128)S(1)} %copy-done.1, f32[4,2,64,128]{3,2,1,0:T(8,128)S(1)} %copy-done, bf16[128,192]{1,0:T(8,128)(2,1)S(1)} %copy-done.9, s32[1,8192]{1,0:T(1,128)S(1)} %bitcast.27, f32[3,8192]{1,0:T(4,128)S(1)} %get-tuple-element.10.force_ref), custom_call_target="tpu_custom_call" | custom-call | flops 1610612736 | bytes 655360 | tf_op jit(solution)/shard_map/along_x/pallas_call | solution.py:229
  35.1 0.0 collective-permute-done.8.refs_2_
  35.1 0.6 %collective-permute-start.9 = (f32[4,2,16,128]{3,2,1,0:T(8,128)S(1)}, f32[4,2,16,128]{3,2,1,0:T(8,128)S(1)}, u32[]{:S(2)}, u32[]{:S(2)}) collective-permute-start(f32[4,2,16,128]{3,2,1,0:T(8,128)S(1)} %get-tuple-element.20), channel_id=1, source_target_pairs={{0,3},{1,0},{2,1},{3,2},{4,7},{5,4},{6,5},{7,6},{8,11},{9,8},{10,9... | collective-permute-start | bytes 196616 | tf_op jit(solution)/shard_map/ppermute | solution.py:378
  35.7 0.0 collective-permute-done.3.refs_4_
  35.7 0.7 %collective-permute-start.4 = (f32[4,2,64,128]{3,2,1,0:T(8,128)S(1)}, f32[4,2,64,128]{3,2,1,0:T(8,128)S(1)}, u32[]{:S(2)}, u32[]{:S(2)}) collective-permute-start(f32[4,2,64,128]{3,2,1,0:T(8,128)S(1)} %collective-permute-done.3.refs_4_), channel_id=1, source_target_pairs={{0,4},{4,0},{8,12},{12,8},{16,20},{20,16},{24,28},{28,24},{1,5},{5... | collective-permute-start | bytes 786440 | tf_op jit(solution)/shard_map/ppermute | solution.py:337
  36.4 0.0 collective-permute-done.5.refs_6_
  36.4 0.1 collective-permute-start.6
  36.5 0.7 %fusion.weight_ref = f32[64]{0:T(128)S(1)} fusion(f32[8,64]{1,0:T(8,128)} %constant.59.clone, s32[]{:T(128)S(6)} %select_n.35), kind=kLoop, calls=%fused_computation.10 | loop fusion | bytes 516 | tf_op jit(solution)/shard_map/jit(dynamic_index_in_dim)/squeeze | solution.py:318
  37.2 1.5 %collective-permute-done.9.refs_3_ = f32[4,2,16,128]{3,2,1,0:T(8,128)S(1)} collective-permute-done((f32[4,2,16,128]{3,2,1,0:T(8,128)S(1)}, f32[4,2,16,128]{3,2,1,0:T(8,128)S(1)}, u32[]{:S(2)}, u32[]{:S(2)}) %collective-permute-start.9) | collective-permute-done | bytes 65568 | tf_op jit(solution)/shard_map/ppermute | solution.py:378
  38.7 2.9 %collective-permute-start.14 = (f32[6,256]{1,0:T(8,128)S(1)}, f32[6,256]{1,0:T(8,128)S(1)}, u32[]{:S(2)}, u32[]{:S(2)}) collective-permute-start(f32[6,256]{1,0:T(8,128)S(1)} %bitcast.28), channel_id=1, source_target_pairs={{4,0},{8,4},{12,8},{16,12},{20,16},{24,20},{28,24},{5,1},{9,5},{13... | collective-permute-start | bytes 18440 | tf_op jit(solution)/shard_map/ppermute | solution.py:408
  41.6 0.0 copy-done.7
  41.6 0.0 copy-done.8
  41.6 1.1 %along_z.1 = (f32[4,2,16,128]{3,2,1,0:T(8,128)S(1)}, f32[4,2,16,128]{3,2,1,0:T(8,128)S(1)}, f32[4,2,16,128]{3,2,1,0:T(8,128)S(1)}, f32[4,2,16,128]{3,2,1,0:T(8,128)S(1)}) custom-call(f32[4]{0:T(128)S(1)} %copy-done.1, bf16[512,256]{1,0:T(8,128)(2,1)S(1)} %copy-done.7, bf16[512,256]{1,0:T(8,128)(2,1)S(1)} %copy-done.8, ...), custom_call_target="tpu_custom_call" | custom-call | flops 402653184 | bytes 524288 | tf_op jit(solution)/shard_map/along_z/pallas_call | solution.py:277
  42.7 0.9 %collective-permute-done.14 = f32[6,256]{1,0:T(8,128)S(1)} collective-permute-done((f32[6,256]{1,0:T(8,128)S(1)}, f32[6,256]{1,0:T(8,128)S(1)}, u32[]{:S(2)}, u32[]{:S(2)}) %collective-permute-start.14) | collective-permute-done | bytes 6176 | tf_op jit(solution)/shard_map/ppermute | solution.py:408
  43.7 0.4 collective-permute-start.10
  44.1 0.0 collective-permute-done.refs_1_
  44.1 2.2 %collective-permute-start.11 = (f32[4,2,16,128]{3,2,1,0:T(8,128)S(1)}, f32[4,2,16,128]{3,2,1,0:T(8,128)S(1)}, u32[]{:S(2)}, u32[]{:S(2)}) collective-permute-start(f32[4,2,16,128]{3,2,1,0:T(8,128)S(1)} %get-tuple-element.13), channel_id=1, source_target_pairs={{0,2},{1,3},{2,0},{3,1},{4,6},{5,7},{6,4},{7,5},{8,10},{9,11},{10,... | collective-permute-start | bytes 196616 | tf_op jit(solution)/shard_map/ppermute | solution.py:378
  46.3 0.0 collective-permute-done.2.refs_3_
  46.3 1.5 %collective-permute-start.12 = (f32[4,2,16,128]{3,2,1,0:T(8,128)S(1)}, f32[4,2,16,128]{3,2,1,0:T(8,128)S(1)}, u32[]{:S(2)}, u32[]{:S(2)}) collective-permute-start(f32[4,2,16,128]{3,2,1,0:T(8,128)S(1)} %get-tuple-element.14), channel_id=1, source_target_pairs={{0,3},{1,0},{2,1},{3,2},{4,7},{5,4},{6,5},{7,6},{8,11},{9,8},{10,9... | collective-permute-start | bytes 196616 | tf_op jit(solution)/shard_map/ppermute | solution.py:378
  47.8 0.6 %copy.23 = f32[4,6,256]{2,0,1:T(4,128)} copy(f32[4,6,256]{2,1,0:T(8,128)S(1)} %pad_maximum_fusion) | data formatting | bytes 49152
  48.4 0.0 collective-permute-done.4.refs_5_
  48.4 0.0 collective-permute-done.6.refs_7_
  48.4 1.2 %along_y.1.refs_1_ = f32[4,2,64,128]{3,2,1,0:T(8,128)S(1)} custom-call(f32[4]{0:T(128)S(1)} %copy-done.1, f32[64]{0:T(128)S(1)} %fusion.weight_ref, f32[4,2,64,128]{3,2,1,0:T(8,128)S(1)} %copy-done, f32[4,2,64,128]{3,2,1,0:T(8,128)S(1)} %collective-permute-done.refs_1_, f32[4,2,64,128]{3,2,1,0:T(8,128)S(1)} %collective-permute-done.1.refs_2_, ...), custom_call_target="tpu_custom_call" | custom-call | flops 4194304 | bytes 2359296 | tf_op jit(solution)/shard_map/along_y/pallas_call | solution.py:320
  49.6 0.0 collective-permute-done.10.refs_3_
  49.6 0.7 %collective-permute-done.11.refs_4_ = f32[4,2,16,128]{3,2,1,0:T(8,128)S(1)} collective-permute-done((f32[4,2,16,128]{3,2,1,0:T(8,128)S(1)}, f32[4,2,16,128]{3,2,1,0:T(8,128)S(1)}, u32[]{:S(2)}, u32[]{:S(2)}) %collective-permute-start.11) | collective-permute-done | bytes 65568 | tf_op jit(solution)/shard_map/ppermute | solution.py:378
  50.3 2.8 %collective-permute-done.12.refs_5_ = f32[4,2,16,128]{3,2,1,0:T(8,128)S(1)} collective-permute-done((f32[4,2,16,128]{3,2,1,0:T(8,128)S(1)}, f32[4,2,16,128]{3,2,1,0:T(8,128)S(1)}, u32[]{:S(2)}, u32[]{:S(2)}) %collective-permute-start.12) | collective-permute-done | bytes 65568 | tf_op jit(solution)/shard_map/ppermute | solution.py:378
  53.1 0.8 %total.1 = f32[4,2,64,128]{3,2,1,0:T(8,128)} custom-call(s32[1]{0:T(128)} %bitcast.place_ref, f32[4,2,64,128]{3,2,1,0:T(8,128)S(1)} %along_x.1.refs_0_, f32[4,2,64,128]{3,2,1,0:T(8,128)S(1)} %along_y.1.refs_1_, f32[4,2,16,128]{3,2,1,0:T(8,128)S(1)} %get-tuple-element.11.refs_2_, f32[4,2,16,128]{3,2,1,0:T(8,128)S(1)} %collective-permute-done.10.refs_3_, ...), custom_call_target="tpu_custom_call" | custom-call | flops 196608 | bytes 1048576 | tf_op jit(solution)/shard_map/total/pallas_call | solution.py:363
  (7 shorter events, 0.0 us)
Async XLA Ops:
  0.6 29.9 %collective-permute-start.1 = (f32[4,2,64,128]{3,2,1,0:T(8,128)}, f32[4,2,64,128]{3,2,1,0:T(8,128)S(1)}, u32[]{:S(2)}, u32[]{:S(2)}) collective-permute-start(f32[4,2,64,128]{3,2,1,0:T(8,128)} %refs_0_.1), channel_id=1, source_target_pairs={{0,8},{4,12},{8,0},{12,4},{16,24},{20,28},{24,16},{28,20},{1,9},{5... | collective-permute-start | bytes 786440 | tf_op jit(solution)/shard_map/ppermute | solution.py:335
  1.9 33.8 %collective-permute-start.3 = (f32[4,2,64,128]{3,2,1,0:T(8,128)}, f32[4,2,64,128]{3,2,1,0:T(8,128)S(1)}, u32[]{:S(2)}, u32[]{:S(2)}) collective-permute-start(f32[4,2,64,128]{3,2,1,0:T(8,128)} %refs_0_.1), channel_id=1, source_target_pairs={{0,16},{4,20},{8,24},{12,28},{16,0},{20,4},{24,8},{28,12},{1,17},{... | collective-permute-start | bytes 786440 | tf_op jit(solution)/shard_map/ppermute | solution.py:335
  2.1 34.3 %collective-permute-start.5 = (f32[4,2,64,128]{3,2,1,0:T(8,128)}, f32[4,2,64,128]{3,2,1,0:T(8,128)S(1)}, u32[]{:S(2)}, u32[]{:S(2)}) collective-permute-start(f32[4,2,64,128]{3,2,1,0:T(8,128)} %refs_0_.1), channel_id=1, source_target_pairs={{0,24},{4,28},{8,16},{12,20},{16,8},{20,12},{24,0},{28,4},{1,25},{... | collective-permute-start | bytes 786440 | tf_op jit(solution)/shard_map/ppermute | solution.py:335
  3.3 3.1 %copy-start.6 = (s32[8192]{0:T(1024)S(1)}, s32[8192]{0:T(1024)}, u32[]{:S(2)}) copy-start(s32[8192]{0:T(1024)} %param.16) | copy-start | bytes 98308
  3.3 3.1 %copy-start.5 = (s32[8192]{0:T(1024)S(1)}, s32[8192]{0:T(1024)}, u32[]{:S(2)}) copy-start(s32[8192]{0:T(1024)} %param.19) | copy-start | bytes 98308
  3.4 3.1 %copy-start.4 = (s32[8192]{0:T(1024)S(1)}, s32[8192]{0:T(1024)}, u32[]{:S(2)}) copy-start(s32[8192]{0:T(1024)} %param.18) | copy-start | bytes 98308
  3.4 3.1 %copy-start.3 = (f32[8192]{0:T(1024)S(1)}, f32[8192]{0:T(1024)}, u32[]{:S(2)}) copy-start(f32[8192]{0:T(1024)} %param.15) | copy-start | bytes 98308
  3.4 3.1 %copy-start = (f32[4,2,64,128]{3,2,1,0:T(8,128)S(1)}, f32[4,2,64,128]{3,2,1,0:T(8,128)}, u32[]{:S(2)}) copy-start(f32[4,2,64,128]{3,2,1,0:T(8,128)} %refs_0_.1) | copy-start | bytes 786436
  3.4 3.1 %copy-start.2 = (f32[6,8192]{1,0:T(8,128)S(1)}, f32[6,8192]{1,0:T(8,128)}, u32[]{:S(2)}) copy-start(f32[6,8192]{1,0:T(8,128)} %records_ref.1) | copy-start | bytes 589828
  4.4 23.3 %collective-permute-start.7 = (f32[4,2,16,128]{3,2,1,0:T(8,128)S(1)}, f32[4,2,16,128]{3,2,1,0:T(8,128)S(1)}, u32[]{:S(2)}, u32[]{:S(2)}) collective-permute-start(f32[4,2,16,128]{3,2,1,0:T(8,128)S(1)} %get-tuple-element.21), channel_id=1, source_target_pairs={{0,1},{1,2},{2,3},{3,0},{4,5},{5,6},{6,7},{7,4},{8,9},{9,10},{10,1... | collective-permute-start | bytes 196616 | tf_op jit(solution)/shard_map/ppermute | solution.py:378
  12.7 18.2 %copy-start.9 = (bf16[128,192]{1,0:T(8,128)(2,1)S(1)}, bf16[128,192]{1,0:T(8,128)(2,1)}, u32[]{:S(2)}) copy-start(bf16[128,192]{1,0:T(8,128)(2,1)} %constant.60.clone.operator_ref) | copy-start | bytes 147460
  12.8 2.8 %collective-permute-start.15 = (f32[6,256]{1,0:T(8,128)S(1)}, f32[6,256]{1,0:T(8,128)S(1)}, u32[]{:S(2)}, u32[]{:S(2)}) collective-permute-start(f32[6,256]{1,0:T(8,128)S(1)} %bitcast.31), channel_id=1, source_target_pairs={{0,1},{1,2},{2,3},{3,0},{4,5},{5,6},{6,7},{7,4},{8,9},{9,10},{10,1... | collective-permute-start | bytes 18440 | tf_op jit(solution)/shard_map/ppermute | solution.py:409
  15.6 2.5 %collective-permute-start.16 = (f32[6,256]{1,0:T(8,128)S(1)}, f32[6,256]{1,0:T(8,128)S(1)}, u32[]{:S(2)}, u32[]{:S(2)}) collective-permute-start(f32[6,256]{1,0:T(8,128)S(1)} %bitcast.29), channel_id=1, source_target_pairs={{1,0},{2,1},{3,2},{0,3},{5,4},{6,5},{7,6},{4,7},{9,8},{10,9},{11,1... | collective-permute-start | bytes 18440 | tf_op jit(solution)/shard_map/ppermute | solution.py:410
  18.1 7.6 %collective-permute-start.13 = (f32[6,256]{1,0:T(8,128)S(1)}, f32[6,256]{1,0:T(8,128)S(1)}, u32[]{:S(2)}, u32[]{:S(2)}) collective-permute-start(f32[6,256]{1,0:T(8,128)S(1)} %bitcast.30), channel_id=1, source_target_pairs={{0,4},{4,8},{8,12},{12,16},{16,20},{20,24},{24,28},{1,5},{5,9},{9,... | collective-permute-start | bytes 18440 | tf_op jit(solution)/shard_map/ppermute | solution.py:407
  25.7 18.4 %collective-permute-start = (f32[4,2,64,128]{3,2,1,0:T(8,128)S(1)}, f32[4,2,64,128]{3,2,1,0:T(8,128)S(1)}, u32[]{:S(2)}, u32[]{:S(2)}) collective-permute-start(f32[4,2,64,128]{3,2,1,0:T(8,128)S(1)} %copy-done), channel_id=1, source_target_pairs={{0,4},{4,0},{8,12},{12,8},{16,20},{20,16},{24,28},{28,24},{1,5},{5... | collective-permute-start | bytes 786440 | tf_op jit(solution)/shard_map/ppermute | solution.py:337
  27.8 3.1 %copy-start.1 = (f32[4]{0:T(128)S(1)}, f32[4]{0:T(128)}, u32[]{:S(2)}) copy-start(f32[4]{0:T(128)} %viscous_ref.5) | copy-start | bytes 52
  27.8 7.4 %collective-permute-start.8 = (f32[4,2,16,128]{3,2,1,0:T(8,128)S(1)}, f32[4,2,16,128]{3,2,1,0:T(8,128)S(1)}, u32[]{:S(2)}, u32[]{:S(2)}) collective-permute-start(f32[4,2,16,128]{3,2,1,0:T(8,128)S(1)} %get-tuple-element.23), channel_id=1, source_target_pairs={{0,2},{1,3},{2,0},{3,1},{4,6},{5,7},{6,4},{7,5},{8,10},{9,11},{10,... | collective-permute-start | bytes 196616 | tf_op jit(solution)/shard_map/ppermute | solution.py:378
  30.5 15.8 %collective-permute-start.2 = (f32[4,2,64,128]{3,2,1,0:T(8,128)S(1)}, f32[4,2,64,128]{3,2,1,0:T(8,128)S(1)}, u32[]{:S(2)}, u32[]{:S(2)}) collective-permute-start(f32[4,2,64,128]{3,2,1,0:T(8,128)S(1)} %collective-permute-done.1.refs_2_), channel_id=1, source_target_pairs={{0,4},{4,0},{8,12},{12,8},{16,20},{20,16},{24,28},{28,24},{1,5},{5... | collective-permute-start | bytes 786440 | tf_op jit(solution)/shard_map/ppermute | solution.py:337
  30.9 10.7 %copy-start.7 = (bf16[512,256]{1,0:T(8,128)(2,1)S(1)}, bf16[512,256]{1,0:T(8,128)(2,1)}, u32[]{:S(2)}) copy-start(bf16[512,256]{1,0:T(8,128)(2,1)} %constant.57.clone.high_ref) | copy-start | bytes 786436
  30.9 10.7 %copy-start.8 = (bf16[512,256]{1,0:T(8,128)(2,1)S(1)}, bf16[512,256]{1,0:T(8,128)(2,1)}, u32[]{:S(2)}) copy-start(bf16[512,256]{1,0:T(8,128)(2,1)} %constant.58.clone.low_ref) | copy-start | bytes 786436
  35.1 3.6 %collective-permute-start.9 = (f32[4,2,16,128]{3,2,1,0:T(8,128)S(1)}, f32[4,2,16,128]{3,2,1,0:T(8,128)S(1)}, u32[]{:S(2)}, u32[]{:S(2)}) collective-permute-start(f32[4,2,16,128]{3,2,1,0:T(8,128)S(1)} %get-tuple-element.20), channel_id=1, source_target_pairs={{0,3},{1,0},{2,1},{3,2},{4,7},{5,4},{6,5},{7,6},{8,11},{9,8},{10,9... | collective-permute-start | bytes 196616 | tf_op jit(solution)/shard_map/ppermute | solution.py:378
  35.7 12.7 %collective-permute-start.4 = (f32[4,2,64,128]{3,2,1,0:T(8,128)S(1)}, f32[4,2,64,128]{3,2,1,0:T(8,128)S(1)}, u32[]{:S(2)}, u32[]{:S(2)}) collective-permute-start(f32[4,2,64,128]{3,2,1,0:T(8,128)S(1)} %collective-permute-done.3.refs_4_), channel_id=1, source_target_pairs={{0,4},{4,0},{8,12},{12,8},{16,20},{20,16},{24,28},{28,24},{1,5},{5... | collective-permute-start | bytes 786440 | tf_op jit(solution)/shard_map/ppermute | solution.py:337
  36.4 12.0 %collective-permute-start.6 = (f32[4,2,64,128]{3,2,1,0:T(8,128)S(1)}, f32[4,2,64,128]{3,2,1,0:T(8,128)S(1)}, u32[]{:S(2)}, u32[]{:S(2)}) collective-permute-start(f32[4,2,64,128]{3,2,1,0:T(8,128)S(1)} %collective-permute-done.5.refs_6_), channel_id=1, source_target_pairs={{0,4},{4,0},{8,12},{12,8},{16,20},{20,16},{24,28},{28,24},{1,5},{5... | collective-permute-start | bytes 786440 | tf_op jit(solution)/shard_map/ppermute | solution.py:337
  38.7 5.0 %collective-permute-start.14 = (f32[6,256]{1,0:T(8,128)S(1)}, f32[6,256]{1,0:T(8,128)S(1)}, u32[]{:S(2)}, u32[]{:S(2)}) collective-permute-start(f32[6,256]{1,0:T(8,128)S(1)} %bitcast.28), channel_id=1, source_target_pairs={{4,0},{8,4},{12,8},{16,12},{20,16},{24,20},{28,24},{5,1},{9,5},{13... | collective-permute-start | bytes 18440 | tf_op jit(solution)/shard_map/ppermute | solution.py:408
  43.7 5.9 %collective-permute-start.10 = (f32[4,2,16,128]{3,2,1,0:T(8,128)S(1)}, f32[4,2,16,128]{3,2,1,0:T(8,128)S(1)}, u32[]{:S(2)}, u32[]{:S(2)}) collective-permute-start(f32[4,2,16,128]{3,2,1,0:T(8,128)S(1)} %get-tuple-element.12), channel_id=1, source_target_pairs={{0,1},{1,2},{2,3},{3,0},{4,5},{5,6},{6,7},{7,4},{8,9},{9,10},{10,1... | collective-permute-start | bytes 196616 | tf_op jit(solution)/shard_map/ppermute | solution.py:378
  44.1 6.2 %collective-permute-start.11 = (f32[4,2,16,128]{3,2,1,0:T(8,128)S(1)}, f32[4,2,16,128]{3,2,1,0:T(8,128)S(1)}, u32[]{:S(2)}, u32[]{:S(2)}) collective-permute-start(f32[4,2,16,128]{3,2,1,0:T(8,128)S(1)} %get-tuple-element.13), channel_id=1, source_target_pairs={{0,2},{1,3},{2,0},{3,1},{4,6},{5,7},{6,4},{7,5},{8,10},{9,11},{10,... | collective-permute-start | bytes 196616 | tf_op jit(solution)/shard_map/ppermute | solution.py:378
  46.3 6.9 %collective-permute-start.12 = (f32[4,2,16,128]{3,2,1,0:T(8,128)S(1)}, f32[4,2,16,128]{3,2,1,0:T(8,128)S(1)}, u32[]{:S(2)}, u32[]{:S(2)}) collective-permute-start(f32[4,2,16,128]{3,2,1,0:T(8,128)S(1)} %get-tuple-element.14), channel_id=1, source_target_pairs={{0,3},{1,0},{2,1},{3,2},{4,7},{5,4},{6,5},{7,6},{8,11},{9,8},{10,9... | collective-permute-start | bytes 196616 | tf_op jit(solution)/shard_map/ppermute | solution.py:378

commit v2 on v1

v2 whole, which is shorter than its diff:
```python
import functools

import jax
import jax.numpy as jnp
import ml_dtypes
import numpy as np
from jax import lax
from jax.experimental import pallas as pl
from jax.experimental.pallas import tpu as pltpu
from jax.sharding import PartitionSpec as P

MIG = 256
LANES = 128
MIB = 1 << 20

time_step = 0.2
coupling = 0.5
stretch = 1.5


def periodic_compact(points):
    index = np.arange(points)
    offset = (index[None, :] - index[:, None]) % points
    lhs = (offset == 0) + ((offset == 1) | (offset == points - 1)) / 3.0
    rhs = 7.0 / 9.0 * ((offset == 1) * 1.0 - (offset == points - 1))
    rhs = rhs + ((offset == 2) * 1.0 - (offset == points - 2)) / 36.0
    return np.linalg.solve(lhs, rhs)


def wall_compact(points):
    lhs = np.eye(points)
    rhs = np.zeros((points, points))
    for row in range(points):
        if row == 0:
            lhs[0, 1] = 2.0
            rhs[0, :3] = (-2.5, 2.0, 0.5)
        elif row == points - 1:
            lhs[row, row - 1] = 2.0
            rhs[row, -3:] = (-0.5, -2.0, 2.5)
        elif row in (1, points - 2):
            lhs[row, [row - 1, row + 1]] = 0.25
            rhs[row, [row - 1, row + 1]] = (-0.75, 0.75)
        else:
            lhs[row, [row - 1, row + 1]] = 1.0 / 3.0
            rhs[row, [row - 2, row - 1, row + 1, row + 2]] = (-1 / 36, -7 / 9, 7 / 9, 1 / 36)
    coord = -1.0 + 2.0 * np.arange(points) / (points - 1)
    slope = stretch * (1.0 - np.tanh(stretch * coord) ** 2) / np.tanh(stretch)
    return np.linalg.solve(lhs, rhs) / slope[:, None]


def spectral_matrix(points):
    index = np.arange(points)
    offset = index[:, None] - index[None, :]
    parity = 1 - 2 * (offset % 2)
    angle = np.pi * np.where(offset == 0, 1, offset) / points
    return np.where(offset == 0, 0.0, np.pi / points * parity / np.tan(angle))


def two_terms(matrix):
    exact = np.asarray(matrix, np.float32)
    high = exact.astype(ml_dtypes.bfloat16)
    low = (exact - high.astype(np.float32)).astype(ml_dtypes.bfloat16)
    return high, low


def split(value, terms):
    pieces = []
    for _ in range(terms):
        piece = value.astype(jnp.bfloat16)
        pieces.append(piece)
        value = value - piece.astype(jnp.float32)
    return pieces


def dot(a, b):
    return lax.dot_general(a, b, (((1,), (0,)), ((), ())), preferred_element_type=jnp.float32)


def dot_transposed(a, b):
    return lax.dot_general(a, b, (((1,), (1,)), ((), ())), preferred_element_type=jnp.float32)


def sublane_iota(rows, columns, dtype=jnp.int32):
    return lax.broadcasted_iota(dtype, (rows, columns), 0)


def is_row(rows, index):
    return sublane_iota(rows, index.shape[1], jnp.int16) == index.astype(jnp.int16)


def one_hot(rows, index):
    return jnp.where(is_row(rows, index), jnp.bfloat16(1), jnp.bfloat16(0))


def chunk_of(particles, rows):
    chunk = particles
    while chunk * rows > 1 << 20 and chunk % 256 == 0:
        chunk //= 2
    return chunk


def params(mib):
    return pltpu.CompilerParams(vmem_limit_bytes=mib * MIB)


CHEAP = pl.CostEstimate(flops=1, bytes_accessed=1, transcendentals=0)


def any_space(shape):
    return jax.ShapeDtypeStruct(tuple(shape), jnp.float32)


VMEM = pl.BlockSpec(memory_space=pltpu.VMEM)
SMEM = pl.BlockSpec(memory_space=pltpu.SMEM)


def advance_kernel(chunk, place_ref, count_ref, fields_ref, records_ref, response_ref, cell_ref, destination_ref,
                   slot_ref, kept_ref, force_ref, near_ref, side_ref, payload_ref, table_ref, total_ref):
    planes, width, lanes = fields_ref.shape[1:]
    rows = planes * width
    particles = records_ref.shape[1]
    for component in range(3):
        plane = fields_ref[component].reshape(rows, lanes).T
        high, low = split(plane, 2)
        table_ref[component * lanes:(component + 1) * lanes, :rows] = high
        table_ref[component * lanes:(component + 1) * lanes, rows:] = low
    groups = 4 * MIG // LANES

    def step(index, sums):
        window = pl.ds(index * chunk, chunk)
        cell = cell_ref[:, window]
        row_hot = one_hot(rows, cell // lanes)
        found = dot(table_ref[...], jnp.concatenate([row_hot, row_hot], axis=0))
        at_lane = sublane_iota(lanes, chunk) == cell % lanes
        fluid = jnp.concatenate(
            [jnp.sum(jnp.where(at_lane, found[a * lanes:(a + 1) * lanes], 0.0), axis=0, keepdims=True) for a in range(3)],
            axis=0)
        records = records_ref[:, window]
        speed = records[3:6]
        drag = (fluid - speed) / response_ref[:, window]
        velocity = speed + time_step * drag
        moved = jnp.concatenate([records[0:3] + time_step * velocity, velocity], axis=0)
        live = index * chunk + lax.broadcasted_iota(jnp.int32, (1, chunk), 1) < count_ref[0]
        destination = destination_ref[:, window]
        kept_ref[:, window] = jnp.where(live & (destination == 0), moved, 0.0)
        force_ref[:, window] = jnp.where(live, -coupling * drag, 0.0)
        target = jnp.where(live & (destination > 0), (destination - 1) * MIG + slot_ref[:, window], -LANES)
        group = target // LANES
        slot_hot = one_hot(LANES, target % LANES)
        padded = jnp.concatenate([moved, jnp.zeros((2, chunk), jnp.float32)], axis=0)
        pieces = []
        for _ in range(2):
            piece = padded.astype(jnp.bfloat16).astype(jnp.float32)
            padded = padded - piece
            pieces += [jnp.where(group == g, piece, 0.0) for g in range(groups)]
        sent = jnp.concatenate(pieces, axis=0).astype(jnp.bfloat16)
        return sums + dot_transposed(sent, slot_hot)

    total_ref[...] = jnp.zeros_like(total_ref)
    if chunk == particles:
        total_ref[...] = step(0, total_ref[...])
    else:
        def loop(index, carry):
            total_ref[...] = step(pl.multiple_of(index, 1), total_ref[...])
            return carry

        lax.fori_loop(0, particles // chunk, loop, 0)
    outgoing = (total_ref[:8 * groups] + total_ref[8 * groups:]).reshape(4, groups // 4, 8, LANES)
    even = lax.rem(place_ref[0], 2) == 0
    near_ref[...] = jnp.where(even, outgoing[0], outgoing[1])
    side_ref[...] = outgoing[2:]
    size = fields_ref.shape[0] * rows
    payload_ref[:size] = fields_ref[...].reshape(size, lanes)
    payload_ref[size:] = jnp.where(even, outgoing[1], outgoing[0]).reshape(-1, LANES)


def advance(place, counts, fields, records, response, cell, destination, slot):
    planes, width, lanes = fields.shape[1:]
    rows = planes * width
    particles = records.shape[1]
    groups = 4 * MIG // LANES
    box = (groups // 4, 8, LANES)
    payload = (fields.size // lanes + groups // 4 * 8, lanes)
    return pl.pallas_call(
        functools.partial(advance_kernel, chunk_of(particles, rows)),
        out_shape=(any_space((6, particles)), any_space((3, particles)), any_space(box), any_space((2, *box)), any_space(payload)),
        in_specs=[SMEM] * 2 + [VMEM] * 6,
        out_specs=(VMEM,) * 5,
        scratch_shapes=[pltpu.VMEM((3 * lanes, 2 * rows), jnp.bfloat16), pltpu.VMEM((16 * groups, LANES), jnp.float32)],
        compiler_params=params(40),
        cost_estimate=CHEAP,
        name="advance",
    )(place, counts, fields, records, response, cell, destination, slot)


def along_x_kernel(chunk, viscous_ref, fields_ref, operator_ref, cell_ref, force_ref, out_ref, total_ref):
    parts, planes, width, lanes = fields_ref.shape
    rows = planes * width
    half = rows // 2
    particles = cell_ref.shape[1]
    total_ref[...] = jnp.zeros_like(total_ref)

    def step(index):
        window = pl.ds(index * chunk, chunk)
        cell = cell_ref[:, window]
        row = cell // lanes
        column = jnp.where(row >= half, lanes, 0) + cell % lanes
        at_row = is_row(half, row % half)
        column_hot = one_hot(2 * lanes, column)
        pieces = []
        force = force_ref[:, window]
        for _ in range(2):
            piece = force.astype(jnp.bfloat16)
            force = force - piece.astype(jnp.float32)
            pieces += [jnp.where(at_row, piece[a:a + 1], jnp.bfloat16(0)) for a in range(3)]
        return dot_transposed(jnp.concatenate(pieces, axis=0), column_hot)

    if chunk == particles:
        total_ref[...] = step(0)
    else:
        def loop(index, carry):
            total_ref[...] += step(index)
            return carry

        lax.fori_loop(0, particles // chunk, loop, 0)
    for component in range(parts):
        viscous = viscous_ref[component]
        for plane in range(planes):
            field = fields_ref[component, plane]
            high, low = split(field, 2)
            stacked = jnp.concatenate([high, low, high], axis=0)
            both = dot(operator_ref[...], stacked)
            value = -fields_ref[0, plane] * both[:width] + viscous * both[width:]
            if component < 3:
                for start in range(plane * width, (plane + 1) * width, min(width, half)):
                    part, first = divmod(start, half)
                    size = min(width, half)
                    columns = slice(part * lanes, (part + 1) * lanes)
                    base = component * half + first
                    deposit = (total_ref[base:base + size, columns]
                               + total_ref[3 * half + base:3 * half + base + size, columns])
                    inside = start - plane * width
                    out_ref[component, plane, inside:inside + size] = value[inside:inside + size] + deposit
            else:
                out_ref[component, plane] = value


def along_x(viscous, fields, cell, force):
    parts, planes, width, lanes = fields.shape
    half = planes * width // 2
    particles = cell.shape[1]
    deriv = periodic_compact(width)
    high, low = two_terms(np.concatenate([deriv, deriv @ deriv], axis=0))
    operator = jnp.asarray(np.concatenate([high, high, low], axis=1))
    return pl.pallas_call(
        functools.partial(along_x_kernel, chunk_of(particles, 2 * half)),
        out_shape=any_space(fields.shape),
        in_specs=[SMEM] + [VMEM] * 4,
        out_specs=VMEM,
        scratch_shapes=[pltpu.VMEM((6 * half, 2 * lanes), jnp.float32)],
        compiler_params=params(40),
        cost_estimate=CHEAP,
        name="along_x",
    )(viscous, fields, operator, cell, force)


def along_z_kernel(viscous_ref, high_ref, low_ref, side_ref, *refs):
    count = len(refs) // 2
    blocks, results = refs[:count], refs[count:]
    parts, planes, width, lanes = blocks[0].shape
    rows = parts * planes * width
    pieces = [split(block[...].reshape(rows, lanes), 2) for block in blocks]

    def lines(term):
        return jnp.concatenate(
            [jnp.concatenate([pieces[(d - s) % count][term] for d in range(count)], axis=1) for s in range(count)], axis=0)

    high = lines(0)
    both = dot(high, high_ref[...]) + dot(lines(1), high_ref[...]) + dot(high, low_ref[...])
    for s in range(count):
        speed = blocks[(-s) % count][2]
        for component in range(parts):
            first = s * rows + component * planes * width
            part = both[first:first + planes * width]
            along = part[:, :lanes].reshape(planes, width, lanes)
            curve = part[:, lanes:].reshape(planes, width, lanes)
            value = -speed * along + viscous_ref[component] * curve
            results[s][component * planes * width:(component + 1) * planes * width] = value.reshape(planes * width, lanes)
        row = rows
        for direction in riding(s, count):
            for group in range(side_ref.shape[1]):
                results[s][row:row + 8] = side_ref[direction - 2, group]
                row += 8


def riding(s, count):
    return [direction for direction, step in ((2, 1), (3, -1)) if s == step % count]


def along_z(viscous, side, blocks):
    count = len(blocks)
    shape = blocks[0].shape
    lanes = shape[3]
    points = count * lanes
    deriv = spectral_matrix(points)
    second = deriv @ deriv
    weights = [
        np.concatenate([matrix[d * lanes:(d + 1) * lanes, :lanes].T for matrix in (deriv, second)], axis=1)
        for d in range(count)
    ]
    high, low = two_terms(np.concatenate(weights, axis=0))
    size = int(np.prod(shape))
    return pl.pallas_call(
        along_z_kernel,
        out_shape=tuple(any_space((size // lanes + MIG // LANES * 8 * len(riding(s, count)), lanes)) for s in range(count)),
        in_specs=[SMEM] + [VMEM] * (3 + count),
        out_specs=(VMEM,) * count,
        compiler_params=params(48),
        cost_estimate=CHEAP,
        name="along_z",
    )(viscous, jnp.asarray(high), jnp.asarray(low), side, *blocks)


def along_y_kernel(place_ref, weight_ref, near_ref, fields_ref, *refs):
    others, (own_ref, sibling_ref) = refs[:-2], refs[-2:]
    parts, planes, width, lanes = fields_ref.shape
    count = 2 * (len(others) + 1)
    size = parts * planes * width
    mine = place_ref[0] * (count * planes * planes * 2)
    step = min(width, 32)
    for component in range(parts):
        for first in range(0, width, step):
            sums = [[None] * 2 for _ in range(2 * planes)]
            for index in range(count // 2):
                for source in range(planes):
                    if index == 0:
                        value = fields_ref[component, source, first:first + step]
                    else:
                        row = (component * planes + source) * width + first
                        value = others[index - 1][row:row + step]
                    for target in range(2 * planes):
                        for kind in range(2):
                            weight = weight_ref[mine + ((index * planes + source) * 2 * planes + target) * 2 + kind]
                            before = sums[target][kind]
                            sums[target][kind] = weight * value if before is None else before + weight * value
            for plane in range(planes):
                for kind in range(2):
                    row = kind * size + (component * planes + plane) * width + first
                    own_ref[row:row + step] = sums[plane][kind]
                    sibling_ref[row:row + step] = sums[planes + plane][kind]
    extra = MIG // LANES * 8
    sibling_ref[2 * size:2 * size + extra] = near_ref[...].reshape(extra, lanes)
    me = place_ref[0]
    sibling = me ^ 1
    origin = jnp.where(lax.rem(sibling, 2) == 0, sibling - 1, sibling + 1)
    passed = jnp.zeros((extra, lanes), jnp.float32)
    for index, other in enumerate(others):
        if other.shape[0] > size:
            here = (origin >= 0) & (origin < count) & ((origin ^ me) == 2 * index + 2)
            passed = jnp.where(here, other[size:], passed)
    sibling_ref[2 * size + extra:] = passed


def carries_particles(s):
    return (s + 2) & (s + 1) == 0


def early_y(fields):
    rows = lax.axis_size("row")
    block = fields.reshape(-1, fields.shape[3])
    return {
        s: lax.ppermute(block, "row", [(i, i ^ s) for i in range(rows)])
        for s in range(2, rows, 2) if not carries_particles(s)
    }


def along_y(place, near, fields, payload, others, after):
    rows = lax.axis_size("row")
    planes = fields.shape[1]
    deriv = wall_compact(rows * planes)
    operators = np.stack([deriv, deriv @ deriv], axis=-1)
    table = np.zeros((rows, rows // 2, planes, 2, planes, 2), np.float32)
    for me in range(rows):
        for index in range(rows // 2):
            for side in range(2):
                target, source = (me ^ side) * planes, (me ^ (2 * index)) * planes
                block = operators[target:target + planes, source:source + planes]
                table[me, index, :, side] = block.transpose(1, 0, 2)
    for s in range(2, rows, 2):
        if carries_particles(s):
            others[s] = lax.ppermute(payload, "row", [(i, i ^ s) for i in range(rows)])
    others = [others[s] for s in range(2, rows, 2)]
    *others, _ = lax.optimization_barrier((*others, after))
    size = fields.size // fields.shape[3]
    own, sibling = pl.pallas_call(
        along_y_kernel,
        out_shape=(any_space((2 * size, LANES)), any_space((2 * size + MIG // LANES * 16, LANES))),
        in_specs=[SMEM] * 2 + [VMEM] * (2 + len(others)),
        out_specs=(VMEM, VMEM),
        compiler_params=params(32),
        cost_estimate=CHEAP,
        name="along_y",
    )(place, jnp.asarray(table.reshape(-1)), near, fields, *others)
    return own, lax.ppermute(sibling, "row", [(i, i ^ 1) for i in range(rows)])


def pencil_along_y(viscous, fields):
    highest = lax.Precision.HIGHEST
    pencil = lax.all_to_all(fields, "row", split_axis=2, concat_axis=1, tiled=True)
    deriv = wall_compact(pencil.shape[1])
    operators = [jnp.asarray(matrix, jnp.float32) for matrix in (deriv, deriv @ deriv)]
    along, curve = (jnp.einsum("ij,cjxz->cixz", matrix, pencil, precision=highest) for matrix in operators)
    partial = -pencil[1] * along + viscous[:, None, None, None] * curve
    return lax.all_to_all(partial, "row", split_axis=1, concat_axis=2, tiled=True)


def total_kernel(gathered, place_ref, viscous_ref, along_x_ref, *refs):
    own, refs = refs[:3] if gathered else refs[:2], refs[3:] if gathered else refs[2:]
    blocks, out_ref, arrivals_ref = refs[:-2], refs[-2], refs[-1]
    count = len(blocks)
    parts, planes, width, lanes = out_ref.shape
    size = width // count
    whole = parts * planes * width
    for s, block in enumerate(blocks):
        start = pl.multiple_of(lax.rem(place_ref[1] + count - s, count) * size, size)
        rows = pl.ds(start, size)
        for component in range(parts):
            for plane in range(planes):
                first = (component * planes + plane) * size
                value = along_x_ref[component, plane, rows, :] + block[first:first + size]
                if gathered:
                    fields_ref, own_ref, sibling_ref = own
                    row = pl.multiple_of((component * planes + plane) * width + start, size)
                    near, far = pl.ds(row, size), pl.ds(whole + row, size)
                    along = own_ref[near] + sibling_ref[near]
                    curve = own_ref[far] + sibling_ref[far]
                    value += viscous_ref[component] * curve - fields_ref[1, plane, rows, :] * along
                out_ref[component, plane, rows, :] = value
        first = parts * planes * size
        for direction in riding(s, count):
            for group in range(MIG // LANES):
                columns = slice(group * LANES, (group + 1) * LANES)
                arrivals_ref[:, direction, columns] = block[first:first + 6]
                first += 8
    even = lax.rem(place_ref[0], 2) == 0
    extra = MIG // LANES * 8
    for group in range(MIG // LANES):
        columns = slice(group * LANES, (group + 1) * LANES)
        if gathered:
            near = own[2][2 * whole + group * 8:2 * whole + group * 8 + 6]
            far = own[2][2 * whole + extra + group * 8:2 * whole + extra + group * 8 + 6]
        else:
            near, far = own[0][group, :6], own[1][group * 8:group * 8 + 6]
        arrivals_ref[:, 0, columns] = jnp.where(even, far, near)
        arrivals_ref[:, 1, columns] = jnp.where(even, near, far)


def total(gathered, place, viscous, along_x_part, own, blocks):
    size = along_x_part.size
    return pl.pallas_call(
        functools.partial(total_kernel, gathered),
        out_shape=(any_space(along_x_part.shape), any_space((6, 4, MIG))),
        in_specs=[SMEM] * 2 + [VMEM] * (1 + len(own) + len(blocks)),
        out_specs=(VMEM, VMEM),
        compiler_params=params(32),
        cost_estimate=CHEAP,
        name="total",
    )(place, viscous, along_x_part, *own, *blocks)


def exchange(blocks):
    count = lax.axis_size("col")
    received = list(blocks)
    for s in sorted(range(1, count), key=lambda s: -min(s, count - s)):
        received[s] = lax.ppermute(blocks[s], "col", [(i, (i + s) % count) for i in range(count)])
    return received


def on_device(fields, diffusivity, records, response_time, cell_index, counts, destination, slot):
    rows, columns = lax.axis_size("row"), lax.axis_size("col")
    column = lax.axis_index("col")
    place = jnp.stack([lax.axis_index("row"), column])
    width = fields.shape[2] // columns
    cell = cell_index.reshape(1, -1)
    blocks = [
        lax.dynamic_slice_in_dim(fields, (column + s) % columns * width, width, axis=2) for s in range(columns)
    ]
    lines = exchange(blocks)
    kept, force, near, side, payload = advance(
        place, counts, fields, records, response_time.reshape(1, -1), cell, destination.reshape(1, -1),
        slot.reshape(1, -1))
    others = early_y(fields)
    payload, side, lines, others = lax.optimization_barrier((payload, side, lines, others))
    terms_z = along_z(diffusivity, side, lines)
    force, *terms_z = lax.optimization_barrier((force, *terms_z))
    terms_z = exchange(terms_z)
    terms_x = along_x(diffusivity, fields, cell, force)
    gathered = rows & (rows - 1) == 0 and rows * fields.size * 4 <= 16 * MIB
    if gathered:
        own = (fields, *along_y(place, near, fields, payload, others, (terms_x, terms_z)))
    else:
        terms_x = terms_x + pencil_along_y(diffusivity, fields)
        pairs = [(i, i + 1) for i in range(1, rows - 1, 2)]
        far = payload[fields.size // fields.shape[3]:]
        own = (
            lax.ppermute(near, "row", [(i, i ^ 1) for i in range(rows) if i ^ 1 < rows]),
            lax.ppermute(far, "row", pairs + [(b, a) for a, b in pairs]),
        )
    tendency, arrivals = total(gathered, place, diffusivity, terms_x, own, terms_z)
    return (tendency, kept, arrivals.transpose(1, 0, 2))


def solution(mesh):
    return jax.shard_map(
        on_device,
        mesh=mesh,
        in_specs=(
            P(None, "row", None, "col"),
            P(),
            P(None, ("row", "col")),
            P(("row", "col")),
            P(("row", "col")),
            P(("row", "col")),
            P(("row", "col")),
            P(("row", "col")),
        ),
        out_specs=(
            P(None, "row", None, "col"),
            P(None, ("row", "col")),
            P(None, None, ("row", "col")),
        ),
        check_vma=False,
    )
```

time: 54.1 us -> 32.5 us (0.60)
  the two profiles are of different devices: /device:TPU:13 before, /device:TPU:0 now
where the time goes in v2:
time: 32.5 us; the launch traced here: 32.3 us
  starting transfers between devices  13.9 us (43%)
  Pallas kernels  10.6 us (33%)
  waiting for transfers between devices  5.3 us (16%)
  between operations  1.42 us (4%)
  local copies, waits for them, and re-layouts  1.08 us (3%)
    ppermute x6, starting transfers between devices, exchange(): lax.ppermute(blocks[s], 'col', [(i, (i + s) % count) for i in range(count)])  8.72 us
    pallas_call x1, Pallas kernels, advance(): pl.pallas_call(functools.partial(advance_kernel, chunk_of(particles, rows...  4.41 us
    ppermute x6, waiting for transfers between devices, exchange(): lax.ppermute(blocks[s], 'col', [(i, (i + s) % count) for i in range(count)])  3.17 us
    ppermute x1, starting transfers between devices, early_y(): lax.ppermute(block, 'row', [(i, i ^ s) for i in range(rows)])  3.03 us
    pallas_call x1, Pallas kernels, along_x(): pl.pallas_call(functools.partial(along_x_kernel, chunk_of(particles, 2 *...  2.51 us
    ppermute x2, starting transfers between devices, along_y(): others[s] = lax.ppermute(payload, 'row', [(i, i ^ s) for i in range(rows)])  2.04 us
    ppermute x1, waiting for transfers between devices, along_y(): lax.ppermute(sibling, 'row', [(i, i ^ 1) for i in range(rows)])  1.92 us
    pallas_call x1, Pallas kernels, total(): pl.pallas_call(functools.partial(total_kernel, gathered), out_shape=(any_...  1.37 us
  transfers between devices with their start and end apart: 10, of which 3 were waited for; matrix products, arithmetic and copies ran while one was open for 3% of the time, Pallas kernels for 25%

profile of v2, /device:TPU:0, one launch (start us, length us, event | category | flops | bytes accessed | tf_op | source)
XLA Modules:
  0.0 32.3 jit_solution(16712898143181797481)
XLA Ops:
  0.6 3.0 %collective-permute-start.3 = (f32[512,128]{1,0:T(8,128)}, f32[512,128]{1,0:T(8,128)S(1)}, u32[]{:S(2)}, u32[]{:S(2)}) collective-permute-start(f32[512,128]{1,0:T(8,128)} %bitcast.8), channel_id=1, source_target_pairs={{0,16},{4,20},{8,24},{12,28},{16,0},{20,4},{24,8},{28,12},{1,17},{... | collective-permute-start | bytes 786440 | tf_op jit(solution)/shard_map/ppermute | solution.py:372
  3.7 0.0 copy-start.8
  3.7 0.0 copy-start.7
  3.7 0.0 copy-start.6
  3.7 0.0 copy-start.4
  3.7 0.0 copy-start
  3.7 0.0 copy-start.1
  3.7 1.0 %constant_dynamic-slice_fusion = (f32[4,2,16,128]{3,2,1,0:T(8,128)S(1)}, f32[4,2,16,128]{3,2,1,0:T(8,128)S(1)}, f32[4,2,16,128]{3,2,1,0:T(8,128)S(1)}, f32[4,2,16,128]{3,2,1,0:T(8,128)S(1)}) fusion(f32[4,2,64,128]{3,2,1,0:T(8,128)} %refs_0_.1, s32[]{:T(128)S(6)} %select_n.38, s32[]{:T(128)S(6)} %select_n.36, s32[]{:T(128)S(6)} %select_n.34, s32[]{:T(128)S(6)} %select_n.32), kind=kLoop, calls=%fused_computation | loop fusion | bytes 524304 | tf_op jit(solution)/shard_map/dynamic_slice | solution.py:486
  4.7 3.7 %collective-permute-start.2 = (f32[4,2,16,128]{3,2,1,0:T(8,128)S(1)}, f32[4,2,16,128]{3,2,1,0:T(8,128)S(1)}, u32[]{:S(2)}, u32[]{:S(2)}) collective-permute-start(f32[4,2,16,128]{3,2,1,0:T(8,128)S(1)} %get-tuple-element.59), channel_id=1, source_target_pairs={{0,3},{1,0},{2,1},{3,2},{4,7},{5,4},{6,5},{7,6},{8,11},{9,8},{10,9... | collective-permute-start | bytes 196616 | tf_op jit(solution)/shard_map/ppermute | solution.py:475
  8.4 0.0 collective-permute-start.1
  8.4 1.0 %collective-permute-start = (f32[4,2,16,128]{3,2,1,0:T(8,128)S(1)}, f32[4,2,16,128]{3,2,1,0:T(8,128)S(1)}, u32[]{:S(2)}, u32[]{:S(2)}) collective-permute-start(f32[4,2,16,128]{3,2,1,0:T(8,128)S(1)} %get-tuple-element.61), channel_id=1, source_target_pairs={{0,1},{1,2},{2,3},{3,0},{4,5},{5,6},{6,7},{7,4},{8,9},{9,10},{10,1... | collective-permute-start | bytes 196616 | tf_op jit(solution)/shard_map/ppermute | solution.py:475
  10.1 0.1 pad_add_fusion.place_ref
  10.1 0.0 copy-done.8
  10.1 0.0 copy-done.7
  10.1 0.0 copy-done.6
  10.1 0.0 copy-done.4
  10.1 0.0 copy-done
  10.2 0.0 copy-done.1
  10.2 0.0 copy-start.2
  10.2 0.0 copy-start.3
  10.2 4.4 %advance.1 = (f32[6,8192]{1,0:T(8,128)}, f32[3,8192]{1,0:T(4,128)S(1)}, f32[2,8,128]{2,1,0:T(8,128)S(1)}, f32[2,2,8,128]{3,2,1,0:T(8,128)S(1)}, f32[528,128]{1,0:T(8,128)S(1)}) custom-call(s32[2]{0:T(128)S(1)} %pad_add_fusion.place_ref, s32[1]{0:T(128)S(6)} %copy.15.count_ref, f32[4,2,64,128]{3,2,1,0:T(8,128)S(1)} %copy-done, f32[6,8192]{1,0:T(8,128)S(1)} %copy-done.1, ...), custom_call_target="tpu_custom_call" | custom-call | flops 1 | bytes 1 | tf_op jit(solution)/shard_map/advance/pallas_call | solution.py:184
  14.6 0.0 collective-permute-done.2.refs_3_
  14.6 0.0 collective-permute-done.1.refs_2_
  14.6 0.0 collective-permute-done.refs_1_
  14.6 0.0 collective-permute-done.3.refs_1_
  14.6 0.0 copy-start.9
  14.6 0.0 copy-start.5
  14.6 1.5 %collective-permute-start.5 = (f32[528,128]{1,0:T(8,128)S(1)}, f32[528,128]{1,0:T(8,128)S(1)}, u32[]{:S(2)}, u32[]{:S(2)}) collective-permute-start(f32[528,128]{1,0:T(8,128)S(1)} %get-tuple-element.45), channel_id=1, source_target_pairs={{0,24},{4,28},{8,16},{12,20},{16,8},{20,12},{24,0},{28,4},{1,25},{... | collective-permute-start | bytes 811016 | tf_op jit(solution)/shard_map/ppermute | solution.py:391
  16.1 0.5 %collective-permute-start.4 = (f32[528,128]{1,0:T(8,128)S(1)}, f32[528,128]{1,0:T(8,128)S(1)}, u32[]{:S(2)}, u32[]{:S(2)}) collective-permute-start(f32[528,128]{1,0:T(8,128)S(1)} %get-tuple-element.45), channel_id=1, source_target_pairs={{0,8},{4,12},{8,0},{12,4},{16,24},{20,28},{24,16},{28,20},{1,9},{5... | collective-permute-start | bytes 811016 | tf_op jit(solution)/shard_map/ppermute | solution.py:391
  16.7 0.0 copy-done.2
  16.7 0.0 copy-done.3
  16.7 0.0 copy-done.9
  16.7 1.1 %along_z.1 = (f32[128,128]{1,0:T(8,128)S(1)}, f32[144,128]{1,0:T(8,128)S(1)}, f32[128,128]{1,0:T(8,128)S(1)}, f32[144,128]{1,0:T(8,128)S(1)}) custom-call(f32[4]{0:T(128)S(1)} %copy-done.9, bf16[512,256]{1,0:T(8,128)(2,1)S(1)} %copy-done.3, bf16[512,256]{1,0:T(8,128)(2,1)S(1)} %copy-done.2, f32[2,2,8,128]{3,2,1,0:T(8,128)S(1)} %get-tuple-element.34.side_ref, ...), custom_call_target="tpu_custom_call" | custom-call | flops 1 | bytes 1 | tf_op jit(solution)/shard_map/along_z/pallas_call | solution.py:313
  17.8 2.5 %collective-permute-start.6 = (f32[144,128]{1,0:T(8,128)S(1)}, f32[144,128]{1,0:T(8,128)S(1)}, u32[]{:S(2)}, u32[]{:S(2)}) collective-permute-start(f32[144,128]{1,0:T(8,128)S(1)} %get-tuple-element.48), channel_id=1, source_target_pairs={{0,1},{1,2},{2,3},{3,0},{4,5},{5,6},{6,7},{7,4},{8,9},{9,10},{10,1... | collective-permute-start | bytes 221192 | tf_op jit(solution)/shard_map/ppermute | solution.py:475
  20.3 1.3 %collective-permute-start.8 = (f32[144,128]{1,0:T(8,128)S(1)}, f32[144,128]{1,0:T(8,128)S(1)}, u32[]{:S(2)}, u32[]{:S(2)}) collective-permute-start(f32[144,128]{1,0:T(8,128)S(1)} %get-tuple-element.50), channel_id=1, source_target_pairs={{0,3},{1,0},{2,1},{3,2},{4,7},{5,4},{6,5},{7,6},{8,11},{9,8},{10,9... | collective-permute-start | bytes 221192 | tf_op jit(solution)/shard_map/ppermute | solution.py:475
  21.7 0.2 collective-permute-start.7
  21.9 0.0 copy-done.5
  21.9 0.0 copy-start.10
  21.9 2.5 %along_x.1.along_x_ref = f32[4,2,64,128]{3,2,1,0:T(8,128)S(1)} custom-call(f32[4]{0:T(128)S(1)} %copy-done.9, f32[4,2,64,128]{3,2,1,0:T(8,128)S(1)} %copy-done, bf16[128,192]{1,0:T(8,128)(2,1)S(1)} %copy-done.5, s32[1,8192]{1,0:T(1,128)S(1)} %bitcast.10, f32[3,8192]{1,0:T(4,128)S(1)} %get-tuple-element.43.force_ref), custom_call_target="tpu_custom_call" | custom-call | flops 1 | bytes 1 | tf_op jit(solution)/shard_map/along_x/pallas_call | solution.py:255
  24.4 3.2 %collective-permute-done.7.refs_5_ = f32[128,128]{1,0:T(8,128)S(1)} collective-permute-done((f32[128,128]{1,0:T(8,128)S(1)}, f32[128,128]{1,0:T(8,128)S(1)}, u32[]{:S(2)}, u32[]{:S(2)}) %collective-permute-start.7) | collective-permute-done | bytes 65568 | tf_op jit(solution)/shard_map/ppermute | solution.py:475
  27.6 0.0 collective-permute-done.6.refs_4_
  27.6 0.0 collective-permute-done.8.refs_6_
  27.6 0.0 collective-permute-done.5.refs_2_
  27.6 0.2 collective-permute-done.4.refs_0_
  27.8 0.0 copy-done.10
  27.8 1.2 %along_y.1 = (f32[1024,128]{1,0:T(8,128)S(1)}, f32[1056,128]{1,0:T(8,128)S(1)}) custom-call(s32[2]{0:T(128)S(1)} %pad_add_fusion.place_ref, f32[512]{0:T(512)S(1)} %copy-done.10, f32[2,8,128]{2,1,0:T(8,128)S(1)} %get-tuple-element.44.near_ref, f32[4,2,64,128]{3,2,1,0:T(8,128)S(1)} %copy-done, f32[528,128]{1,0:T(8,128)S(1)} %collective-permute-done.4.refs_0_, ...), custom_call_target="tpu_custom_call" | custom-call | flops 1 | bytes 1 | tf_op jit(solution)/shard_map/along_y/pallas_call | solution.py:395
  29.0 0.1 collective-permute-start.9
  29.0 1.9 %collective-permute-done.9.refs_2_ = f32[1056,128]{1,0:T(8,128)S(1)} collective-permute-done((f32[1056,128]{1,0:T(8,128)S(1)}, f32[1056,128]{1,0:T(8,128)S(1)}, u32[]{:S(2)}, u32[]{:S(2)}) %collective-permute-start.9) | collective-permute-done | bytes 540704 | tf_op jit(solution)/shard_map/ppermute | solution.py:404
  31.0 1.4 %total.1 = (f32[4,2,64,128]{3,2,1,0:T(8,128)}, f32[6,4,256]{2,1,0:T(4,128)}) custom-call(s32[2]{0:T(128)S(1)} %pad_add_fusion.place_ref, f32[4]{0:T(128)S(1)} %copy-done.9, f32[4,2,64,128]{3,2,1,0:T(8,128)S(1)} %along_x.1.along_x_ref, f32[4,2,64,128]{3,2,1,0:T(8,128)S(1)} %copy-done, f32[1024,128]{1,0:T(8,128)S(1)} %get-tuple-element.54.refs_1_, ...), custom_call_target="tpu_custom_call" | custom-call | flops 1 | bytes 1 | tf_op jit(solution)/shard_map/total/pallas_call | solution.py:460
Async XLA Ops:
  0.6 14.0 %collective-permute-start.3 = (f32[512,128]{1,0:T(8,128)}, f32[512,128]{1,0:T(8,128)S(1)}, u32[]{:S(2)}, u32[]{:S(2)}) collective-permute-start(f32[512,128]{1,0:T(8,128)} %bitcast.8), channel_id=1, source_target_pairs={{0,16},{4,20},{8,24},{12,28},{16,0},{20,4},{24,8},{28,12},{1,17},{... | collective-permute-start | bytes 786440 | tf_op jit(solution)/shard_map/ppermute | solution.py:372
  3.7 6.5 %copy-start.8 = (s32[8192]{0:T(1024)S(1)}, s32[8192]{0:T(1024)}, u32[]{:S(2)}) copy-start(s32[8192]{0:T(1024)} %param.19) | copy-start | bytes 98308
  3.7 6.5 %copy-start.7 = (s32[8192]{0:T(1024)S(1)}, s32[8192]{0:T(1024)}, u32[]{:S(2)}) copy-start(s32[8192]{0:T(1024)} %param.18) | copy-start | bytes 98308
  3.7 6.5 %copy-start.6 = (f32[8192]{0:T(1024)S(1)}, f32[8192]{0:T(1024)}, u32[]{:S(2)}) copy-start(f32[8192]{0:T(1024)} %param.15) | copy-start | bytes 98308
  3.7 6.5 %copy-start.4 = (s32[8192]{0:T(1024)S(1)}, s32[8192]{0:T(1024)}, u32[]{:S(2)}) copy-start(s32[8192]{0:T(1024)} %param.16) | copy-start | bytes 98308
  3.7 6.5 %copy-start = (f32[4,2,64,128]{3,2,1,0:T(8,128)S(1)}, f32[4,2,64,128]{3,2,1,0:T(8,128)}, u32[]{:S(2)}) copy-start(f32[4,2,64,128]{3,2,1,0:T(8,128)} %refs_0_.1) | copy-start | bytes 786436
  3.7 6.5 %copy-start.1 = (f32[6,8192]{1,0:T(8,128)S(1)}, f32[6,8192]{1,0:T(8,128)}, u32[]{:S(2)}) copy-start(f32[6,8192]{1,0:T(8,128)} %records_ref.1) | copy-start | bytes 589828
  4.7 9.9 %collective-permute-start.2 = (f32[4,2,16,128]{3,2,1,0:T(8,128)S(1)}, f32[4,2,16,128]{3,2,1,0:T(8,128)S(1)}, u32[]{:S(2)}, u32[]{:S(2)}) collective-permute-start(f32[4,2,16,128]{3,2,1,0:T(8,128)S(1)} %get-tuple-element.59), channel_id=1, source_target_pairs={{0,3},{1,0},{2,1},{3,2},{4,7},{5,4},{6,5},{7,6},{8,11},{9,8},{10,9... | collective-permute-start | bytes 196616 | tf_op jit(solution)/shard_map/ppermute | solution.py:475
  8.4 6.2 %collective-permute-start.1 = (f32[4,2,16,128]{3,2,1,0:T(8,128)S(1)}, f32[4,2,16,128]{3,2,1,0:T(8,128)S(1)}, u32[]{:S(2)}, u32[]{:S(2)}) collective-permute-start(f32[4,2,16,128]{3,2,1,0:T(8,128)S(1)} %get-tuple-element.60), channel_id=1, source_target_pairs={{0,2},{1,3},{2,0},{3,1},{4,6},{5,7},{6,4},{7,5},{8,10},{9,11},{10,... | collective-permute-start | bytes 196616 | tf_op jit(solution)/shard_map/ppermute | solution.py:475
  8.4 6.2 %collective-permute-start = (f32[4,2,16,128]{3,2,1,0:T(8,128)S(1)}, f32[4,2,16,128]{3,2,1,0:T(8,128)S(1)}, u32[]{:S(2)}, u32[]{:S(2)}) collective-permute-start(f32[4,2,16,128]{3,2,1,0:T(8,128)S(1)} %get-tuple-element.61), channel_id=1, source_target_pairs={{0,1},{1,2},{2,3},{3,0},{4,5},{5,6},{6,7},{7,4},{8,9},{9,10},{10,1... | collective-permute-start | bytes 196616 | tf_op jit(solution)/shard_map/ppermute | solution.py:475
  10.2 6.5 %copy-start.2 = (bf16[512,256]{1,0:T(8,128)(2,1)S(1)}, bf16[512,256]{1,0:T(8,128)(2,1)}, u32[]{:S(2)}) copy-start(bf16[512,256]{1,0:T(8,128)(2,1)} %constant.53.clone.low_ref) | copy-start | bytes 786436
  10.2 6.5 %copy-start.3 = (bf16[512,256]{1,0:T(8,128)(2,1)S(1)}, bf16[512,256]{1,0:T(8,128)(2,1)}, u32[]{:S(2)}) copy-start(bf16[512,256]{1,0:T(8,128)(2,1)} %constant.52.clone.high_ref) | copy-start | bytes 786436
  14.6 2.1 %copy-start.9 = (f32[4]{0:T(128)S(1)}, f32[4]{0:T(128)}, u32[]{:S(2)}) copy-start(f32[4]{0:T(128)} %viscous_ref.5) | copy-start | bytes 52
  14.6 7.2 %copy-start.5 = (bf16[128,192]{1,0:T(8,128)(2,1)S(1)}, bf16[128,192]{1,0:T(8,128)(2,1)}, u32[]{:S(2)}) copy-start(bf16[128,192]{1,0:T(8,128)(2,1)} %constant.54.clone.operator_ref) | copy-start | bytes 147460
  14.6 12.9 %collective-permute-start.5 = (f32[528,128]{1,0:T(8,128)S(1)}, f32[528,128]{1,0:T(8,128)S(1)}, u32[]{:S(2)}, u32[]{:S(2)}) collective-permute-start(f32[528,128]{1,0:T(8,128)S(1)} %get-tuple-element.45), channel_id=1, source_target_pairs={{0,24},{4,28},{8,16},{12,20},{16,8},{20,12},{24,0},{28,4},{1,25},{... | collective-permute-start | bytes 811016 | tf_op jit(solution)/shard_map/ppermute | solution.py:391
  16.1 11.6 %collective-permute-start.4 = (f32[528,128]{1,0:T(8,128)S(1)}, f32[528,128]{1,0:T(8,128)S(1)}, u32[]{:S(2)}, u32[]{:S(2)}) collective-permute-start(f32[528,128]{1,0:T(8,128)S(1)} %get-tuple-element.45), channel_id=1, source_target_pairs={{0,8},{4,12},{8,0},{12,4},{16,24},{20,28},{24,16},{28,20},{1,9},{5... | collective-permute-start | bytes 811016 | tf_op jit(solution)/shard_map/ppermute | solution.py:391
  17.8 9.7 %collective-permute-start.6 = (f32[144,128]{1,0:T(8,128)S(1)}, f32[144,128]{1,0:T(8,128)S(1)}, u32[]{:S(2)}, u32[]{:S(2)}) collective-permute-start(f32[144,128]{1,0:T(8,128)S(1)} %get-tuple-element.48), channel_id=1, source_target_pairs={{0,1},{1,2},{2,3},{3,0},{4,5},{5,6},{6,7},{7,4},{8,9},{9,10},{10,1... | collective-permute-start | bytes 221192 | tf_op jit(solution)/shard_map/ppermute | solution.py:475
  20.3 7.2 %collective-permute-start.8 = (f32[144,128]{1,0:T(8,128)S(1)}, f32[144,128]{1,0:T(8,128)S(1)}, u32[]{:S(2)}, u32[]{:S(2)}) collective-permute-start(f32[144,128]{1,0:T(8,128)S(1)} %get-tuple-element.50), channel_id=1, source_target_pairs={{0,3},{1,0},{2,1},{3,2},{4,7},{5,4},{6,5},{7,6},{8,11},{9,8},{10,9... | collective-permute-start | bytes 221192 | tf_op jit(solution)/shard_map/ppermute | solution.py:475
  21.7 5.9 %collective-permute-start.7 = (f32[128,128]{1,0:T(8,128)S(1)}, f32[128,128]{1,0:T(8,128)S(1)}, u32[]{:S(2)}, u32[]{:S(2)}) collective-permute-start(f32[128,128]{1,0:T(8,128)S(1)} %get-tuple-element.49), channel_id=1, source_target_pairs={{0,2},{1,3},{2,0},{3,1},{4,6},{5,7},{6,4},{7,5},{8,10},{9,11},{10,... | collective-permute-start | bytes 196616 | tf_op jit(solution)/shard_map/ppermute | solution.py:475
  21.9 5.9 %copy-start.10 = (f32[512]{0:T(512)S(1)}, f32[512]{0:T(512)}, u32[]{:S(2)}) copy-start(f32[512]{0:T(512)} %constant.55.clone.weight_ref) | copy-start | bytes 6148
  29.0 2.0 %collective-permute-start.9 = (f32[1056,128]{1,0:T(8,128)S(1)}, f32[1056,128]{1,0:T(8,128)S(1)}, u32[]{:S(2)}, u32[]{:S(2)}) collective-permute-start(f32[1056,128]{1,0:T(8,128)S(1)} %get-tuple-element.55), channel_id=1, source_target_pairs={{0,4},{4,0},{8,12},{12,8},{16,20},{20,16},{24,28},{28,24},{1,5},{5... | collective-permute-start | bytes 1622024 | tf_op jit(solution)/shard_map/ppermute | solution.py:404

commit v3 on v2

v3 whole, which is shorter than its diff:
```python
import functools

import jax
import jax.numpy as jnp
import ml_dtypes
import numpy as np
from jax import lax
from jax.experimental import pallas as pl
from jax.experimental.pallas import tpu as pltpu
from jax.sharding import PartitionSpec as P

MIG = 256
LANES = 128
MIB = 1 << 20

time_step = 0.2
coupling = 0.5
stretch = 1.5


def periodic_compact(points):
    index = np.arange(points)
    offset = (index[None, :] - index[:, None]) % points
    lhs = (offset == 0) + ((offset == 1) | (offset == points - 1)) / 3.0
    rhs = 7.0 / 9.0 * ((offset == 1) * 1.0 - (offset == points - 1))
    rhs = rhs + ((offset == 2) * 1.0 - (offset == points - 2)) / 36.0
    return np.linalg.solve(lhs, rhs)


def wall_compact(points):
    lhs = np.eye(points)
    rhs = np.zeros((points, points))
    for row in range(points):
        if row == 0:
            lhs[0, 1] = 2.0
            rhs[0, :3] = (-2.5, 2.0, 0.5)
        elif row == points - 1:
            lhs[row, row - 1] = 2.0
            rhs[row, -3:] = (-0.5, -2.0, 2.5)
        elif row in (1, points - 2):
            lhs[row, [row - 1, row + 1]] = 0.25
            rhs[row, [row - 1, row + 1]] = (-0.75, 0.75)
        else:
            lhs[row, [row - 1, row + 1]] = 1.0 / 3.0
            rhs[row, [row - 2, row - 1, row + 1, row + 2]] = (-1 / 36, -7 / 9, 7 / 9, 1 / 36)
    coord = -1.0 + 2.0 * np.arange(points) / (points - 1)
    slope = stretch * (1.0 - np.tanh(stretch * coord) ** 2) / np.tanh(stretch)
    return np.linalg.solve(lhs, rhs) / slope[:, None]


def spectral_matrix(points):
    index = np.arange(points)
    offset = index[:, None] - index[None, :]
    parity = 1 - 2 * (offset % 2)
    angle = np.pi * np.where(offset == 0, 1, offset) / points
    return np.where(offset == 0, 0.0, np.pi / points * parity / np.tan(angle))


def two_terms(matrix):
    exact = np.asarray(matrix, np.float32)
    high = exact.astype(ml_dtypes.bfloat16)
    low = (exact - high.astype(np.float32)).astype(ml_dtypes.bfloat16)
    return high, low


def split(value, terms):
    pieces = []
    for _ in range(terms):
        piece = value.astype(jnp.bfloat16)
        pieces.append(piece)
        value = value - piece.astype(jnp.float32)
    return pieces


def dot(a, b):
    return lax.dot_general(a, b, (((1,), (0,)), ((), ())), preferred_element_type=jnp.float32)


def dot_transposed(a, b):
    return lax.dot_general(a, b, (((1,), (1,)), ((), ())), preferred_element_type=jnp.float32)


def sublane_iota(rows, columns, dtype=jnp.int32):
    return lax.broadcasted_iota(dtype, (rows, columns), 0)


def is_row(rows, index):
    return sublane_iota(rows, index.shape[1], jnp.int16) == index.astype(jnp.int16)


def one_hot(rows, index):
    return jnp.where(is_row(rows, index), jnp.bfloat16(1), jnp.bfloat16(0))


def divide(value, by):
    if by & (by - 1):
        return lax.div(value, by), lax.rem(value, by)
    return lax.shift_right_logical(value, by.bit_length() - 1), value & (by - 1)


def chunk_of(particles, rows):
    chunk = particles
    while chunk * rows > 1 << 20 and chunk % 256 == 0:
        chunk //= 2
    return chunk


def params(mib):
    return pltpu.CompilerParams(vmem_limit_bytes=mib * MIB)


CHEAP = pl.CostEstimate(flops=1, bytes_accessed=1, transcendentals=0)
LONG = pl.CostEstimate(flops=20 * 10**9, bytes_accessed=100 * 10**6, transcendentals=0)


def any_space(shape):
    return jax.ShapeDtypeStruct(tuple(shape), jnp.float32)


VMEM = pl.BlockSpec(memory_space=pltpu.VMEM)
SMEM = pl.BlockSpec(memory_space=pltpu.SMEM)


def advance_kernel(chunk, row_ref, count_ref, fields_ref, records_ref, response_ref, cell_ref, destination_ref,
                   slot_ref, kept_ref, force_ref, near_ref, far_ref, side_ref, table_ref, total_ref):
    planes, width, lanes = fields_ref.shape[1:]
    rows = planes * width
    particles = records_ref.shape[1]
    for component in range(3):
        plane = fields_ref[component].reshape(rows, lanes).T
        high, low = split(plane, 2)
        table_ref[component * lanes:(component + 1) * lanes, :rows] = high
        table_ref[component * lanes:(component + 1) * lanes, rows:] = low
    groups = 4 * MIG // LANES

    def step(index, sums):
        window = pl.ds(index * chunk, chunk)
        cell = cell_ref[:, window]
        row, lane = divide(cell, lanes)
        row_hot = one_hot(rows, row)
        found = dot(table_ref[...], jnp.concatenate([row_hot, row_hot], axis=0))
        at_lane = sublane_iota(lanes, chunk) == lane
        fluid = jnp.concatenate(
            [jnp.sum(jnp.where(at_lane, found[a * lanes:(a + 1) * lanes], 0.0), axis=0, keepdims=True) for a in range(3)],
            axis=0)
        records = records_ref[:, window]
        speed = records[3:6]
        drag = (fluid - speed) / response_ref[:, window]
        velocity = speed + time_step * drag
        moved = jnp.concatenate([records[0:3] + time_step * velocity, velocity], axis=0)
        live = index * chunk + lax.broadcasted_iota(jnp.int32, (1, chunk), 1) < count_ref[...]
        destination = destination_ref[:, window]
        kept_ref[:, window] = jnp.where(live & (destination == 0), moved, 0.0)
        force_ref[:, window] = jnp.where(live, -coupling * drag, 0.0)
        leaving = live & (destination > 0)
        group, place = divide(slot_ref[:, window], LANES)
        group = jnp.where(leaving, (destination - 1) * (MIG // LANES) + group, -1)
        slot_hot = one_hot(LANES, place)
        padded = jnp.concatenate([moved, jnp.zeros((2, chunk), jnp.float32)], axis=0)
        pieces = []
        for _ in range(2):
            piece = padded.astype(jnp.bfloat16).astype(jnp.float32)
            padded = padded - piece
            pieces += [jnp.where(group == g, piece, 0.0) for g in range(groups)]
        sent = jnp.concatenate(pieces, axis=0).astype(jnp.bfloat16)
        return sums + dot_transposed(sent, slot_hot)

    total_ref[...] = jnp.zeros_like(total_ref)
    if chunk == particles:
        total_ref[...] = step(0, total_ref[...])
    else:
        def loop(index, carry):
            total_ref[...] = step(pl.multiple_of(index, 1), total_ref[...])
            return carry

        lax.fori_loop(0, particles // chunk, loop, 0)
    outgoing = (total_ref[:8 * groups] + total_ref[8 * groups:]).reshape(4, groups // 4, 8, LANES)
    even = lax.rem(row_ref[0], 2) == 0
    near_ref[...] = jnp.where(even, outgoing[0], outgoing[1])
    side_ref[...] = outgoing[2:]
    far_ref[...] = jnp.where(even, outgoing[1], outgoing[0])


def advance(row, counts, fields, records, response, cell, destination, slot):
    planes, width, lanes = fields.shape[1:]
    rows = planes * width
    particles = records.shape[1]
    groups = 4 * MIG // LANES
    box = (groups // 4, 8, LANES)
    return pl.pallas_call(
        functools.partial(advance_kernel, chunk_of(particles, rows)),
        out_shape=(any_space((6, particles)), any_space((3, particles)), any_space(box), any_space(box), any_space((2, *box))),
        in_specs=[SMEM] + [VMEM] * 7,
        out_specs=(VMEM,) * 5,
        scratch_shapes=[pltpu.VMEM((3 * lanes, 2 * rows), jnp.bfloat16), pltpu.VMEM((16 * groups, LANES), jnp.float32)],
        compiler_params=params(40),
        cost_estimate=CHEAP,
        name="advance",
    )(row, counts, fields, records, response, cell, destination, slot)


def along_xy_kernel(chunk, viscous_ref, fields_ref, operator_ref, cell_ref, force_ref, *refs):
    *y_refs, out_ref, total_ref = refs
    if y_refs:
        *y_refs, out_ref, sibling_ref, total_ref = refs
    parts, planes, width, lanes = fields_ref.shape
    rows = planes * width
    half = rows // 2
    particles = cell_ref.shape[1]
    total_ref[...] = jnp.zeros_like(total_ref)

    def step(index):
        window = pl.ds(index * chunk, chunk)
        cell = cell_ref[:, window]
        row, lane = divide(cell, lanes)
        part, row = divide(row, half)
        column = part * lanes + lane
        at_row = is_row(half, row)
        column_hot = one_hot(2 * lanes, column)
        pieces = []
        force = force_ref[:, window]
        for _ in range(2):
            piece = force.astype(jnp.bfloat16)
            force = force - piece.astype(jnp.float32)
            pieces += [jnp.where(at_row, piece[a:a + 1], jnp.bfloat16(0)) for a in range(3)]
        return dot_transposed(jnp.concatenate(pieces, axis=0), column_hot)

    if chunk == particles:
        total_ref[...] = step(0)
    else:
        def loop(index, carry):
            total_ref[...] += step(index)
            return carry

        lax.fori_loop(0, particles // chunk, loop, 0)
    for component in range(parts):
        viscous = viscous_ref[component]
        for plane in range(planes):
            field = fields_ref[component, plane]
            high, low = split(field, 2)
            stacked = jnp.concatenate([high, low, high], axis=0)
            both = dot(operator_ref[...], stacked)
            value = -fields_ref[0, plane] * both[:width] + viscous * both[width:]
            if component < 3:
                for start in range(plane * width, (plane + 1) * width, min(width, half)):
                    part, first = divmod(start, half)
                    size = min(width, half)
                    columns = slice(part * lanes, (part + 1) * lanes)
                    base = component * half + first
                    deposit = (total_ref[base:base + size, columns]
                               + total_ref[3 * half + base:3 * half + base + size, columns])
                    inside = start - plane * width
                    out_ref[component, plane, inside:inside + size] = value[inside:inside + size] + deposit
            else:
                out_ref[component, plane] = value
    if not y_refs:
        return
    row_ref, weight_ref, near_ref, mate_ref, *others = y_refs
    count = 2 * (len(others) + 1)
    size = parts * planes * width
    mine = row_ref[0] * (count * planes * planes * 2)
    step = min(width, 32)
    for component in range(parts):
        for first in range(0, width, step):
            inside = slice(first, first + step)
            sums = [[None] * 2 for _ in range(2 * planes)]
            for index in range(count // 2):
                block = others[index - 1] if index else fields_ref
                for source in range(planes):
                    value = block[component, source, inside]
                    for target in range(2 * planes):
                        for kind in range(2):
                            weight = weight_ref[mine + ((index * planes + source) * 2 * planes + target) * 2 + kind]
                            before = sums[target][kind]
                            sums[target][kind] = weight * value if before is None else before + weight * value
            for plane in range(planes):
                along, curve = sums[plane]
                out_ref[component, plane, inside] += viscous_ref[component] * curve - fields_ref[1, plane, inside] * along
                along, curve = sums[planes + plane]
                row = (component * planes + plane) * width + first
                sibling_ref[row:row + step] = viscous_ref[component] * curve - mate_ref[1, plane, inside] * along
    sibling_ref[size:] = near_ref[...].reshape(MIG // LANES * 8, lanes)


def same_core(block, s):
    return lax.ppermute(block, "row", [(i, i ^ s) for i in range(lax.axis_size("row"))])


def along_y_weights(rows, planes):
    deriv = wall_compact(rows * planes)
    operators = np.stack([deriv, deriv @ deriv], axis=-1)
    table = np.zeros((rows, rows // 2, planes, 2, planes, 2), np.float32)
    for me in range(rows):
        for index in range(rows // 2):
            for side in range(2):
                target, source = (me ^ side) * planes, (me ^ (2 * index)) * planes
                block = operators[target:target + planes, source:source + planes]
                table[me, index, :, side] = block.transpose(1, 0, 2)
    return jnp.asarray(table.reshape(-1))


def along_xy(viscous, fields, cell, force, y_part):
    parts, planes, width, lanes = fields.shape
    half = planes * width // 2
    particles = cell.shape[1]
    deriv = periodic_compact(width)
    high, low = two_terms(np.concatenate([deriv, deriv @ deriv], axis=0))
    operator = jnp.asarray(np.concatenate([high, high, low], axis=1))
    specs, outs = [], [any_space(fields.shape)]
    if y_part:
        row, near, mate, others = y_part
        y_part = (row, along_y_weights(lax.axis_size("row"), planes), near, mate, *others)
        specs = [SMEM] * 2 + [VMEM] * (2 + len(others))
        outs.append(any_space((fields.size // lanes + MIG // LANES * 8, lanes)))
    return pl.pallas_call(
        functools.partial(along_xy_kernel, chunk_of(particles, 2 * half)),
        out_shape=tuple(outs),
        in_specs=[SMEM] + [VMEM] * 4 + specs,
        out_specs=(VMEM,) * len(outs),
        scratch_shapes=[pltpu.VMEM((6 * half, 2 * lanes), jnp.float32)],
        compiler_params=params(40),
        cost_estimate=CHEAP,
        name="along_xy",
    )(viscous, fields, operator, cell, force, *y_part)


def along_z_kernel(viscous_ref, high_ref, low_ref, side_ref, *refs):
    count = len(refs) // 2
    blocks, results = refs[:count], refs[count:]
    parts, planes, width, lanes = blocks[0].shape
    rows = parts * planes * width
    pieces = [split(block[...].reshape(rows, lanes), 2) for block in blocks]

    def lines(term):
        return jnp.concatenate(
            [jnp.concatenate([pieces[(d - s) % count][term] for d in range(count)], axis=1) for s in range(count)], axis=0)

    high = lines(0)
    both = dot(high, high_ref[...]) + dot(lines(1), high_ref[...]) + dot(high, low_ref[...])
    for s in range(count):
        speed = blocks[(-s) % count][2]
        for component in range(parts):
            first = s * rows + component * planes * width
            part = both[first:first + planes * width]
            along = part[:, :lanes].reshape(planes, width, lanes)
            curve = part[:, lanes:].reshape(planes, width, lanes)
            value = -speed * along + viscous_ref[component] * curve
            results[s][component * planes * width:(component + 1) * planes * width] = value.reshape(planes * width, lanes)
        row = rows
        for direction in riding(s, count):
            for group in range(side_ref.shape[1]):
                results[s][row:row + 8] = side_ref[direction - 2, group]
                row += 8


def riding(s, count):
    return [direction for direction, step in ((2, 1), (3, -1)) if s == step % count]


def along_z(viscous, side, blocks):
    count = len(blocks)
    shape = blocks[0].shape
    lanes = shape[3]
    points = count * lanes
    deriv = spectral_matrix(points)
    second = deriv @ deriv
    weights = [
        np.concatenate([matrix[d * lanes:(d + 1) * lanes, :lanes].T for matrix in (deriv, second)], axis=1)
        for d in range(count)
    ]
    high, low = two_terms(np.concatenate(weights, axis=0))
    size = int(np.prod(shape))
    return pl.pallas_call(
        along_z_kernel,
        out_shape=tuple(any_space((size // lanes + MIG // LANES * 8 * len(riding(s, count)), lanes)) for s in range(count)),
        in_specs=[SMEM] + [VMEM] * (3 + count),
        out_specs=(VMEM,) * count,
        compiler_params=params(48),
        cost_estimate=CHEAP,
        name="along_z",
    )(viscous, jnp.asarray(high), jnp.asarray(low), side, *blocks)


def pencil_along_y(viscous, fields):
    highest = lax.Precision.HIGHEST
    pencil = lax.all_to_all(fields, "row", split_axis=2, concat_axis=1, tiled=True)
    deriv = wall_compact(pencil.shape[1])
    operators = [jnp.asarray(matrix, jnp.float32) for matrix in (deriv, deriv @ deriv)]
    along, curve = (jnp.einsum("ij,cjxz->cixz", matrix, pencil, precision=highest) for matrix in operators)
    partial = -pencil[1] * along + viscous[:, None, None, None] * curve
    return lax.all_to_all(partial, "row", split_axis=1, concat_axis=2, tiled=True)


def side_kernel(first, *refs):
    blocks, out_ref = refs[:-1], refs[-1]
    for s, block in enumerate(blocks):
        row = first
        for direction in riding(s, len(blocks)):
            for group in range(out_ref.shape[1]):
                out_ref[direction - 2, group] = block[row:row + 8]
                row += 8


def side_particles(blocks):
    first = min(block.shape[0] for block in blocks)
    return pl.pallas_call(
        functools.partial(side_kernel, first),
        out_shape=any_space((2, MIG // LANES, 8, LANES)),
        in_specs=[VMEM] * len(blocks),
        out_specs=VMEM,
        compiler_params=params(8),
        cost_estimate=LONG,
        name="side_particles",
    )(*blocks)


def total_kernel(gathered, row_ref, column_ref, along_x_ref, far_ref, side_ref, near_ref, *refs):
    blocks, out_ref, arrivals_ref = refs[:-2], refs[-2], refs[-1]
    count = len(blocks)
    parts, planes, width, lanes = out_ref.shape
    size = width // count
    whole = parts * planes * width
    for s, block in enumerate(blocks):
        start = pl.multiple_of(lax.rem(column_ref[0] + count - s, count) * size, size)
        rows = pl.ds(start, size)
        for component in range(parts):
            for plane in range(planes):
                first = (component * planes + plane) * size
                value = along_x_ref[component, plane, rows, :] + block[first:first + size]
                if gathered:
                    row = pl.multiple_of((component * planes + plane) * width + start, size)
                    value += near_ref[pl.ds(row, size)]
                out_ref[component, plane, rows, :] = value
    even = lax.rem(row_ref[0], 2) == 0
    for group in range(MIG // LANES):
        columns = slice(group * LANES, (group + 1) * LANES)
        if gathered:
            near = near_ref[whole + group * 8:whole + group * 8 + 6]
        else:
            near = near_ref[group, :6]
        far = far_ref[group, :6]
        arrivals_ref[:, 0, columns] = jnp.where(even, far, near)
        arrivals_ref[:, 1, columns] = jnp.where(even, near, far)
        for direction in (2, 3):
            arrivals_ref[:, direction, columns] = side_ref[direction - 2, group, :6]


def total(gathered, row, column, along_x_part, far, side, near, blocks):
    size = along_x_part.size
    return pl.pallas_call(
        functools.partial(total_kernel, gathered),
        out_shape=(any_space(along_x_part.shape), any_space((6, 4, MIG))),
        in_specs=[SMEM] * 2 + [VMEM] * (4 + len(blocks)),
        out_specs=(VMEM, VMEM),
        compiler_params=params(32),
        cost_estimate=CHEAP,
        name="total",
    )(row, column, along_x_part, far, side, near, *blocks)


def exchange(blocks):
    count = lax.axis_size("col")
    received = list(blocks)
    for s in sorted(range(1, count), key=lambda s: -min(s, count - s)):
        received[s] = lax.ppermute(blocks[s], "col", [(i, (i + s) % count) for i in range(count)])
    return received


def on_device(fields, diffusivity, records, response_time, cell_index, counts, destination, slot):
    rows, columns = lax.axis_size("row"), lax.axis_size("col")
    row, column = lax.axis_index("row"), lax.axis_index("col")
    width = fields.shape[2] // columns
    cell = cell_index.reshape(1, -1)
    blocks = [
        lax.dynamic_slice_in_dim(fields, (column + s) % columns * width, width, axis=2) for s in range(columns)
    ]
    row, column = row.reshape(1), column.reshape(1)
    gathered = rows & (rows - 1) == 0 and rows * fields.size * 4 <= 16 * MIB
    if gathered:
        mate = same_core(fields, 1)
        mate, blocks = lax.optimization_barrier((mate, blocks))
    lines = exchange(blocks)
    others = [same_core(fields, s) for s in range(2, rows - 2, 2)] if gathered else []
    kept, force, near, far, side = advance(
        row, counts.reshape(1, 1), fields, records, response_time.reshape(1, -1), cell, destination.reshape(1, -1),
        slot.reshape(1, -1))
    side, lines, others, later = lax.optimization_barrier((side, lines, others, fields))
    pairs = [(i, i + 1) for i in range(1, rows - 1, 2)]
    far = lax.ppermute(far, "row", pairs + [(b, a) for a, b in pairs])
    if gathered:
        others.append(same_core(later, rows - 2))
    terms_z = exchange(along_z(diffusivity, side, lines))
    terms_x, *near_y = along_xy(diffusivity, fields, cell, force, (row, near, mate, others) if gathered else ())
    if gathered:
        near = same_core(near_y[0], 1)
    else:
        terms_x = terms_x + pencil_along_y(diffusivity, fields)
        near = lax.ppermute(near, "row", [(i, i ^ 1) for i in range(rows) if i ^ 1 < rows])
    tendency, arrivals = total(gathered, row, column, terms_x, far, side_particles(terms_z), near, terms_z)
    return (tendency, kept, arrivals.transpose(1, 0, 2))


def solution(mesh):
    return jax.shard_map(
        on_device,
        mesh=mesh,
        in_specs=(
            P(None, "row", None, "col"),
            P(),
            P(None, ("row", "col")),
            P(("row", "col")),
            P(("row", "col")),
            P(("row", "col")),
            P(("row", "col")),
            P(("row", "col")),
        ),
        out_specs=(
            P(None, "row", None, "col"),
            P(None, ("row", "col")),
            P(None, None, ("row", "col")),
        ),
        check_vma=False,
    )
```

time: 32.5 us -> 31 us (0.954)
  starting transfers between devices: 13.9 us -> 16.5 us
  waiting for transfers between devices: 5.3 us -> 2.98 us
  Pallas kernels: 10.6 us -> 8.76 us
    ppermute x6, waiting for transfers between devices: 3.17 us -> 0.02 us  [exchange(): lax.ppermute(blocks[s], 'col', [(i, (i + s) % count) for i in range(count)])]
    ppermute x4 -> x6, starting transfers between devices: 5.14 us -> 7.01 us  [the longest x5 6.22 us: same_core(): lax.ppermute(block, 'row', [(i, i ^ s) for i in range(lax.axis_size('row'...]
    ppermute x4 -> x6, waiting for transfers between devices: 2.12 us -> 2.96 us  [the longest x5 2.96 us: same_core(): lax.ppermute(block, 'row', [(i, i ^ s) for i in range(lax.axis_size('row'...]
    pallas_call x1, Pallas kernels: 4.41 us -> 3.66 us  [advance(): pl.pallas_call(functools.partial(advance_kernel, chunk_of(particles, rows...]
    ppermute x6, starting transfers between devices: 8.72 us -> 9.45 us  [exchange(): lax.ppermute(blocks[s], 'col', [(i, (i + s) % count) for i in range(count)])]
    pallas_call x1, Pallas kernels: 1.37 us -> 0.76 us  [total(): pl.pallas_call(functools.partial(total_kernel, gathered), out_shape=(any_...]
    pallas_call x2, Pallas kernels: 3.7 us -> 3.23 us  [the longest x1 3.23 us: along_xy(): pl.pallas_call(functools.partial(along_xy_kernel, chunk_of(particles, 2 *...]
  transfers between devices with their start and end apart: 10 -> 12, of which waited for: 3 -> 2; matrix products, arithmetic and copies ran while one was open for 3% -> 3% of each run, Pallas kernels for 25% -> 26%
where the time goes in v3:
time: 31 us; the launch traced here: 30.8 us
  starting transfers between devices  16.5 us (53%)
  Pallas kernels  8.76 us (28%)
  waiting for transfers between devices  2.98 us (10%)
  between operations  1.47 us (5%)
  local copies, waits for them, and re-layouts  1.13 us (4%)
    ppermute x6, starting transfers between devices, exchange(): lax.ppermute(blocks[s], 'col', [(i, (i + s) % count) for i in range(count)])  9.45 us
    ppermute x5, starting transfers between devices, same_core(): lax.ppermute(block, 'row', [(i, i ^ s) for i in range(lax.axis_size('row'...  6.22 us
    pallas_call x1, Pallas kernels, advance(): pl.pallas_call(functools.partial(advance_kernel, chunk_of(particles, rows...  3.66 us
    pallas_call x1, Pallas kernels, along_xy(): pl.pallas_call(functools.partial(along_xy_kernel, chunk_of(particles, 2 *...  3.23 us
    ppermute x5, waiting for transfers between devices, same_core(): lax.ppermute(block, 'row', [(i, i ^ s) for i in range(lax.axis_size('row'...  2.96 us
    pallas_call x1, Pallas kernels, along_z(): pl.pallas_call(along_z_kernel, out_shape=tuple((any_space((size // lanes...  1.12 us
    dynamic_slice x1, local copies, waits for them, and re-layouts, on_device(): lax.dynamic_slice_in_dim(fields, (column + s) % columns * width, width, a...  1.03 us
    ppermute x1, starting transfers between devices, on_device(): far = lax.ppermute(far, 'row', pairs + [(b, a) for a, b in pairs])  0.78 us
  transfers between devices with their start and end apart: 12, of which 2 were waited for; matrix products, arithmetic and copies ran while one was open for 3% of the time, Pallas kernels for 26%

profile of v3, /device:TPU:0, one launch (start us, length us, event | category | flops | bytes accessed | tf_op | source)
XLA Modules:
  0.0 30.8 jit_solution(14684230721368387978)
XLA Ops:
  0.6 0.5 %collective-permute-start = (f32[4,2,64,128]{3,2,1,0:T(8,128)}, f32[4,2,64,128]{3,2,1,0:T(8,128)S(1)}, u32[]{:S(2)}, u32[]{:S(2)}) collective-permute-start(f32[4,2,64,128]{3,2,1,0:T(8,128)} %fields_ref.3), channel_id=1, source_target_pairs={{0,4},{4,0},{8,12},{12,8},{16,20},{20,16},{24,28},{28,24},{1,5},{5... | collective-permute-start | bytes 786440 | tf_op jit(solution)/shard_map/ppermute | solution.py:286
  1.1 2.6 %collective-permute-start.5 = (f32[4,2,64,128]{3,2,1,0:T(8,128)}, f32[4,2,64,128]{3,2,1,0:T(8,128)S(1)}, u32[]{:S(2)}, u32[]{:S(2)}) collective-permute-start(f32[4,2,64,128]{3,2,1,0:T(8,128)} %fields_ref.3), channel_id=1, source_target_pairs={{0,16},{4,20},{8,24},{12,28},{16,0},{20,4},{24,8},{28,12},{1,17},{... | collective-permute-start | bytes 786440 | tf_op jit(solution)/shard_map/ppermute | solution.py:286
  3.7 1.5 %collective-permute-start.4 = (f32[4,2,64,128]{3,2,1,0:T(8,128)}, f32[4,2,64,128]{3,2,1,0:T(8,128)S(1)}, u32[]{:S(2)}, u32[]{:S(2)}) collective-permute-start(f32[4,2,64,128]{3,2,1,0:T(8,128)} %fields_ref.3), channel_id=1, source_target_pairs={{0,8},{4,12},{8,0},{12,4},{16,24},{20,28},{24,16},{28,20},{1,9},{5... | collective-permute-start | bytes 786440 | tf_op jit(solution)/shard_map/ppermute | solution.py:286
  5.2 0.0 copy-start.8
  5.2 0.0 copy-start.7
  5.2 0.0 copy-start.6
  5.2 0.0 copy-start.4
  5.2 0.0 copy-start
  5.3 0.0 copy-start.1
  5.3 1.0 %constant_dynamic-slice_fusion = (f32[4,2,16,128]{3,2,1,0:T(8,128)S(1)}, f32[4,2,16,128]{3,2,1,0:T(8,128)S(1)}, f32[4,2,16,128]{3,2,1,0:T(8,128)S(1)}, f32[4,2,16,128]{3,2,1,0:T(8,128)S(1)}) fusion(f32[4,2,64,128]{3,2,1,0:T(8,128)} %fields_ref.3, s32[]{:T(128)S(6)} %select_n.38, s32[]{:T(128)S(6)} %select_n.36, s32[]{:T(128)S(6)} %select_n.34, s32[]{:T(128)S(6)} %select_n.32), kind=kLoop, calls=%fused_computation | loop fusion | bytes 524304 | tf_op jit(solution)/shard_map/dynamic_slice | solution.py:475
  6.3 0.0 collective-permute-done.refs_3_
  6.3 1.6 %collective-permute-start.1 = (f32[4,2,16,128]{3,2,1,0:T(8,128)S(1)}, f32[4,2,16,128]{3,2,1,0:T(8,128)S(1)}, u32[]{:S(2)}, u32[]{:S(2)}) collective-permute-start(f32[4,2,16,128]{3,2,1,0:T(8,128)S(1)} %get-tuple-element.34), channel_id=1, source_target_pairs={{0,1},{1,2},{2,3},{3,0},{4,5},{5,6},{6,7},{7,4},{8,9},{9,10},{10,1... | collective-permute-start | bytes 196616 | tf_op jit(solution)/shard_map/ppermute | solution.py:465
  7.9 2.6 %collective-permute-start.2 = (f32[4,2,16,128]{3,2,1,0:T(8,128)S(1)}, f32[4,2,16,128]{3,2,1,0:T(8,128)S(1)}, u32[]{:S(2)}, u32[]{:S(2)}) collective-permute-start(f32[4,2,16,128]{3,2,1,0:T(8,128)S(1)} %get-tuple-element.35), channel_id=1, source_target_pairs={{0,2},{1,3},{2,0},{3,1},{4,6},{5,7},{6,4},{7,5},{8,10},{9,11},{10,... | collective-permute-start | bytes 196616 | tf_op jit(solution)/shard_map/ppermute | solution.py:465
  10.5 1.3 %collective-permute-start.3 = (f32[4,2,16,128]{3,2,1,0:T(8,128)S(1)}, f32[4,2,16,128]{3,2,1,0:T(8,128)S(1)}, u32[]{:S(2)}, u32[]{:S(2)}) collective-permute-start(f32[4,2,16,128]{3,2,1,0:T(8,128)S(1)} %get-tuple-element.36), channel_id=1, source_target_pairs={{0,3},{1,0},{2,1},{3,2},{4,7},{5,4},{6,5},{7,6},{8,11},{9,8},{10,9... | collective-permute-start | bytes 196616 | tf_op jit(solution)/shard_map/ppermute | solution.py:465
  12.5 0.0 copy-done.8
  12.5 0.0 copy-done.7
  12.6 0.0 copy-done.6
  12.6 0.0 copy-done.4
  12.6 0.0 copy-done
  12.6 0.0 copy-done.1
  12.6 0.0 copy-start.2
  12.6 0.0 copy-start.3
  12.6 3.7 %advance.1 = (f32[6,8192]{1,0:T(8,128)}, f32[3,8192]{1,0:T(4,128)S(1)}, f32[2,8,128]{2,1,0:T(8,128)S(1)}, f32[2,8,128]{2,1,0:T(8,128)S(1)}, f32[2,2,8,128]{3,2,1,0:T(8,128)S(1)}) custom-call(s32[1]{0:T(128)} %bitcast.row_ref.refs_0_, s32[1,1]{1,0:T(1,128)} %bitcast.8.count_ref, f32[4,2,64,128]{3,2,1,0:T(8,128)S(1)} %copy-done, f32[6,8192]{1,0:T(8,128)S(1)} %copy-done.1, ...), custom_call_target="tpu_custom_call" | custom-call | flops 1 | bytes 1 | tf_op jit(solution)/shard_map/advance/pallas_call | solution.py:190
  16.3 0.0 copy-start.10
  16.3 0.0 collective-permute-done.5.refs_5_
  16.3 0.0 collective-permute-done.4.refs_4_
  16.3 0.0 collective-permute-done.1.refs_1_
  16.3 0.0 collective-permute-done.2.refs_2_
  16.3 0.0 collective-permute-done.3.refs_3_
  16.3 0.0 copy-start.5
  16.3 0.5 %collective-permute-start.6 = (f32[4,2,64,128]{3,2,1,0:T(8,128)S(1)}, f32[4,2,64,128]{3,2,1,0:T(8,128)S(1)}, u32[]{:S(2)}, u32[]{:S(2)}) collective-permute-start(f32[4,2,64,128]{3,2,1,0:T(8,128)S(1)} %copy-done), channel_id=1, source_target_pairs={{0,24},{4,28},{8,16},{12,20},{16,8},{20,12},{24,0},{28,4},{1,25},{... | collective-permute-start | bytes 786440 | tf_op jit(solution)/shard_map/ppermute | solution.py:286
  16.9 0.0 copy-done.2
  16.9 0.0 copy-done.3
  16.9 0.1 copy-done.10
  16.9 1.1 %along_z.1 = (f32[128,128]{1,0:T(8,128)S(1)}, f32[144,128]{1,0:T(8,128)S(1)}, f32[128,128]{1,0:T(8,128)S(1)}, f32[144,128]{1,0:T(8,128)S(1)}) custom-call(f32[4]{0:T(128)S(1)} %copy-done.10, bf16[512,256]{1,0:T(8,128)(2,1)S(1)} %copy-done.3, bf16[512,256]{1,0:T(8,128)(2,1)S(1)} %copy-done.2, f32[2,2,8,128]{3,2,1,0:T(8,128)S(1)} %get-tuple-element.42.side_ref, ...), custom_call_target="tpu_custom_call" | custom-call | flops 1 | bytes 1 | tf_op jit(solution)/shard_map/along_z/pallas_call | solution.py:373
  18.1 0.7 %collective-permute-start.8 = (f32[144,128]{1,0:T(8,128)S(1)}, f32[144,128]{1,0:T(8,128)S(1)}, u32[]{:S(2)}, u32[]{:S(2)}) collective-permute-start(f32[144,128]{1,0:T(8,128)S(1)} %get-tuple-element.48), channel_id=1, source_target_pairs={{0,1},{1,2},{2,3},{3,0},{4,5},{5,6},{6,7},{7,4},{8,9},{9,10},{10,1... | collective-permute-start | bytes 221192 | tf_op jit(solution)/shard_map/ppermute | solution.py:465
  18.8 3.2 %collective-permute-start.10 = (f32[144,128]{1,0:T(8,128)S(1)}, f32[144,128]{1,0:T(8,128)S(1)}, u32[]{:S(2)}, u32[]{:S(2)}) collective-permute-start(f32[144,128]{1,0:T(8,128)S(1)} %get-tuple-element.50), channel_id=1, source_target_pairs={{0,3},{1,0},{2,1},{3,2},{4,7},{5,4},{6,5},{7,6},{8,11},{9,8},{10,9... | collective-permute-start | bytes 221192 | tf_op jit(solution)/shard_map/ppermute | solution.py:465
  21.9 0.0 collective-permute-start.9
  21.9 0.0 copy-start.9
  21.9 0.8 %collective-permute-start.7 = (f32[2,8,128]{2,1,0:T(8,128)S(1)}, f32[2,8,128]{2,1,0:T(8,128)S(1)}, u32[]{:S(2)}, u32[]{:S(2)}) collective-permute-start(f32[2,8,128]{2,1,0:T(8,128)S(1)} %get-tuple-element.41), channel_id=1, source_target_pairs={{4,8},{12,16},{20,24},{8,4},{16,12},{24,20},{5,9},{13,17},{21,25},... | collective-permute-start | bytes 24584 | tf_op jit(solution)/shard_map/ppermute | solution.py:489
  22.7 1.8 %collective-permute-done.6.refs_6_ = f32[4,2,64,128]{3,2,1,0:T(8,128)S(1)} collective-permute-done((f32[4,2,64,128]{3,2,1,0:T(8,128)S(1)}, f32[4,2,64,128]{3,2,1,0:T(8,128)S(1)}, u32[]{:S(2)}, u32[]{:S(2)}) %collective-permute-start.6) | collective-permute-done | bytes 262176 | tf_op jit(solution)/shard_map/ppermute | solution.py:286
  24.5 0.0 copy-done.5
  24.5 0.0 copy-done.9
  24.5 3.2 %along_xy.1 = (f32[4,2,64,128]{3,2,1,0:T(8,128)S(1)}, f32[528,128]{1,0:T(8,128)S(1)}) custom-call(f32[4]{0:T(128)S(1)} %copy-done.10, f32[4,2,64,128]{3,2,1,0:T(8,128)S(1)} %copy-done, bf16[128,192]{1,0:T(8,128)(2,1)S(1)} %copy-done.5, s32[1,8192]{1,0:T(1,128)S(1)} %bitcast.10, f32[3,8192]{1,0:T(4,128)S(1)} %get-tuple-element.29.force_ref, ...), custom_call_target="tpu_custom_call" | custom-call | flops 1 | bytes 1 | tf_op jit(solution)/shard_map/along_xy/pallas_call | solution.py:315
  27.8 1.1 %collective-permute-start.11 = (f32[528,128]{1,0:T(8,128)S(1)}, f32[528,128]{1,0:T(8,128)S(1)}, u32[]{:S(2)}, u32[]{:S(2)}) collective-permute-start(f32[528,128]{1,0:T(8,128)S(1)} %get-tuple-element.51), channel_id=1, source_target_pairs={{0,4},{4,0},{8,12},{12,8},{16,20},{20,16},{24,28},{28,24},{1,5},{5... | collective-permute-start | bytes 811016 | tf_op jit(solution)/shard_map/ppermute | solution.py:286
  28.9 0.0 collective-permute-done.9.refs_2_
  28.9 0.0 collective-permute-done.8.refs_1_
  28.9 0.0 collective-permute-done.10.refs_3_
  28.9 0.0 collective-permute-done.7.far_ref
  28.9 1.1 %collective-permute-done.11.near_ref = f32[528,128]{1,0:T(8,128)S(1)} collective-permute-done((f32[528,128]{1,0:T(8,128)S(1)}, f32[528,128]{1,0:T(8,128)S(1)}, u32[]{:S(2)}, u32[]{:S(2)}) %collective-permute-start.11) | collective-permute-done | bytes 270368 | tf_op jit(solution)/shard_map/ppermute | solution.py:286
  30.0 0.8 %total.1 = (f32[4,2,64,128]{3,2,1,0:T(8,128)}, f32[6,4,256]{2,1,0:T(4,128)}) custom-call(s32[1]{0:T(128)} %bitcast.row_ref.refs_0_, s32[1]{0:T(128)} %bitcast.1.column_ref, f32[4,2,64,128]{3,2,1,0:T(8,128)S(1)} %get-tuple-element.40.along_x_ref, f32[2,8,128]{2,1,0:T(8,128)S(1)} %collective-permute-done.7.far_ref, ...), custom_call_target="tpu_custom_call" | custom-call | flops 1 | bytes 1 | tf_op jit(solution)/shard_map/total/pallas_call | solution.py:450
  (1 shorter events, 0.0 us)
Async XLA Ops:
  0.6 5.7 %collective-permute-start = (f32[4,2,64,128]{3,2,1,0:T(8,128)}, f32[4,2,64,128]{3,2,1,0:T(8,128)S(1)}, u32[]{:S(2)}, u32[]{:S(2)}) collective-permute-start(f32[4,2,64,128]{3,2,1,0:T(8,128)} %fields_ref.3), channel_id=1, source_target_pairs={{0,4},{4,0},{8,12},{12,8},{16,20},{20,16},{24,28},{28,24},{1,5},{5... | collective-permute-start | bytes 786440 | tf_op jit(solution)/shard_map/ppermute | solution.py:286
  1.1 15.1 %collective-permute-start.5 = (f32[4,2,64,128]{3,2,1,0:T(8,128)}, f32[4,2,64,128]{3,2,1,0:T(8,128)S(1)}, u32[]{:S(2)}, u32[]{:S(2)}) collective-permute-start(f32[4,2,64,128]{3,2,1,0:T(8,128)} %fields_ref.3), channel_id=1, source_target_pairs={{0,16},{4,20},{8,24},{12,28},{16,0},{20,4},{24,8},{28,12},{1,17},{... | collective-permute-start | bytes 786440 | tf_op jit(solution)/shard_map/ppermute | solution.py:286
  3.7 12.5 %collective-permute-start.4 = (f32[4,2,64,128]{3,2,1,0:T(8,128)}, f32[4,2,64,128]{3,2,1,0:T(8,128)S(1)}, u32[]{:S(2)}, u32[]{:S(2)}) collective-permute-start(f32[4,2,64,128]{3,2,1,0:T(8,128)} %fields_ref.3), channel_id=1, source_target_pairs={{0,8},{4,12},{8,0},{12,4},{16,24},{20,28},{24,16},{28,20},{1,9},{5... | collective-permute-start | bytes 786440 | tf_op jit(solution)/shard_map/ppermute | solution.py:286
  5.2 7.3 %copy-start.8 = (s32[8192]{0:T(1024)S(1)}, s32[8192]{0:T(1024)}, u32[]{:S(2)}) copy-start(s32[8192]{0:T(1024)} %param.19) | copy-start | bytes 98308
  5.2 7.3 %copy-start.7 = (s32[8192]{0:T(1024)S(1)}, s32[8192]{0:T(1024)}, u32[]{:S(2)}) copy-start(s32[8192]{0:T(1024)} %param.18) | copy-start | bytes 98308
  5.2 7.3 %copy-start.6 = (f32[8192]{0:T(1024)S(1)}, f32[8192]{0:T(1024)}, u32[]{:S(2)}) copy-start(f32[8192]{0:T(1024)} %param.15) | copy-start | bytes 98308
  5.2 7.3 %copy-start.4 = (s32[8192]{0:T(1024)S(1)}, s32[8192]{0:T(1024)}, u32[]{:S(2)}) copy-start(s32[8192]{0:T(1024)} %param.16) | copy-start | bytes 98308
  5.2 7.3 %copy-start = (f32[4,2,64,128]{3,2,1,0:T(8,128)S(1)}, f32[4,2,64,128]{3,2,1,0:T(8,128)}, u32[]{:S(2)}) copy-start(f32[4,2,64,128]{3,2,1,0:T(8,128)} %fields_ref.3) | copy-start | bytes 786436
  5.3 7.3 %copy-start.1 = (f32[6,8192]{1,0:T(8,128)S(1)}, f32[6,8192]{1,0:T(8,128)}, u32[]{:S(2)}) copy-start(f32[6,8192]{1,0:T(8,128)} %records_ref.1) | copy-start | bytes 589828
  6.3 10.0 %collective-permute-start.1 = (f32[4,2,16,128]{3,2,1,0:T(8,128)S(1)}, f32[4,2,16,128]{3,2,1,0:T(8,128)S(1)}, u32[]{:S(2)}, u32[]{:S(2)}) collective-permute-start(f32[4,2,16,128]{3,2,1,0:T(8,128)S(1)} %get-tuple-element.34), channel_id=1, source_target_pairs={{0,1},{1,2},{2,3},{3,0},{4,5},{5,6},{6,7},{7,4},{8,9},{9,10},{10,1... | collective-permute-start | bytes 196616 | tf_op jit(solution)/shard_map/ppermute | solution.py:465
  7.9 8.4 %collective-permute-start.2 = (f32[4,2,16,128]{3,2,1,0:T(8,128)S(1)}, f32[4,2,16,128]{3,2,1,0:T(8,128)S(1)}, u32[]{:S(2)}, u32[]{:S(2)}) collective-permute-start(f32[4,2,16,128]{3,2,1,0:T(8,128)S(1)} %get-tuple-element.35), channel_id=1, source_target_pairs={{0,2},{1,3},{2,0},{3,1},{4,6},{5,7},{6,4},{7,5},{8,10},{9,11},{10,... | collective-permute-start | bytes 196616 | tf_op jit(solution)/shard_map/ppermute | solution.py:465
  10.5 5.8 %collective-permute-start.3 = (f32[4,2,16,128]{3,2,1,0:T(8,128)S(1)}, f32[4,2,16,128]{3,2,1,0:T(8,128)S(1)}, u32[]{:S(2)}, u32[]{:S(2)}) collective-permute-start(f32[4,2,16,128]{3,2,1,0:T(8,128)S(1)} %get-tuple-element.36), channel_id=1, source_target_pairs={{0,3},{1,0},{2,1},{3,2},{4,7},{5,4},{6,5},{7,6},{8,11},{9,8},{10,9... | collective-permute-start | bytes 196616 | tf_op jit(solution)/shard_map/ppermute | solution.py:465
  12.6 4.3 %copy-start.2 = (bf16[512,256]{1,0:T(8,128)(2,1)S(1)}, bf16[512,256]{1,0:T(8,128)(2,1)}, u32[]{:S(2)}) copy-start(bf16[512,256]{1,0:T(8,128)(2,1)} %constant.53.clone.low_ref) | copy-start | bytes 786436
  12.6 4.3 %copy-start.3 = (bf16[512,256]{1,0:T(8,128)(2,1)S(1)}, bf16[512,256]{1,0:T(8,128)(2,1)}, u32[]{:S(2)}) copy-start(bf16[512,256]{1,0:T(8,128)(2,1)} %constant.52.clone.high_ref) | copy-start | bytes 786436
  16.3 0.7 %copy-start.10 = (f32[4]{0:T(128)S(1)}, f32[4]{0:T(128)}, u32[]{:S(2)}) copy-start(f32[4]{0:T(128)} %viscous_ref.3) | copy-start | bytes 52
  16.3 8.2 %copy-start.5 = (bf16[128,192]{1,0:T(8,128)(2,1)S(1)}, bf16[128,192]{1,0:T(8,128)(2,1)}, u32[]{:S(2)}) copy-start(bf16[128,192]{1,0:T(8,128)(2,1)} %constant.54.clone.operator_ref) | copy-start | bytes 147460
  16.3 8.2 %collective-permute-start.6 = (f32[4,2,64,128]{3,2,1,0:T(8,128)S(1)}, f32[4,2,64,128]{3,2,1,0:T(8,128)S(1)}, u32[]{:S(2)}, u32[]{:S(2)}) collective-permute-start(f32[4,2,64,128]{3,2,1,0:T(8,128)S(1)} %copy-done), channel_id=1, source_target_pairs={{0,24},{4,28},{8,16},{12,20},{16,8},{20,12},{24,0},{28,4},{1,25},{... | collective-permute-start | bytes 786440 | tf_op jit(solution)/shard_map/ppermute | solution.py:286
  18.1 10.8 %collective-permute-start.8 = (f32[144,128]{1,0:T(8,128)S(1)}, f32[144,128]{1,0:T(8,128)S(1)}, u32[]{:S(2)}, u32[]{:S(2)}) collective-permute-start(f32[144,128]{1,0:T(8,128)S(1)} %get-tuple-element.48), channel_id=1, source_target_pairs={{0,1},{1,2},{2,3},{3,0},{4,5},{5,6},{6,7},{7,4},{8,9},{9,10},{10,1... | collective-permute-start | bytes 221192 | tf_op jit(solution)/shard_map/ppermute | solution.py:465
  18.8 10.1 %collective-permute-start.10 = (f32[144,128]{1,0:T(8,128)S(1)}, f32[144,128]{1,0:T(8,128)S(1)}, u32[]{:S(2)}, u32[]{:S(2)}) collective-permute-start(f32[144,128]{1,0:T(8,128)S(1)} %get-tuple-element.50), channel_id=1, source_target_pairs={{0,3},{1,0},{2,1},{3,2},{4,7},{5,4},{6,5},{7,6},{8,11},{9,8},{10,9... | collective-permute-start | bytes 221192 | tf_op jit(solution)/shard_map/ppermute | solution.py:465
  21.9 6.9 %collective-permute-start.9 = (f32[128,128]{1,0:T(8,128)S(1)}, f32[128,128]{1,0:T(8,128)S(1)}, u32[]{:S(2)}, u32[]{:S(2)}) collective-permute-start(f32[128,128]{1,0:T(8,128)S(1)} %get-tuple-element.49), channel_id=1, source_target_pairs={{0,2},{1,3},{2,0},{3,1},{4,6},{5,7},{6,4},{7,5},{8,10},{9,11},{10,... | collective-permute-start | bytes 196616 | tf_op jit(solution)/shard_map/ppermute | solution.py:465
  21.9 2.6 %copy-start.9 = (f32[512]{0:T(512)S(1)}, f32[512]{0:T(512)}, u32[]{:S(2)}) copy-start(f32[512]{0:T(512)} %constant.55.clone.refs_1_) | copy-start | bytes 6148
  21.9 7.0 %collective-permute-start.7 = (f32[2,8,128]{2,1,0:T(8,128)S(1)}, f32[2,8,128]{2,1,0:T(8,128)S(1)}, u32[]{:S(2)}, u32[]{:S(2)}) collective-permute-start(f32[2,8,128]{2,1,0:T(8,128)S(1)} %get-tuple-element.41), channel_id=1, source_target_pairs={{4,8},{12,16},{20,24},{8,4},{16,12},{24,20},{5,9},{13,17},{21,25},... | collective-permute-start | bytes 24584 | tf_op jit(solution)/shard_map/ppermute | solution.py:489
  27.8 2.3 %collective-permute-start.11 = (f32[528,128]{1,0:T(8,128)S(1)}, f32[528,128]{1,0:T(8,128)S(1)}, u32[]{:S(2)}, u32[]{:S(2)}) collective-permute-start(f32[528,128]{1,0:T(8,128)S(1)} %get-tuple-element.51), channel_id=1, source_target_pairs={{0,4},{4,0},{8,12},{12,8},{16,20},{20,16},{24,28},{28,24},{1,5},{5... | collective-permute-start | bytes 811016 | tf_op jit(solution)/shard_map/ppermute | solution.py:286

commit v4 on v3

--- a/solution.py
+++ b/solution.py
@@ -256,16 +256,16 @@
     if not y_refs:
         return
     row_ref, weight_ref, near_ref, mate_ref, *others = y_refs
-    count = 2 * (len(others) + 1)
+    both_ref, diagonal_ref = others
+    blocks = [fields_ref, diagonal_ref, both_ref.at[0], both_ref.at[1]]
     size = parts * planes * width
-    mine = row_ref[0] * (count * planes * planes * 2)
+    mine = row_ref[0] * (len(blocks) * planes * 2 * planes * 2)
     step = min(width, 32)
     for component in range(parts):
         for first in range(0, width, step):
             inside = slice(first, first + step)
             sums = [[None] * 2 for _ in range(2 * planes)]
-            for index in range(count // 2):
-                block = others[index - 1] if index else fields_ref
+            for index, block in enumerate(blocks):
                 for source in range(planes):
                     value = block[component, source, inside]
                     for target in range(2 * planes):
@@ -286,14 +286,18 @@
     return lax.ppermute(block, "row", [(i, i ^ s) for i in range(lax.axis_size("row"))])
 
 
+def neighbour(row):
+    return row ^ 4 if row % 2 else row ^ 2
+
+
 def along_y_weights(rows, planes):
     deriv = wall_compact(rows * planes)
     operators = np.stack([deriv, deriv @ deriv], axis=-1)
-    table = np.zeros((rows, rows // 2, planes, 2, planes, 2), np.float32)
+    table = np.zeros((rows, 4, planes, 2, planes, 2), np.float32)
     for me in range(rows):
-        for index in range(rows // 2):
+        for index, other in enumerate((me, me ^ 6, neighbour(me), neighbour(me) ^ 1)):
             for side in range(2):
-                target, source = (me ^ side) * planes, (me ^ (2 * index)) * planes
+                target, source = (me ^ side) * planes, other * planes
                 block = operators[target:target + planes, source:source + planes]
                 table[me, index, :, side] = block.transpose(1, 0, 2)
     return jnp.asarray(table.reshape(-1))
@@ -319,7 +323,7 @@
         out_specs=(VMEM,) * len(outs),
         scratch_shapes=[pltpu.VMEM((6 * half, 2 * lanes), jnp.float32)],
         compiler_params=params(40),
-        cost_estimate=CHEAP,
+        cost_estimate=LONG,
         name="along_xy",
     )(viscous, fields, operator, cell, force, *y_part)
 
@@ -475,20 +479,23 @@
         lax.dynamic_slice_in_dim(fields, (column + s) % columns * width, width, axis=2) for s in range(columns)
     ]
     row, column = row.reshape(1), column.reshape(1)
-    gathered = rows & (rows - 1) == 0 and rows * fields.size * 4 <= 16 * MIB
+    gathered = rows == 8 and rows * fields.size * 4 <= 16 * MIB
     if gathered:
         mate = same_core(fields, 1)
         mate, blocks = lax.optimization_barrier((mate, blocks))
     lines = exchange(blocks)
-    others = [same_core(fields, s) for s in range(2, rows - 2, 2)] if gathered else []
+    others = []
+    if gathered:
+        both = jnp.stack([fields, mate])
+        later, both = lax.optimization_barrier((fields, both))
+        both = lax.ppermute(both, "row", [(i, neighbour(i)) for i in range(rows)])
+        others = [both, same_core(later, 6)]
     kept, force, near, far, side = advance(
         row, counts.reshape(1, 1), fields, records, response_time.reshape(1, -1), cell, destination.reshape(1, -1),
         slot.reshape(1, -1))
-    side, lines, others, later = lax.optimization_barrier((side, lines, others, fields))
+    side, lines = lax.optimization_barrier((side, lines))
     pairs = [(i, i + 1) for i in range(1, rows - 1, 2)]
     far = lax.ppermute(far, "row", pairs + [(b, a) for a, b in pairs])
-    if gathered:
-        others.append(same_core(later, rows - 2))
     terms_z = exchange(along_z(diffusivity, side, lines))
     terms_x, *near_y = along_xy(diffusivity, fields, cell, force, (row, near, mate, others) if gathered else ())
     if gathered:

time: 31 us -> 30.6 us (0.987)
  waiting for transfers between devices: 2.98 us -> 1.53 us
  starting transfers between devices: 16.5 us -> 17.5 us
    ppermute x0 -> x1, starting transfers between devices: none -> 2.93 us  [on_device(): both = lax.ppermute(both, 'row', [(i, neighbour(i)) for i in range(rows)])]
    ppermute x5 -> x3, starting transfers between devices: 6.22 us -> 3.82 us  [same_core(): lax.ppermute(block, 'row', [(i, i ^ s) for i in range(lax.axis_size('row'...]
    ppermute x5 -> x3, waiting for transfers between devices: 2.96 us -> 1.51 us  [same_core(): lax.ppermute(block, 'row', [(i, i ^ s) for i in range(lax.axis_size('row'...]
    ppermute x6, starting transfers between devices: 9.45 us -> 10 us  [exchange(): lax.ppermute(blocks[s], 'col', [(i, (i + s) % count) for i in range(count)])]
  transfers between devices with their start and end apart: 12 -> 11, of which waited for: 2 -> 2; matrix products, arithmetic and copies ran while one was open for 3% -> 3% of each run, Pallas kernels for 26% -> 26%
where the time goes in v4:
time: 30.6 us; the launch traced here: 30.4 us
  starting transfers between devices  17.5 us (57%)
  Pallas kernels  8.75 us (29%)
  waiting for transfers between devices  1.53 us (5%)
  between operations  1.47 us (5%)
  local copies, waits for them, and re-layouts  1.05 us (3%)
    ppermute x6, starting transfers between devices, exchange(): lax.ppermute(blocks[s], 'col', [(i, (i + s) % count) for i in range(count)])  10 us
    ppermute x3, starting transfers between devices, same_core(): lax.ppermute(block, 'row', [(i, i ^ s) for i in range(lax.axis_size('row'...  3.82 us
    pallas_call x1, Pallas kernels, advance(): pl.pallas_call(functools.partial(advance_kernel, chunk_of(particles, rows...  3.64 us
    pallas_call x1, Pallas kernels, along_xy(): pl.pallas_call(functools.partial(along_xy_kernel, chunk_of(particles, 2 *...  3.23 us
    ppermute x1, starting transfers between devices, on_device(): both = lax.ppermute(both, 'row', [(i, neighbour(i)) for i in range(rows)])  2.93 us
    ppermute x3, waiting for transfers between devices, same_core(): lax.ppermute(block, 'row', [(i, i ^ s) for i in range(lax.axis_size('row'...  1.51 us
    pallas_call x1, Pallas kernels, along_z(): pl.pallas_call(along_z_kernel, out_shape=tuple((any_space((size // lanes...  1.12 us
    dynamic_slice x1, local copies, waits for them, and re-layouts, on_device(): lax.dynamic_slice_in_dim(fields, (column + s) % columns * width, width, a...  1 us
  transfers between devices with their start and end apart: 11, of which 2 were waited for; matrix products, arithmetic and copies ran while one was open for 3% of the time, Pallas kernels for 26%

profile of v4, /device:TPU:0, one launch (start us, length us, event | category | flops | bytes accessed | tf_op | source)
XLA Modules:
  0.0 30.4 jit_solution(6738455532058455470)
XLA Ops:
  0.6 0.5 %collective-permute-start = (f32[4,2,64,128]{3,2,1,0:T(8,128)}, f32[4,2,64,128]{3,2,1,0:T(8,128)S(1)}, u32[]{:S(2)}, u32[]{:S(2)}) collective-permute-start(f32[4,2,64,128]{3,2,1,0:T(8,128)} %fields_ref.3), channel_id=1, source_target_pairs={{0,4},{4,0},{8,12},{12,8},{16,20},{20,16},{24,28},{28,24},{1,5},{5... | collective-permute-start | bytes 786440 | tf_op jit(solution)/shard_map/ppermute | solution.py:286
  1.1 0.0 copy-start
  1.1 1.0 %constant_dynamic-slice_fusion = (f32[4,2,16,128]{3,2,1,0:T(8,128)S(1)}, f32[4,2,16,128]{3,2,1,0:T(8,128)S(1)}, f32[4,2,16,128]{3,2,1,0:T(8,128)S(1)}, f32[4,2,16,128]{3,2,1,0:T(8,128)S(1)}) fusion(f32[4,2,64,128]{3,2,1,0:T(8,128)} %fields_ref.3, s32[]{:T(128)S(6)} %select_n.38, s32[]{:T(128)S(6)} %select_n.36, s32[]{:T(128)S(6)} %select_n.34, s32[]{:T(128)S(6)} %select_n.32), kind=kLoop, calls=%fused_computation.1 | loop fusion | bytes 524304 | tf_op jit(solution)/shard_map/dynamic_slice | solution.py:479
  2.2 0.4 %collective-permute-done.refs_3_ = f32[4,2,64,128]{3,2,1,0:T(8,128)S(1)} collective-permute-done((f32[4,2,64,128]{3,2,1,0:T(8,128)}, f32[4,2,64,128]{3,2,1,0:T(8,128)S(1)}, u32[]{:S(2)}, u32[]{:S(2)}) %collective-permute-start) | collective-permute-done | bytes 262176 | tf_op jit(solution)/shard_map/ppermute | solution.py:286
  2.5 0.0 copy-done
  2.5 0.0 copy-start.1
  2.5 0.0 copy-start.4
  2.5 0.0 copy-start.5
  2.5 0.0 copy-start.6
  2.5 0.0 copy-start.7
  2.6 2.9 %collective-permute-start.1 = (f32[2,4,2,64,128]{4,3,2,1,0:T(8,128)S(1)}, f32[2,4,2,64,128]{4,3,2,1,0:T(8,128)S(1)}, u32[]{:S(2)}, u32[]{:S(2)}) collective-permute-start(f32[2,4,2,64,128]{4,3,2,1,0:T(8,128)S(1)} %pad_maximum_fusion), channel_id=1, source_target_pairs={{0,8},{4,20},{8,0},{12,28},{16,24},{20,4},{24,16},{28,12},{1,9},{5... | collective-permute-start | bytes 1572872 | tf_op jit(solution)/shard_map/ppermute | solution.py:491
  5.5 1.5 %collective-permute-start.2 = (f32[4,2,64,128]{3,2,1,0:T(8,128)S(1)}, f32[4,2,64,128]{3,2,1,0:T(8,128)S(1)}, u32[]{:S(2)}, u32[]{:S(2)}) collective-permute-start(f32[4,2,64,128]{3,2,1,0:T(8,128)S(1)} %copy-done), channel_id=1, source_target_pairs={{0,24},{4,28},{8,16},{12,20},{16,8},{20,12},{24,0},{28,4},{1,25},{... | collective-permute-start | bytes 786440 | tf_op jit(solution)/shard_map/ppermute | solution.py:286
  7.0 1.6 %collective-permute-start.4 = (f32[4,2,16,128]{3,2,1,0:T(8,128)S(1)}, f32[4,2,16,128]{3,2,1,0:T(8,128)S(1)}, u32[]{:S(2)}, u32[]{:S(2)}) collective-permute-start(f32[4,2,16,128]{3,2,1,0:T(8,128)S(1)} %get-tuple-element.37), channel_id=1, source_target_pairs={{0,1},{1,2},{2,3},{3,0},{4,5},{5,6},{6,7},{7,4},{8,9},{9,10},{10,1... | collective-permute-start | bytes 196616 | tf_op jit(solution)/shard_map/ppermute | solution.py:469
  8.6 2.6 %collective-permute-start.5 = (f32[4,2,16,128]{3,2,1,0:T(8,128)S(1)}, f32[4,2,16,128]{3,2,1,0:T(8,128)S(1)}, u32[]{:S(2)}, u32[]{:S(2)}) collective-permute-start(f32[4,2,16,128]{3,2,1,0:T(8,128)S(1)} %get-tuple-element.38), channel_id=1, source_target_pairs={{0,2},{1,3},{2,0},{3,1},{4,6},{5,7},{6,4},{7,5},{8,10},{9,11},{10,... | collective-permute-start | bytes 196616 | tf_op jit(solution)/shard_map/ppermute | solution.py:469
  11.2 1.3 %collective-permute-start.6 = (f32[4,2,16,128]{3,2,1,0:T(8,128)S(1)}, f32[4,2,16,128]{3,2,1,0:T(8,128)S(1)}, u32[]{:S(2)}, u32[]{:S(2)}) collective-permute-start(f32[4,2,16,128]{3,2,1,0:T(8,128)S(1)} %get-tuple-element.39), channel_id=1, source_target_pairs={{0,3},{1,0},{2,1},{3,2},{4,7},{5,4},{6,5},{7,6},{8,11},{9,8},{10,9... | collective-permute-start | bytes 196616 | tf_op jit(solution)/shard_map/ppermute | solution.py:469
  13.2 0.0 copy-done.1
  13.2 0.0 copy-done.4
  13.2 0.0 copy-done.5
  13.2 0.0 copy-done.6
  13.2 0.0 copy-done.7
  13.2 0.0 copy-start.2
  13.3 0.0 copy-start.3
  13.3 3.6 %advance.1 = (f32[6,8192]{1,0:T(8,128)}, f32[3,8192]{1,0:T(4,128)S(1)}, f32[2,8,128]{2,1,0:T(8,128)S(1)}, f32[2,8,128]{2,1,0:T(8,128)S(1)}, f32[2,2,8,128]{3,2,1,0:T(8,128)S(1)}) custom-call(s32[1]{0:T(128)} %bitcast.row_ref.refs_0_, s32[1,1]{1,0:T(1,128)} %bitcast.10.count_ref, f32[4,2,64,128]{3,2,1,0:T(8,128)S(1)} %copy-done, f32[6,8192]{1,0:T(8,128)S(1)} %copy-done.1, ...), custom_call_target="tpu_custom_call" | custom-call | flops 1 | bytes 1 | tf_op jit(solution)/shard_map/advance/pallas_call | solution.py:190
  16.9 0.0 collective-permute-done.4.refs_1_
  16.9 0.0 copy-start.8
  16.9 0.8 %collective-permute-start.3 = (f32[2,8,128]{2,1,0:T(8,128)S(1)}, f32[2,8,128]{2,1,0:T(8,128)S(1)}, u32[]{:S(2)}, u32[]{:S(2)}) collective-permute-start(f32[2,8,128]{2,1,0:T(8,128)S(1)} %get-tuple-element.34), channel_id=1, source_target_pairs={{4,8},{12,16},{20,24},{8,4},{16,12},{24,20},{5,9},{13,17},{21,25},... | collective-permute-start | bytes 24584 | tf_op jit(solution)/shard_map/ppermute | solution.py:498
  17.7 0.0 collective-permute-done.5.refs_2_
  17.7 0.0 collective-permute-done.6.refs_3_
  17.7 0.0 copy-done.2
  17.7 0.0 copy-done.3
  17.7 0.0 copy-done.8
  17.8 0.0 copy-start.9
  17.8 1.1 %along_z.1 = (f32[128,128]{1,0:T(8,128)S(1)}, f32[144,128]{1,0:T(8,128)S(1)}, f32[128,128]{1,0:T(8,128)S(1)}, f32[144,128]{1,0:T(8,128)S(1)}) custom-call(f32[4]{0:T(128)S(1)} %copy-done.8, bf16[512,256]{1,0:T(8,128)(2,1)S(1)} %copy-done.2, bf16[512,256]{1,0:T(8,128)(2,1)S(1)} %copy-done.3, f32[2,2,8,128]{3,2,1,0:T(8,128)S(1)} %get-tuple-element.40.side_ref, ...), custom_call_target="tpu_custom_call" | custom-call | flops 1 | bytes 1 | tf_op jit(solution)/shard_map/along_z/pallas_call | solution.py:377
  18.9 0.7 %collective-permute-start.7 = (f32[144,128]{1,0:T(8,128)S(1)}, f32[144,128]{1,0:T(8,128)S(1)}, u32[]{:S(2)}, u32[]{:S(2)}) collective-permute-start(f32[144,128]{1,0:T(8,128)S(1)} %get-tuple-element.46), channel_id=1, source_target_pairs={{0,1},{1,2},{2,3},{3,0},{4,5},{5,6},{6,7},{7,4},{8,9},{9,10},{10,1... | collective-permute-start | bytes 221192 | tf_op jit(solution)/shard_map/ppermute | solution.py:469
  19.6 0.7 %collective-permute-start.8 = (f32[128,128]{1,0:T(8,128)S(1)}, f32[128,128]{1,0:T(8,128)S(1)}, u32[]{:S(2)}, u32[]{:S(2)}) collective-permute-start(f32[128,128]{1,0:T(8,128)S(1)} %get-tuple-element.47), channel_id=1, source_target_pairs={{0,2},{1,3},{2,0},{3,1},{4,6},{5,7},{6,4},{7,5},{8,10},{9,11},{10,... | collective-permute-start | bytes 196616 | tf_op jit(solution)/shard_map/ppermute | solution.py:469
  20.4 0.0 collective-permute-done.2.refs_5_
  20.4 0.0 copy-start.10
  20.4 3.0 %collective-permute-start.9 = (f32[144,128]{1,0:T(8,128)S(1)}, f32[144,128]{1,0:T(8,128)S(1)}, u32[]{:S(2)}, u32[]{:S(2)}) collective-permute-start(f32[144,128]{1,0:T(8,128)S(1)} %get-tuple-element.48), channel_id=1, source_target_pairs={{0,3},{1,0},{2,1},{3,2},{4,7},{5,4},{6,5},{7,6},{8,11},{9,8},{10,9... | collective-permute-start | bytes 221192 | tf_op jit(solution)/shard_map/ppermute | solution.py:469
  23.4 0.0 collective-permute-done.1.refs_4_
  23.4 0.0 copy-done.9
  23.4 0.0 copy-done.10
  23.4 3.2 %along_xy.1 = (f32[4,2,64,128]{3,2,1,0:T(8,128)S(1)}, f32[528,128]{1,0:T(8,128)S(1)}) custom-call(f32[4]{0:T(128)S(1)} %copy-done.8, f32[4,2,64,128]{3,2,1,0:T(8,128)S(1)} %copy-done, bf16[128,192]{1,0:T(8,128)(2,1)S(1)} %copy-done.9, s32[1,8192]{1,0:T(1,128)S(1)} %bitcast.17, f32[3,8192]{1,0:T(4,128)S(1)} %get-tuple-element.28.force_ref, ...), custom_call_target="tpu_custom_call" | custom-call | flops 20000000000 | bytes 100000000 | tf_op jit(solution)/shard_map/along_xy/pallas_call | solution.py:319
  26.6 1.8 %collective-permute-start.10 = (f32[528,128]{1,0:T(8,128)S(1)}, f32[528,128]{1,0:T(8,128)S(1)}, u32[]{:S(2)}, u32[]{:S(2)}) collective-permute-start(f32[528,128]{1,0:T(8,128)S(1)} %get-tuple-element.49), channel_id=1, source_target_pairs={{0,4},{4,0},{8,12},{12,8},{16,20},{20,16},{24,28},{28,24},{1,5},{5... | collective-permute-start | bytes 811016 | tf_op jit(solution)/shard_map/ppermute | solution.py:286
  28.5 0.0 collective-permute-done.8.refs_2_
  28.5 0.0 collective-permute-done.7.refs_1_
  28.5 0.0 collective-permute-done.9.refs_3_
  28.5 0.0 collective-permute-done.3.far_ref
  28.5 1.1 %collective-permute-done.10.near_ref = f32[528,128]{1,0:T(8,128)S(1)} collective-permute-done((f32[528,128]{1,0:T(8,128)S(1)}, f32[528,128]{1,0:T(8,128)S(1)}, u32[]{:S(2)}, u32[]{:S(2)}) %collective-permute-start.10) | collective-permute-done | bytes 270368 | tf_op jit(solution)/shard_map/ppermute | solution.py:286
  29.6 0.8 %total.1 = (f32[4,2,64,128]{3,2,1,0:T(8,128)}, f32[6,4,256]{2,1,0:T(4,128)}) custom-call(s32[1]{0:T(128)} %bitcast.row_ref.refs_0_, s32[1]{0:T(128)} %bitcast.1.column_ref, f32[4,2,64,128]{3,2,1,0:T(8,128)S(1)} %get-tuple-element.33.along_x_ref, f32[2,8,128]{2,1,0:T(8,128)S(1)} %collective-permute-done.3.far_ref, ...), custom_call_target="tpu_custom_call" | custom-call | flops 1 | bytes 1 | tf_op jit(solution)/shard_map/total/pallas_call | solution.py:454
  (2 shorter events, 0.0 us)
Async XLA Ops:
  0.6 1.9 %collective-permute-start = (f32[4,2,64,128]{3,2,1,0:T(8,128)}, f32[4,2,64,128]{3,2,1,0:T(8,128)S(1)}, u32[]{:S(2)}, u32[]{:S(2)}) collective-permute-start(f32[4,2,64,128]{3,2,1,0:T(8,128)} %fields_ref.3), channel_id=1, source_target_pairs={{0,4},{4,0},{8,12},{12,8},{16,20},{20,16},{24,28},{28,24},{1,5},{5... | collective-permute-start | bytes 786440 | tf_op jit(solution)/shard_map/ppermute | solution.py:286
  1.1 1.4 %copy-start = (f32[4,2,64,128]{3,2,1,0:T(8,128)S(1)}, f32[4,2,64,128]{3,2,1,0:T(8,128)}, u32[]{:S(2)}) copy-start(f32[4,2,64,128]{3,2,1,0:T(8,128)} %fields_ref.3) | copy-start | bytes 786436
  2.5 10.7 %copy-start.1 = (f32[6,8192]{1,0:T(8,128)S(1)}, f32[6,8192]{1,0:T(8,128)}, u32[]{:S(2)}) copy-start(f32[6,8192]{1,0:T(8,128)} %records_ref.1) | copy-start | bytes 589828
  2.5 10.7 %copy-start.4 = (f32[8192]{0:T(1024)S(1)}, f32[8192]{0:T(1024)}, u32[]{:S(2)}) copy-start(f32[8192]{0:T(1024)} %param.15) | copy-start | bytes 98308
  2.5 10.7 %copy-start.5 = (s32[8192]{0:T(1024)S(1)}, s32[8192]{0:T(1024)}, u32[]{:S(2)}) copy-start(s32[8192]{0:T(1024)} %param.18) | copy-start | bytes 98308
  2.5 10.7 %copy-start.6 = (s32[8192]{0:T(1024)S(1)}, s32[8192]{0:T(1024)}, u32[]{:S(2)}) copy-start(s32[8192]{0:T(1024)} %param.19) | copy-start | bytes 98308
  2.5 10.7 %copy-start.7 = (s32[8192]{0:T(1024)S(1)}, s32[8192]{0:T(1024)}, u32[]{:S(2)}) copy-start(s32[8192]{0:T(1024)} %param.16) | copy-start | bytes 98308
  2.6 20.8 %collective-permute-start.1 = (f32[2,4,2,64,128]{4,3,2,1,0:T(8,128)S(1)}, f32[2,4,2,64,128]{4,3,2,1,0:T(8,128)S(1)}, u32[]{:S(2)}, u32[]{:S(2)}) collective-permute-start(f32[2,4,2,64,128]{4,3,2,1,0:T(8,128)S(1)} %pad_maximum_fusion), channel_id=1, source_target_pairs={{0,8},{4,20},{8,0},{12,28},{16,24},{20,4},{24,16},{28,12},{1,9},{5... | collective-permute-start | bytes 1572872 | tf_op jit(solution)/shard_map/ppermute | solution.py:491
  5.5 14.8 %collective-permute-start.2 = (f32[4,2,64,128]{3,2,1,0:T(8,128)S(1)}, f32[4,2,64,128]{3,2,1,0:T(8,128)S(1)}, u32[]{:S(2)}, u32[]{:S(2)}) collective-permute-start(f32[4,2,64,128]{3,2,1,0:T(8,128)S(1)} %copy-done), channel_id=1, source_target_pairs={{0,24},{4,28},{8,16},{12,20},{16,8},{20,12},{24,0},{28,4},{1,25},{... | collective-permute-start | bytes 786440 | tf_op jit(solution)/shard_map/ppermute | solution.py:286
  7.0 9.9 %collective-permute-start.4 = (f32[4,2,16,128]{3,2,1,0:T(8,128)S(1)}, f32[4,2,16,128]{3,2,1,0:T(8,128)S(1)}, u32[]{:S(2)}, u32[]{:S(2)}) collective-permute-start(f32[4,2,16,128]{3,2,1,0:T(8,128)S(1)} %get-tuple-element.37), channel_id=1, source_target_pairs={{0,1},{1,2},{2,3},{3,0},{4,5},{5,6},{6,7},{7,4},{8,9},{9,10},{10,1... | collective-permute-start | bytes 196616 | tf_op jit(solution)/shard_map/ppermute | solution.py:469
  8.6 9.1 %collective-permute-start.5 = (f32[4,2,16,128]{3,2,1,0:T(8,128)S(1)}, f32[4,2,16,128]{3,2,1,0:T(8,128)S(1)}, u32[]{:S(2)}, u32[]{:S(2)}) collective-permute-start(f32[4,2,16,128]{3,2,1,0:T(8,128)S(1)} %get-tuple-element.38), channel_id=1, source_target_pairs={{0,2},{1,3},{2,0},{3,1},{4,6},{5,7},{6,4},{7,5},{8,10},{9,11},{10,... | collective-permute-start | bytes 196616 | tf_op jit(solution)/shard_map/ppermute | solution.py:469
  11.2 6.5 %collective-permute-start.6 = (f32[4,2,16,128]{3,2,1,0:T(8,128)S(1)}, f32[4,2,16,128]{3,2,1,0:T(8,128)S(1)}, u32[]{:S(2)}, u32[]{:S(2)}) collective-permute-start(f32[4,2,16,128]{3,2,1,0:T(8,128)S(1)} %get-tuple-element.39), channel_id=1, source_target_pairs={{0,3},{1,0},{2,1},{3,2},{4,7},{5,4},{6,5},{7,6},{8,11},{9,8},{10,9... | collective-permute-start | bytes 196616 | tf_op jit(solution)/shard_map/ppermute | solution.py:469
  13.2 4.5 %copy-start.2 = (bf16[512,256]{1,0:T(8,128)(2,1)S(1)}, bf16[512,256]{1,0:T(8,128)(2,1)}, u32[]{:S(2)}) copy-start(bf16[512,256]{1,0:T(8,128)(2,1)} %constant.52.clone.high_ref) | copy-start | bytes 786436
  13.3 4.5 %copy-start.3 = (bf16[512,256]{1,0:T(8,128)(2,1)S(1)}, bf16[512,256]{1,0:T(8,128)(2,1)}, u32[]{:S(2)}) copy-start(bf16[512,256]{1,0:T(8,128)(2,1)} %constant.53.clone.low_ref) | copy-start | bytes 786436
  16.9 0.8 %copy-start.8 = (f32[4]{0:T(128)S(1)}, f32[4]{0:T(128)}, u32[]{:S(2)}) copy-start(f32[4]{0:T(128)} %viscous_ref.3) | copy-start | bytes 52
  16.9 11.6 %collective-permute-start.3 = (f32[2,8,128]{2,1,0:T(8,128)S(1)}, f32[2,8,128]{2,1,0:T(8,128)S(1)}, u32[]{:S(2)}, u32[]{:S(2)}) collective-permute-start(f32[2,8,128]{2,1,0:T(8,128)S(1)} %get-tuple-element.34), channel_id=1, source_target_pairs={{4,8},{12,16},{20,24},{8,4},{16,12},{24,20},{5,9},{13,17},{21,25},... | collective-permute-start | bytes 24584 | tf_op jit(solution)/shard_map/ppermute | solution.py:498
  17.8 5.6 %copy-start.9 = (bf16[128,192]{1,0:T(8,128)(2,1)S(1)}, bf16[128,192]{1,0:T(8,128)(2,1)}, u32[]{:S(2)}) copy-start(bf16[128,192]{1,0:T(8,128)(2,1)} %constant.54.clone.operator_ref) | copy-start | bytes 147460
  18.9 9.6 %collective-permute-start.7 = (f32[144,128]{1,0:T(8,128)S(1)}, f32[144,128]{1,0:T(8,128)S(1)}, u32[]{:S(2)}, u32[]{:S(2)}) collective-permute-start(f32[144,128]{1,0:T(8,128)S(1)} %get-tuple-element.46), channel_id=1, source_target_pairs={{0,1},{1,2},{2,3},{3,0},{4,5},{5,6},{6,7},{7,4},{8,9},{9,10},{10,1... | collective-permute-start | bytes 221192 | tf_op jit(solution)/shard_map/ppermute | solution.py:469
  19.6 8.8 %collective-permute-start.8 = (f32[128,128]{1,0:T(8,128)S(1)}, f32[128,128]{1,0:T(8,128)S(1)}, u32[]{:S(2)}, u32[]{:S(2)}) collective-permute-start(f32[128,128]{1,0:T(8,128)S(1)} %get-tuple-element.47), channel_id=1, source_target_pairs={{0,2},{1,3},{2,0},{3,1},{4,6},{5,7},{6,4},{7,5},{8,10},{9,11},{10,... | collective-permute-start | bytes 196616 | tf_op jit(solution)/shard_map/ppermute | solution.py:469
  20.4 3.0 %copy-start.10 = (f32[512]{0:T(512)S(1)}, f32[512]{0:T(512)}, u32[]{:S(2)}) copy-start(f32[512]{0:T(512)} %constant.55.clone.refs_1_) | copy-start | bytes 6148
  20.4 8.1 %collective-permute-start.9 = (f32[144,128]{1,0:T(8,128)S(1)}, f32[144,128]{1,0:T(8,128)S(1)}, u32[]{:S(2)}, u32[]{:S(2)}) collective-permute-start(f32[144,128]{1,0:T(8,128)S(1)} %get-tuple-element.48), channel_id=1, source_target_pairs={{0,3},{1,0},{2,1},{3,2},{4,7},{5,4},{6,5},{7,6},{8,11},{9,8},{10,9... | collective-permute-start | bytes 221192 | tf_op jit(solution)/shard_map/ppermute | solution.py:469
  26.6 3.0 %collective-permute-start.10 = (f32[528,128]{1,0:T(8,128)S(1)}, f32[528,128]{1,0:T(8,128)S(1)}, u32[]{:S(2)}, u32[]{:S(2)}) collective-permute-start(f32[528,128]{1,0:T(8,128)S(1)} %get-tuple-element.49), channel_id=1, source_target_pairs={{0,4},{4,0},{8,12},{12,8},{16,20},{20,16},{24,28},{28,24},{1,5},{5... | collective-permute-start | bytes 811016 | tf_op jit(solution)/shard_map/ppermute | solution.py:286

commit v5 on v4

--- a/solution.py
+++ b/solution.py
@@ -328,6 +328,25 @@
     )(viscous, fields, operator, cell, force, *y_part)
 
 
+def store_kernel(source_ref, target_ref, sem):
+    copy = pltpu.make_async_copy(source_ref, target_ref, sem)
+    copy.start()
+    copy.wait()
+
+
+def stored(value):
+    return pl.pallas_call(
+        store_kernel,
+        out_shape=any_space(value.shape),
+        in_specs=[VMEM],
+        out_specs=pl.BlockSpec(memory_space=pl.ANY),
+        scratch_shapes=[pltpu.SemaphoreType.DMA(())],
+        compiler_params=params(8),
+        cost_estimate=CHEAP,
+        name="stored",
+    )(value)
+
+
 def along_z_kernel(viscous_ref, high_ref, low_ref, side_ref, *refs):
     count = len(refs) // 2
     blocks, results = refs[:count], refs[count:]
@@ -498,13 +517,14 @@
     far = lax.ppermute(far, "row", pairs + [(b, a) for a, b in pairs])
     terms_z = exchange(along_z(diffusivity, side, lines))
     terms_x, *near_y = along_xy(diffusivity, fields, cell, force, (row, near, mate, others) if gathered else ())
+    kept, terms_x, near_y = lax.optimization_barrier((kept, terms_x, near_y))
     if gathered:
         near = same_core(near_y[0], 1)
     else:
         terms_x = terms_x + pencil_along_y(diffusivity, fields)
         near = lax.ppermute(near, "row", [(i, i ^ 1) for i in range(rows) if i ^ 1 < rows])
     tendency, arrivals = total(gathered, row, column, terms_x, far, side_particles(terms_z), near, terms_z)
-    return (tendency, kept, arrivals.transpose(1, 0, 2))
+    return (tendency, stored(kept), arrivals.transpose(1, 0, 2))
 
 
 def solution(mesh):

time: 30.6 us -> 29.9 us (0.977)
  waiting for transfers between devices: 1.53 us -> 0.83 us
    ppermute x3, waiting for transfers between devices: 1.51 us -> 0.79 us  [same_core(): lax.ppermute(block, 'row', [(i, i ^ s) for i in range(lax.axis_size('row'...]
    pallas_call x0 -> x1, Pallas kernels: none -> 0.71 us  [stored(): pl.pallas_call(store_kernel, out_shape=any_space(value.shape), in_specs=[...]
    ppermute x3, starting transfers between devices: 3.82 us -> 3.14 us  [same_core(): lax.ppermute(block, 'row', [(i, i ^ s) for i in range(lax.axis_size('row'...]
    ppermute x6, starting transfers between devices: 10 us -> 10.7 us  [exchange(): lax.ppermute(blocks[s], 'col', [(i, (i + s) % count) for i in range(count)])]
    pallas_call x1, Pallas kernels: 3.64 us -> 3.07 us  [advance(): pl.pallas_call(functools.partial(advance_kernel, chunk_of(particles, rows...]
  transfers between devices with their start and end apart: 11 -> 11, of which waited for: 2 -> 2; matrix products, arithmetic and copies ran while one was open for 3% -> 3% of each run, Pallas kernels for 26% -> 27%
where the time goes in v5:
time: 29.9 us; the launch traced here: 29.7 us
  starting transfers between devices  17.4 us (58%)
  Pallas kernels  8.9 us (30%)
  between operations  1.49 us (5%)
  local copies, waits for them, and re-layouts  1.06 us (4%)
  waiting for transfers between devices  0.83 us (3%)
    ppermute x6, starting transfers between devices, exchange(): lax.ppermute(blocks[s], 'col', [(i, (i + s) % count) for i in range(count)])  10.7 us
    pallas_call x1, Pallas kernels, along_xy(): pl.pallas_call(functools.partial(along_xy_kernel, chunk_of(particles, 2 *...  3.23 us
    ppermute x3, starting transfers between devices, same_core(): lax.ppermute(block, 'row', [(i, i ^ s) for i in range(lax.axis_size('row'...  3.14 us
    pallas_call x1, Pallas kernels, advance(): pl.pallas_call(functools.partial(advance_kernel, chunk_of(particles, rows...  3.07 us
    ppermute x1, starting transfers between devices, on_device(): both = lax.ppermute(both, 'row', [(i, neighbour(i)) for i in range(rows)])  2.93 us
    pallas_call x1, Pallas kernels, along_z(): pl.pallas_call(along_z_kernel, out_shape=tuple((any_space((size // lanes...  1.12 us
    dynamic_slice x1, local copies, waits for them, and re-layouts, on_device(): lax.dynamic_slice_in_dim(fields, (column + s) % columns * width, width, a...  1 us
    ppermute x3, waiting for transfers between devices, same_core(): lax.ppermute(block, 'row', [(i, i ^ s) for i in range(lax.axis_size('row'...  0.79 us
  transfers between devices with their start and end apart: 11, of which 2 were waited for; matrix products, arithmetic and copies ran while one was open for 3% of the time, Pallas kernels for 27%

profile of v5, /device:TPU:0, one launch (start us, length us, event | category | flops | bytes accessed | tf_op | source)
XLA Modules:
  0.0 29.7 jit_solution(16216156433185320497)
XLA Ops:
  0.6 0.5 %collective-permute-start = (f32[4,2,64,128]{3,2,1,0:T(8,128)}, f32[4,2,64,128]{3,2,1,0:T(8,128)S(1)}, u32[]{:S(2)}, u32[]{:S(2)}) collective-permute-start(f32[4,2,64,128]{3,2,1,0:T(8,128)} %fields_ref.3), channel_id=1, source_target_pairs={{0,4},{4,0},{8,12},{12,8},{16,20},{20,16},{24,28},{28,24},{1,5},{5... | collective-permute-start | bytes 786440 | tf_op jit(solution)/shard_map/ppermute | solution.py:286
  1.1 0.0 copy-start
  1.1 1.0 %constant_dynamic-slice_fusion = (f32[4,2,16,128]{3,2,1,0:T(8,128)S(1)}, f32[4,2,16,128]{3,2,1,0:T(8,128)S(1)}, f32[4,2,16,128]{3,2,1,0:T(8,128)S(1)}, f32[4,2,16,128]{3,2,1,0:T(8,128)S(1)}) fusion(f32[4,2,64,128]{3,2,1,0:T(8,128)} %fields_ref.3, s32[]{:T(128)S(6)} %select_n.38, s32[]{:T(128)S(6)} %select_n.36, s32[]{:T(128)S(6)} %select_n.34, s32[]{:T(128)S(6)} %select_n.32), kind=kLoop, calls=%fused_computation.1 | loop fusion | bytes 524304 | tf_op jit(solution)/shard_map/dynamic_slice | solution.py:498
  2.2 0.4 %collective-permute-done.refs_3_ = f32[4,2,64,128]{3,2,1,0:T(8,128)S(1)} collective-permute-done((f32[4,2,64,128]{3,2,1,0:T(8,128)}, f32[4,2,64,128]{3,2,1,0:T(8,128)S(1)}, u32[]{:S(2)}, u32[]{:S(2)}) %collective-permute-start) | collective-permute-done | bytes 262176 | tf_op jit(solution)/shard_map/ppermute | solution.py:286
  2.5 0.0 copy-done
  2.5 0.0 copy-start.1
  2.5 0.0 copy-start.4
  2.5 0.0 copy-start.5
  2.5 0.0 copy-start.6
  2.5 0.0 copy-start.7
  2.6 2.9 %collective-permute-start.1 = (f32[2,4,2,64,128]{4,3,2,1,0:T(8,128)S(1)}, f32[2,4,2,64,128]{4,3,2,1,0:T(8,128)S(1)}, u32[]{:S(2)}, u32[]{:S(2)}) collective-permute-start(f32[2,4,2,64,128]{4,3,2,1,0:T(8,128)S(1)} %pad_maximum_fusion), channel_id=1, source_target_pairs={{0,8},{4,20},{8,0},{12,28},{16,24},{20,4},{24,16},{28,12},{1,9},{5... | collective-permute-start | bytes 1572872 | tf_op jit(solution)/shard_map/ppermute | solution.py:510
  5.5 1.5 %collective-permute-start.2 = (f32[4,2,64,128]{3,2,1,0:T(8,128)S(1)}, f32[4,2,64,128]{3,2,1,0:T(8,128)S(1)}, u32[]{:S(2)}, u32[]{:S(2)}) collective-permute-start(f32[4,2,64,128]{3,2,1,0:T(8,128)S(1)} %copy-done), channel_id=1, source_target_pairs={{0,24},{4,28},{8,16},{12,20},{16,8},{20,12},{24,0},{28,4},{1,25},{... | collective-permute-start | bytes 786440 | tf_op jit(solution)/shard_map/ppermute | solution.py:286
  7.0 1.6 %collective-permute-start.4 = (f32[4,2,16,128]{3,2,1,0:T(8,128)S(1)}, f32[4,2,16,128]{3,2,1,0:T(8,128)S(1)}, u32[]{:S(2)}, u32[]{:S(2)}) collective-permute-start(f32[4,2,16,128]{3,2,1,0:T(8,128)S(1)} %get-tuple-element.43), channel_id=1, source_target_pairs={{0,1},{1,2},{2,3},{3,0},{4,5},{5,6},{6,7},{7,4},{8,9},{9,10},{10,1... | collective-permute-start | bytes 196616 | tf_op jit(solution)/shard_map/ppermute | solution.py:488
  8.6 2.6 %collective-permute-start.5 = (f32[4,2,16,128]{3,2,1,0:T(8,128)S(1)}, f32[4,2,16,128]{3,2,1,0:T(8,128)S(1)}, u32[]{:S(2)}, u32[]{:S(2)}) collective-permute-start(f32[4,2,16,128]{3,2,1,0:T(8,128)S(1)} %get-tuple-element.44), channel_id=1, source_target_pairs={{0,2},{1,3},{2,0},{3,1},{4,6},{5,7},{6,4},{7,5},{8,10},{9,11},{10,... | collective-permute-start | bytes 196616 | tf_op jit(solution)/shard_map/ppermute | solution.py:488
  11.2 1.3 %collective-permute-start.6 = (f32[4,2,16,128]{3,2,1,0:T(8,128)S(1)}, f32[4,2,16,128]{3,2,1,0:T(8,128)S(1)}, u32[]{:S(2)}, u32[]{:S(2)}) collective-permute-start(f32[4,2,16,128]{3,2,1,0:T(8,128)S(1)} %get-tuple-element.45), channel_id=1, source_target_pairs={{0,3},{1,0},{2,1},{3,2},{4,7},{5,4},{6,5},{7,6},{8,11},{9,8},{10,9... | collective-permute-start | bytes 196616 | tf_op jit(solution)/shard_map/ppermute | solution.py:488
  13.2 0.0 copy-done.1
  13.2 0.0 copy-done.4
  13.2 0.0 copy-done.5
  13.2 0.0 copy-done.6
  13.2 0.0 copy-done.7
  13.2 0.0 copy-start.2
  13.3 0.0 copy-start.3
  13.3 3.1 %advance.1 = (f32[6,8192]{1,0:T(8,128)S(1)}, f32[3,8192]{1,0:T(4,128)S(1)}, f32[2,8,128]{2,1,0:T(8,128)S(1)}, f32[2,8,128]{2,1,0:T(8,128)S(1)}, f32[2,2,8,128]{3,2,1,0:T(8,128)S(1)}) custom-call(s32[1]{0:T(128)} %bitcast.row_ref.refs_0_, s32[1,1]{1,0:T(1,128)} %bitcast.10.count_ref, f32[4,2,64,128]{3,2,1,0:T(8,128)S(1)} %copy-done, f32[6,8192]{1,0:T(8,128)S(1)} %copy-done.1, ...), custom_call_target="tpu_custom_call" | custom-call | flops 1 | bytes 1 | tf_op jit(solution)/shard_map/advance/pallas_call | solution.py:190
  16.3 0.0 collective-permute-done.4.refs_1_
  16.4 0.0 copy-start.8
  16.4 0.7 %collective-permute-start.3 = (f32[2,8,128]{2,1,0:T(8,128)S(1)}, f32[2,8,128]{2,1,0:T(8,128)S(1)}, u32[]{:S(2)}, u32[]{:S(2)}) collective-permute-start(f32[2,8,128]{2,1,0:T(8,128)S(1)} %get-tuple-element.40), channel_id=1, source_target_pairs={{4,8},{12,16},{20,24},{8,4},{16,12},{24,20},{5,9},{13,17},{21,25},... | collective-permute-start | bytes 24584 | tf_op jit(solution)/shard_map/ppermute | solution.py:517
  17.1 0.0 collective-permute-done.5.refs_2_
  17.1 0.0 collective-permute-done.6.refs_3_
  17.1 0.0 copy-done.2
  17.1 0.0 copy-done.3
  17.1 0.0 copy-done.8
  17.1 0.0 copy-start.9
  17.1 1.1 %along_z.1 = (f32[128,128]{1,0:T(8,128)S(1)}, f32[144,128]{1,0:T(8,128)S(1)}, f32[128,128]{1,0:T(8,128)S(1)}, f32[144,128]{1,0:T(8,128)S(1)}) custom-call(f32[4]{0:T(128)S(1)} %copy-done.8, bf16[512,256]{1,0:T(8,128)(2,1)S(1)} %copy-done.2, bf16[512,256]{1,0:T(8,128)(2,1)S(1)} %copy-done.3, f32[2,2,8,128]{3,2,1,0:T(8,128)S(1)} %get-tuple-element.46.side_ref, ...), custom_call_target="tpu_custom_call" | custom-call | flops 1 | bytes 1 | tf_op jit(solution)/shard_map/along_z/pallas_call | solution.py:396
  18.2 0.7 %collective-permute-start.7 = (f32[144,128]{1,0:T(8,128)S(1)}, f32[144,128]{1,0:T(8,128)S(1)}, u32[]{:S(2)}, u32[]{:S(2)}) collective-permute-start(f32[144,128]{1,0:T(8,128)S(1)} %get-tuple-element.52), channel_id=1, source_target_pairs={{0,1},{1,2},{2,3},{3,0},{4,5},{5,6},{6,7},{7,4},{8,9},{9,10},{10,1... | collective-permute-start | bytes 221192 | tf_op jit(solution)/shard_map/ppermute | solution.py:488
  19.0 1.4 %collective-permute-start.8 = (f32[128,128]{1,0:T(8,128)S(1)}, f32[128,128]{1,0:T(8,128)S(1)}, u32[]{:S(2)}, u32[]{:S(2)}) collective-permute-start(f32[128,128]{1,0:T(8,128)S(1)} %get-tuple-element.53), channel_id=1, source_target_pairs={{0,2},{1,3},{2,0},{3,1},{4,6},{5,7},{6,4},{7,5},{8,10},{9,11},{10,... | collective-permute-start | bytes 196616 | tf_op jit(solution)/shard_map/ppermute | solution.py:488
  20.4 0.0 collective-permute-done.2.refs_5_
  20.4 0.0 copy-start.10
  20.4 3.0 %collective-permute-start.9 = (f32[144,128]{1,0:T(8,128)S(1)}, f32[144,128]{1,0:T(8,128)S(1)}, u32[]{:S(2)}, u32[]{:S(2)}) collective-permute-start(f32[144,128]{1,0:T(8,128)S(1)} %get-tuple-element.54), channel_id=1, source_target_pairs={{0,3},{1,0},{2,1},{3,2},{4,7},{5,4},{6,5},{7,6},{8,11},{9,8},{10,9... | collective-permute-start | bytes 221192 | tf_op jit(solution)/shard_map/ppermute | solution.py:488
  23.4 0.0 collective-permute-done.1.refs_4_
  23.4 0.0 copy-done.9
  23.4 0.0 copy-done.10
  23.4 3.2 %along_xy.1 = (f32[4,2,64,128]{3,2,1,0:T(8,128)S(1)}, f32[528,128]{1,0:T(8,128)S(1)}) custom-call(f32[4]{0:T(128)S(1)} %copy-done.8, f32[4,2,64,128]{3,2,1,0:T(8,128)S(1)} %copy-done, bf16[128,192]{1,0:T(8,128)(2,1)S(1)} %copy-done.9, s32[1,8192]{1,0:T(1,128)S(1)} %bitcast.17, f32[3,8192]{1,0:T(4,128)S(1)} %get-tuple-element.32.force_ref, ...), custom_call_target="tpu_custom_call" | custom-call | flops 20000000000 | bytes 100000000 | tf_op jit(solution)/shard_map/along_xy/pallas_call | solution.py:319
  26.6 1.1 %collective-permute-start.10 = (f32[528,128]{1,0:T(8,128)S(1)}, f32[528,128]{1,0:T(8,128)S(1)}, u32[]{:S(2)}, u32[]{:S(2)}) collective-permute-start(f32[528,128]{1,0:T(8,128)S(1)} %get-tuple-element.55), channel_id=1, source_target_pairs={{0,4},{4,0},{8,12},{12,8},{16,20},{20,16},{24,28},{28,24},{1,5},{5... | collective-permute-start | bytes 811016 | tf_op jit(solution)/shard_map/ppermute | solution.py:286
  27.8 0.0 collective-permute-done.8.refs_2_
  27.8 0.0 collective-permute-done.7.refs_1_
  27.8 0.0 collective-permute-done.9.refs_3_
  27.8 0.7 %stored.1 = f32[6,8192]{1,0:T(8,128)} custom-call(f32[6,8192]{1,0:T(8,128)S(1)} %get-tuple-element.57.source_ref), custom_call_target="tpu_custom_call" | custom-call | flops 1 | bytes 1 | tf_op jit(solution)/shard_map/stored/pallas_call | solution.py:338
  28.5 0.0 collective-permute-done.3.far_ref
  28.5 0.4 %collective-permute-done.10.near_ref = f32[528,128]{1,0:T(8,128)S(1)} collective-permute-done((f32[528,128]{1,0:T(8,128)S(1)}, f32[528,128]{1,0:T(8,128)S(1)}, u32[]{:S(2)}, u32[]{:S(2)}) %collective-permute-start.10) | collective-permute-done | bytes 270368 | tf_op jit(solution)/shard_map/ppermute | solution.py:286
  29.0 0.8 %total.1 = (f32[4,2,64,128]{3,2,1,0:T(8,128)}, f32[6,4,256]{2,1,0:T(4,128)}) custom-call(s32[1]{0:T(128)} %bitcast.row_ref.refs_0_, s32[1]{0:T(128)} %bitcast.1.column_ref, f32[4,2,64,128]{3,2,1,0:T(8,128)S(1)} %get-tuple-element.39.along_x_ref, f32[2,8,128]{2,1,0:T(8,128)S(1)} %collective-permute-done.3.far_ref, ...), custom_call_target="tpu_custom_call" | custom-call | flops 1 | bytes 1 | tf_op jit(solution)/shard_map/total/pallas_call | solution.py:473
  (2 shorter events, 0.0 us)
Async XLA Ops:
  0.6 1.9 %collective-permute-start = (f32[4,2,64,128]{3,2,1,0:T(8,128)}, f32[4,2,64,128]{3,2,1,0:T(8,128)S(1)}, u32[]{:S(2)}, u32[]{:S(2)}) collective-permute-start(f32[4,2,64,128]{3,2,1,0:T(8,128)} %fields_ref.3), channel_id=1, source_target_pairs={{0,4},{4,0},{8,12},{12,8},{16,20},{20,16},{24,28},{28,24},{1,5},{5... | collective-permute-start | bytes 786440 | tf_op jit(solution)/shard_map/ppermute | solution.py:286
  1.1 1.4 %copy-start = (f32[4,2,64,128]{3,2,1,0:T(8,128)S(1)}, f32[4,2,64,128]{3,2,1,0:T(8,128)}, u32[]{:S(2)}) copy-start(f32[4,2,64,128]{3,2,1,0:T(8,128)} %fields_ref.3) | copy-start | bytes 786436
  2.5 10.7 %copy-start.1 = (f32[6,8192]{1,0:T(8,128)S(1)}, f32[6,8192]{1,0:T(8,128)}, u32[]{:S(2)}) copy-start(f32[6,8192]{1,0:T(8,128)} %records_ref.1) | copy-start | bytes 589828
  2.5 10.7 %copy-start.4 = (f32[8192]{0:T(1024)S(1)}, f32[8192]{0:T(1024)}, u32[]{:S(2)}) copy-start(f32[8192]{0:T(1024)} %param.15) | copy-start | bytes 98308
  2.5 10.7 %copy-start.5 = (s32[8192]{0:T(1024)S(1)}, s32[8192]{0:T(1024)}, u32[]{:S(2)}) copy-start(s32[8192]{0:T(1024)} %param.18) | copy-start | bytes 98308
  2.5 10.7 %copy-start.6 = (s32[8192]{0:T(1024)S(1)}, s32[8192]{0:T(1024)}, u32[]{:S(2)}) copy-start(s32[8192]{0:T(1024)} %param.19) | copy-start | bytes 98308
  2.5 10.7 %copy-start.7 = (s32[8192]{0:T(1024)S(1)}, s32[8192]{0:T(1024)}, u32[]{:S(2)}) copy-start(s32[8192]{0:T(1024)} %param.16) | copy-start | bytes 98308
  2.6 20.8 %collective-permute-start.1 = (f32[2,4,2,64,128]{4,3,2,1,0:T(8,128)S(1)}, f32[2,4,2,64,128]{4,3,2,1,0:T(8,128)S(1)}, u32[]{:S(2)}, u32[]{:S(2)}) collective-permute-start(f32[2,4,2,64,128]{4,3,2,1,0:T(8,128)S(1)} %pad_maximum_fusion), channel_id=1, source_target_pairs={{0,8},{4,20},{8,0},{12,28},{16,24},{20,4},{24,16},{28,12},{1,9},{5... | collective-permute-start | bytes 1572872 | tf_op jit(solution)/shard_map/ppermute | solution.py:510
  5.5 14.8 %collective-permute-start.2 = (f32[4,2,64,128]{3,2,1,0:T(8,128)S(1)}, f32[4,2,64,128]{3,2,1,0:T(8,128)S(1)}, u32[]{:S(2)}, u32[]{:S(2)}) collective-permute-start(f32[4,2,64,128]{3,2,1,0:T(8,128)S(1)} %copy-done), channel_id=1, source_target_pairs={{0,24},{4,28},{8,16},{12,20},{16,8},{20,12},{24,0},{28,4},{1,25},{... | collective-permute-start | bytes 786440 | tf_op jit(solution)/shard_map/ppermute | solution.py:286
  7.0 9.3 %collective-permute-start.4 = (f32[4,2,16,128]{3,2,1,0:T(8,128)S(1)}, f32[4,2,16,128]{3,2,1,0:T(8,128)S(1)}, u32[]{:S(2)}, u32[]{:S(2)}) collective-permute-start(f32[4,2,16,128]{3,2,1,0:T(8,128)S(1)} %get-tuple-element.43), channel_id=1, source_target_pairs={{0,1},{1,2},{2,3},{3,0},{4,5},{5,6},{6,7},{7,4},{8,9},{9,10},{10,1... | collective-permute-start | bytes 196616 | tf_op jit(solution)/shard_map/ppermute | solution.py:488
  8.6 8.5 %collective-permute-start.5 = (f32[4,2,16,128]{3,2,1,0:T(8,128)S(1)}, f32[4,2,16,128]{3,2,1,0:T(8,128)S(1)}, u32[]{:S(2)}, u32[]{:S(2)}) collective-permute-start(f32[4,2,16,128]{3,2,1,0:T(8,128)S(1)} %get-tuple-element.44), channel_id=1, source_target_pairs={{0,2},{1,3},{2,0},{3,1},{4,6},{5,7},{6,4},{7,5},{8,10},{9,11},{10,... | collective-permute-start | bytes 196616 | tf_op jit(solution)/shard_map/ppermute | solution.py:488
  11.2 5.9 %collective-permute-start.6 = (f32[4,2,16,128]{3,2,1,0:T(8,128)S(1)}, f32[4,2,16,128]{3,2,1,0:T(8,128)S(1)}, u32[]{:S(2)}, u32[]{:S(2)}) collective-permute-start(f32[4,2,16,128]{3,2,1,0:T(8,128)S(1)} %get-tuple-element.45), channel_id=1, source_target_pairs={{0,3},{1,0},{2,1},{3,2},{4,7},{5,4},{6,5},{7,6},{8,11},{9,8},{10,9... | collective-permute-start | bytes 196616 | tf_op jit(solution)/shard_map/ppermute | solution.py:488
  13.2 3.8 %copy-start.2 = (bf16[512,256]{1,0:T(8,128)(2,1)S(1)}, bf16[512,256]{1,0:T(8,128)(2,1)}, u32[]{:S(2)}) copy-start(bf16[512,256]{1,0:T(8,128)(2,1)} %constant.52.clone.high_ref) | copy-start | bytes 786436
  13.3 3.8 %copy-start.3 = (bf16[512,256]{1,0:T(8,128)(2,1)S(1)}, bf16[512,256]{1,0:T(8,128)(2,1)}, u32[]{:S(2)}) copy-start(bf16[512,256]{1,0:T(8,128)(2,1)} %constant.53.clone.low_ref) | copy-start | bytes 786436
  16.4 0.7 %copy-start.8 = (f32[4]{0:T(128)S(1)}, f32[4]{0:T(128)}, u32[]{:S(2)}) copy-start(f32[4]{0:T(128)} %viscous_ref.3) | copy-start | bytes 52
  16.4 12.1 %collective-permute-start.3 = (f32[2,8,128]{2,1,0:T(8,128)S(1)}, f32[2,8,128]{2,1,0:T(8,128)S(1)}, u32[]{:S(2)}, u32[]{:S(2)}) collective-permute-start(f32[2,8,128]{2,1,0:T(8,128)S(1)} %get-tuple-element.40), channel_id=1, source_target_pairs={{4,8},{12,16},{20,24},{8,4},{16,12},{24,20},{5,9},{13,17},{21,25},... | collective-permute-start | bytes 24584 | tf_op jit(solution)/shard_map/ppermute | solution.py:517
  17.1 6.3 %copy-start.9 = (bf16[128,192]{1,0:T(8,128)(2,1)S(1)}, bf16[128,192]{1,0:T(8,128)(2,1)}, u32[]{:S(2)}) copy-start(bf16[128,192]{1,0:T(8,128)(2,1)} %constant.54.clone.operator_ref) | copy-start | bytes 147460
  18.2 9.5 %collective-permute-start.7 = (f32[144,128]{1,0:T(8,128)S(1)}, f32[144,128]{1,0:T(8,128)S(1)}, u32[]{:S(2)}, u32[]{:S(2)}) collective-permute-start(f32[144,128]{1,0:T(8,128)S(1)} %get-tuple-element.52), channel_id=1, source_target_pairs={{0,1},{1,2},{2,3},{3,0},{4,5},{5,6},{6,7},{7,4},{8,9},{9,10},{10,1... | collective-permute-start | bytes 221192 | tf_op jit(solution)/shard_map/ppermute | solution.py:488
  19.0 8.8 %collective-permute-start.8 = (f32[128,128]{1,0:T(8,128)S(1)}, f32[128,128]{1,0:T(8,128)S(1)}, u32[]{:S(2)}, u32[]{:S(2)}) collective-permute-start(f32[128,128]{1,0:T(8,128)S(1)} %get-tuple-element.53), channel_id=1, source_target_pairs={{0,2},{1,3},{2,0},{3,1},{4,6},{5,7},{6,4},{7,5},{8,10},{9,11},{10,... | collective-permute-start | bytes 196616 | tf_op jit(solution)/shard_map/ppermute | solution.py:488
  20.4 3.0 %copy-start.10 = (f32[512]{0:T(512)S(1)}, f32[512]{0:T(512)}, u32[]{:S(2)}) copy-start(f32[512]{0:T(512)} %constant.55.clone.refs_1_) | copy-start | bytes 6148
  20.4 7.4 %collective-permute-start.9 = (f32[144,128]{1,0:T(8,128)S(1)}, f32[144,128]{1,0:T(8,128)S(1)}, u32[]{:S(2)}, u32[]{:S(2)}) collective-permute-start(f32[144,128]{1,0:T(8,128)S(1)} %get-tuple-element.54), channel_id=1, source_target_pairs={{0,3},{1,0},{2,1},{3,2},{4,7},{5,4},{6,5},{7,6},{8,11},{9,8},{10,9... | collective-permute-start | bytes 221192 | tf_op jit(solution)/shard_map/ppermute | solution.py:488
  26.6 2.3 %collective-permute-start.10 = (f32[528,128]{1,0:T(8,128)S(1)}, f32[528,128]{1,0:T(8,128)S(1)}, u32[]{:S(2)}, u32[]{:S(2)}) collective-permute-start(f32[528,128]{1,0:T(8,128)S(1)} %get-tuple-element.55), channel_id=1, source_target_pairs={{0,4},{4,0},{8,12},{12,8},{16,20},{20,16},{24,28},{28,24},{1,5},{5... | collective-permute-start | bytes 811016 | tf_op jit(solution)/shard_map/ppermute | solution.py:286

commit v6 on v5

--- a/solution.py
+++ b/solution.py
@@ -347,7 +347,10 @@
     )(value)
 
 
-def along_z_kernel(viscous_ref, high_ref, low_ref, side_ref, *refs):
+def along_z_kernel(diffusivity_ref, high_ref, low_ref, side_ref, *refs):
+    *refs, viscous_ref, viscous_sem = refs
+    fetch = pltpu.make_async_copy(diffusivity_ref, viscous_ref, viscous_sem)
+    fetch.start()
     count = len(refs) // 2
     blocks, results = refs[:count], refs[count:]
     parts, planes, width, lanes = blocks[0].shape
@@ -360,6 +363,7 @@
 
     high = lines(0)
     both = dot(high, high_ref[...]) + dot(lines(1), high_ref[...]) + dot(high, low_ref[...])
+    fetch.wait()
     for s in range(count):
         speed = blocks[(-s) % count][2]
         for component in range(parts):
@@ -396,8 +400,9 @@
     return pl.pallas_call(
         along_z_kernel,
         out_shape=tuple(any_space((size // lanes + MIG // LANES * 8 * len(riding(s, count)), lanes)) for s in range(count)),
-        in_specs=[SMEM] + [VMEM] * (3 + count),
+        in_specs=[pl.BlockSpec(memory_space=pl.ANY)] + [VMEM] * (3 + count),
         out_specs=(VMEM,) * count,
+        scratch_shapes=[pltpu.SMEM(viscous.shape, jnp.float32), pltpu.SemaphoreType.DMA(())],
         compiler_params=params(48),
         cost_estimate=CHEAP,
         name="along_z",

time: 29.9 us -> 29.4 us (0.983)
  Pallas kernels: 8.9 us -> 8.41 us
    pallas_call x1, Pallas kernels: 1.12 us -> 0.63 us  [along_z(): pl.pallas_call(along_z_kernel, out_shape=tuple((any_space((size // lanes...]
    ppermute x6, starting transfers between devices: 10.7 us -> 11.2 us  [exchange(): lax.ppermute(blocks[s], 'col', [(i, (i + s) % count) for i in range(count)])]
    ppermute x3, starting transfers between devices: 3.14 us -> 2.66 us  [same_core(): lax.ppermute(block, 'row', [(i, i ^ s) for i in range(lax.axis_size('row'...]
  transfers between devices with their start and end apart: 11 -> 11, of which waited for: 2 -> 2; matrix products, arithmetic and copies ran while one was open for 3% -> 3% of each run, Pallas kernels for 27% -> 26%
where the time goes in v6:
time: 29.4 us; the launch traced here: 29.2 us
  starting transfers between devices  17.4 us (59%)
  Pallas kernels  8.41 us (29%)
  between operations  1.49 us (5%)
  local copies, waits for them, and re-layouts  1.06 us (4%)
  waiting for transfers between devices  0.83 us (3%)
    ppermute x6, starting transfers between devices, exchange(): lax.ppermute(blocks[s], 'col', [(i, (i + s) % count) for i in range(count)])  11.2 us
    pallas_call x1, Pallas kernels, along_xy(): pl.pallas_call(functools.partial(along_xy_kernel, chunk_of(particles, 2 *...  3.23 us
    pallas_call x1, Pallas kernels, advance(): pl.pallas_call(functools.partial(advance_kernel, chunk_of(particles, rows...  3.07 us
    ppermute x1, starting transfers between devices, on_device(): both = lax.ppermute(both, 'row', [(i, neighbour(i)) for i in range(rows)])  2.93 us
    ppermute x3, starting transfers between devices, same_core(): lax.ppermute(block, 'row', [(i, i ^ s) for i in range(lax.axis_size('row'...  2.66 us
    dynamic_slice x1, local copies, waits for them, and re-layouts, on_device(): lax.dynamic_slice_in_dim(fields, (column + s) % columns * width, width, a...  1 us
    ppermute x3, waiting for transfers between devices, same_core(): lax.ppermute(block, 'row', [(i, i ^ s) for i in range(lax.axis_size('row'...  0.79 us
    pallas_call x1, Pallas kernels, total(): pl.pallas_call(functools.partial(total_kernel, gathered), out_shape=(any_...  0.76 us
  transfers between devices with their start and end apart: 11, of which 2 were waited for; matrix products, arithmetic and copies ran while one was open for 3% of the time, Pallas kernels for 26%

profile of v6, /device:TPU:0, one launch (start us, length us, event | category | flops | bytes accessed | tf_op | source)
XLA Modules:
  0.0 29.2 jit_solution(5884578854600963035)
XLA Ops:
  0.6 0.5 %collective-permute-start = (f32[4,2,64,128]{3,2,1,0:T(8,128)}, f32[4,2,64,128]{3,2,1,0:T(8,128)S(1)}, u32[]{:S(2)}, u32[]{:S(2)}) collective-permute-start(f32[4,2,64,128]{3,2,1,0:T(8,128)} %fields_ref.3), channel_id=1, source_target_pairs={{0,4},{4,0},{8,12},{12,8},{16,20},{20,16},{24,28},{28,24},{1,5},{5... | collective-permute-start | bytes 786440 | tf_op jit(solution)/shard_map/ppermute | solution.py:286
  1.1 0.0 copy-start
  1.1 1.0 %constant_dynamic-slice_fusion = (f32[4,2,16,128]{3,2,1,0:T(8,128)S(1)}, f32[4,2,16,128]{3,2,1,0:T(8,128)S(1)}, f32[4,2,16,128]{3,2,1,0:T(8,128)S(1)}, f32[4,2,16,128]{3,2,1,0:T(8,128)S(1)}) fusion(f32[4,2,64,128]{3,2,1,0:T(8,128)} %fields_ref.3, s32[]{:T(128)S(6)} %select_n.38, s32[]{:T(128)S(6)} %select_n.36, s32[]{:T(128)S(6)} %select_n.34, s32[]{:T(128)S(6)} %select_n.32), kind=kLoop, calls=%fused_computation.1 | loop fusion | bytes 524304 | tf_op jit(solution)/shard_map/dynamic_slice | solution.py:503
  2.2 0.4 %collective-permute-done.refs_3_ = f32[4,2,64,128]{3,2,1,0:T(8,128)S(1)} collective-permute-done((f32[4,2,64,128]{3,2,1,0:T(8,128)}, f32[4,2,64,128]{3,2,1,0:T(8,128)S(1)}, u32[]{:S(2)}, u32[]{:S(2)}) %collective-permute-start) | collective-permute-done | bytes 262176 | tf_op jit(solution)/shard_map/ppermute | solution.py:286
  2.5 0.0 copy-done
  2.5 0.0 copy-start.1
  2.5 0.0 copy-start.4
  2.5 0.0 copy-start.5
  2.5 0.0 copy-start.6
  2.5 0.0 copy-start.7
  2.6 2.9 %collective-permute-start.1 = (f32[2,4,2,64,128]{4,3,2,1,0:T(8,128)S(1)}, f32[2,4,2,64,128]{4,3,2,1,0:T(8,128)S(1)}, u32[]{:S(2)}, u32[]{:S(2)}) collective-permute-start(f32[2,4,2,64,128]{4,3,2,1,0:T(8,128)S(1)} %pad_maximum_fusion), channel_id=1, source_target_pairs={{0,8},{4,20},{8,0},{12,28},{16,24},{20,4},{24,16},{28,12},{1,9},{5... | collective-permute-start | bytes 1572872 | tf_op jit(solution)/shard_map/ppermute | solution.py:515
  5.5 1.5 %collective-permute-start.2 = (f32[4,2,64,128]{3,2,1,0:T(8,128)S(1)}, f32[4,2,64,128]{3,2,1,0:T(8,128)S(1)}, u32[]{:S(2)}, u32[]{:S(2)}) collective-permute-start(f32[4,2,64,128]{3,2,1,0:T(8,128)S(1)} %copy-done), channel_id=1, source_target_pairs={{0,24},{4,28},{8,16},{12,20},{16,8},{20,12},{24,0},{28,4},{1,25},{... | collective-permute-start | bytes 786440 | tf_op jit(solution)/shard_map/ppermute | solution.py:286
  7.0 1.6 %collective-permute-start.4 = (f32[4,2,16,128]{3,2,1,0:T(8,128)S(1)}, f32[4,2,16,128]{3,2,1,0:T(8,128)S(1)}, u32[]{:S(2)}, u32[]{:S(2)}) collective-permute-start(f32[4,2,16,128]{3,2,1,0:T(8,128)S(1)} %get-tuple-element.43), channel_id=1, source_target_pairs={{0,1},{1,2},{2,3},{3,0},{4,5},{5,6},{6,7},{7,4},{8,9},{9,10},{10,1... | collective-permute-start | bytes 196616 | tf_op jit(solution)/shard_map/ppermute | solution.py:493
  8.6 2.6 %collective-permute-start.5 = (f32[4,2,16,128]{3,2,1,0:T(8,128)S(1)}, f32[4,2,16,128]{3,2,1,0:T(8,128)S(1)}, u32[]{:S(2)}, u32[]{:S(2)}) collective-permute-start(f32[4,2,16,128]{3,2,1,0:T(8,128)S(1)} %get-tuple-element.44), channel_id=1, source_target_pairs={{0,2},{1,3},{2,0},{3,1},{4,6},{5,7},{6,4},{7,5},{8,10},{9,11},{10,... | collective-permute-start | bytes 196616 | tf_op jit(solution)/shard_map/ppermute | solution.py:493
  11.2 1.3 %collective-permute-start.6 = (f32[4,2,16,128]{3,2,1,0:T(8,128)S(1)}, f32[4,2,16,128]{3,2,1,0:T(8,128)S(1)}, u32[]{:S(2)}, u32[]{:S(2)}) collective-permute-start(f32[4,2,16,128]{3,2,1,0:T(8,128)S(1)} %get-tuple-element.45), channel_id=1, source_target_pairs={{0,3},{1,0},{2,1},{3,2},{4,7},{5,4},{6,5},{7,6},{8,11},{9,8},{10,9... | collective-permute-start | bytes 196616 | tf_op jit(solution)/shard_map/ppermute | solution.py:493
  13.2 0.0 copy-done.1
  13.2 0.0 copy-done.4
  13.2 0.0 copy-done.5
  13.2 0.0 copy-done.6
  13.2 0.0 copy-done.7
  13.2 0.0 copy-start.2
  13.3 0.0 copy-start.3
  13.3 3.1 %advance.1 = (f32[6,8192]{1,0:T(8,128)S(1)}, f32[3,8192]{1,0:T(4,128)S(1)}, f32[2,8,128]{2,1,0:T(8,128)S(1)}, f32[2,8,128]{2,1,0:T(8,128)S(1)}, f32[2,2,8,128]{3,2,1,0:T(8,128)S(1)}) custom-call(s32[1]{0:T(128)} %bitcast.row_ref.refs_0_, s32[1,1]{1,0:T(1,128)} %bitcast.10.count_ref, f32[4,2,64,128]{3,2,1,0:T(8,128)S(1)} %copy-done, f32[6,8192]{1,0:T(8,128)S(1)} %copy-done.1, ...), custom_call_target="tpu_custom_call" | custom-call | flops 1 | bytes 1 | tf_op jit(solution)/shard_map/advance/pallas_call | solution.py:190
  16.3 0.0 collective-permute-done.4.refs_1_
  16.4 0.0 copy-start.8
  16.4 0.7 %collective-permute-start.3 = (f32[2,8,128]{2,1,0:T(8,128)S(1)}, f32[2,8,128]{2,1,0:T(8,128)S(1)}, u32[]{:S(2)}, u32[]{:S(2)}) collective-permute-start(f32[2,8,128]{2,1,0:T(8,128)S(1)} %get-tuple-element.40), channel_id=1, source_target_pairs={{4,8},{12,16},{20,24},{8,4},{16,12},{24,20},{5,9},{13,17},{21,25},... | collective-permute-start | bytes 24584 | tf_op jit(solution)/shard_map/ppermute | solution.py:522
  17.1 0.0 collective-permute-done.5.refs_2_
  17.1 0.0 collective-permute-done.6.refs_3_
  17.1 0.0 copy-done.2
  17.1 0.0 copy-done.3
  17.1 0.0 copy-done.8
  17.1 0.0 copy-start.9
  17.1 0.6 %along_z.1 = (f32[128,128]{1,0:T(8,128)S(1)}, f32[144,128]{1,0:T(8,128)S(1)}, f32[128,128]{1,0:T(8,128)S(1)}, f32[144,128]{1,0:T(8,128)S(1)}) custom-call(f32[4]{0:T(128)S(1)} %copy-done.8, bf16[512,256]{1,0:T(8,128)(2,1)S(1)} %copy-done.2, bf16[512,256]{1,0:T(8,128)(2,1)S(1)} %copy-done.3, f32[2,2,8,128]{3,2,1,0:T(8,128)S(1)} %get-tuple-element.46.side_ref, ...), custom_call_target="tpu_custom_call" | custom-call | flops 1 | bytes 1 | tf_op jit(solution)/shard_map/along_z/pallas_call | solution.py:400
  17.8 0.7 %collective-permute-start.7 = (f32[144,128]{1,0:T(8,128)S(1)}, f32[144,128]{1,0:T(8,128)S(1)}, u32[]{:S(2)}, u32[]{:S(2)}) collective-permute-start(f32[144,128]{1,0:T(8,128)S(1)} %get-tuple-element.52), channel_id=1, source_target_pairs={{0,1},{1,2},{2,3},{3,0},{4,5},{5,6},{6,7},{7,4},{8,9},{9,10},{10,1... | collective-permute-start | bytes 221192 | tf_op jit(solution)/shard_map/ppermute | solution.py:493
  18.5 1.4 %collective-permute-start.8 = (f32[128,128]{1,0:T(8,128)S(1)}, f32[128,128]{1,0:T(8,128)S(1)}, u32[]{:S(2)}, u32[]{:S(2)}) collective-permute-start(f32[128,128]{1,0:T(8,128)S(1)} %get-tuple-element.53), channel_id=1, source_target_pairs={{0,2},{1,3},{2,0},{3,1},{4,6},{5,7},{6,4},{7,5},{8,10},{9,11},{10,... | collective-permute-start | bytes 196616 | tf_op jit(solution)/shard_map/ppermute | solution.py:493
  19.9 0.0 collective-permute-done.2.refs_5_
  19.9 0.0 copy-start.10
  19.9 3.5 %collective-permute-start.9 = (f32[144,128]{1,0:T(8,128)S(1)}, f32[144,128]{1,0:T(8,128)S(1)}, u32[]{:S(2)}, u32[]{:S(2)}) collective-permute-start(f32[144,128]{1,0:T(8,128)S(1)} %get-tuple-element.54), channel_id=1, source_target_pairs={{0,3},{1,0},{2,1},{3,2},{4,7},{5,4},{6,5},{7,6},{8,11},{9,8},{10,9... | collective-permute-start | bytes 221192 | tf_op jit(solution)/shard_map/ppermute | solution.py:493
  23.4 0.0 collective-permute-done.1.refs_4_
  23.4 0.0 copy-done.9
  23.4 0.0 copy-done.10
  23.4 3.2 %along_xy.1 = (f32[4,2,64,128]{3,2,1,0:T(8,128)S(1)}, f32[528,128]{1,0:T(8,128)S(1)}) custom-call(f32[4]{0:T(128)S(1)} %copy-done.8, f32[4,2,64,128]{3,2,1,0:T(8,128)S(1)} %copy-done, bf16[128,192]{1,0:T(8,128)(2,1)S(1)} %copy-done.9, s32[1,8192]{1,0:T(1,128)S(1)} %bitcast.17, f32[3,8192]{1,0:T(4,128)S(1)} %get-tuple-element.32.force_ref, ...), custom_call_target="tpu_custom_call" | custom-call | flops 20000000000 | bytes 100000000 | tf_op jit(solution)/shard_map/along_xy/pallas_call | solution.py:319
  26.6 0.7 %collective-permute-start.10 = (f32[528,128]{1,0:T(8,128)S(1)}, f32[528,128]{1,0:T(8,128)S(1)}, u32[]{:S(2)}, u32[]{:S(2)}) collective-permute-start(f32[528,128]{1,0:T(8,128)S(1)} %get-tuple-element.55), channel_id=1, source_target_pairs={{0,4},{4,0},{8,12},{12,8},{16,20},{20,16},{24,28},{28,24},{1,5},{5... | collective-permute-start | bytes 811016 | tf_op jit(solution)/shard_map/ppermute | solution.py:286
  27.3 0.0 collective-permute-done.8.refs_2_
  27.3 0.0 collective-permute-done.7.refs_1_
  27.3 0.0 collective-permute-done.9.refs_3_
  27.3 0.7 %stored.1 = f32[6,8192]{1,0:T(8,128)} custom-call(f32[6,8192]{1,0:T(8,128)S(1)} %get-tuple-element.57.source_ref), custom_call_target="tpu_custom_call" | custom-call | flops 1 | bytes 1 | tf_op jit(solution)/shard_map/stored/pallas_call | solution.py:338
  28.0 0.0 collective-permute-done.3.far_ref
  28.1 0.4 %collective-permute-done.10.near_ref = f32[528,128]{1,0:T(8,128)S(1)} collective-permute-done((f32[528,128]{1,0:T(8,128)S(1)}, f32[528,128]{1,0:T(8,128)S(1)}, u32[]{:S(2)}, u32[]{:S(2)}) %collective-permute-start.10) | collective-permute-done | bytes 270368 | tf_op jit(solution)/shard_map/ppermute | solution.py:286
  28.5 0.8 %total.1 = (f32[4,2,64,128]{3,2,1,0:T(8,128)}, f32[6,4,256]{2,1,0:T(4,128)}) custom-call(s32[1]{0:T(128)} %bitcast.row_ref.refs_0_, s32[1]{0:T(128)} %bitcast.1.column_ref, f32[4,2,64,128]{3,2,1,0:T(8,128)S(1)} %get-tuple-element.39.along_x_ref, f32[2,8,128]{2,1,0:T(8,128)S(1)} %collective-permute-done.3.far_ref, ...), custom_call_target="tpu_custom_call" | custom-call | flops 1 | bytes 1 | tf_op jit(solution)/shard_map/total/pallas_call | solution.py:478
  (2 shorter events, 0.0 us)
Async XLA Ops:
  0.6 1.9 %collective-permute-start = (f32[4,2,64,128]{3,2,1,0:T(8,128)}, f32[4,2,64,128]{3,2,1,0:T(8,128)S(1)}, u32[]{:S(2)}, u32[]{:S(2)}) collective-permute-start(f32[4,2,64,128]{3,2,1,0:T(8,128)} %fields_ref.3), channel_id=1, source_target_pairs={{0,4},{4,0},{8,12},{12,8},{16,20},{20,16},{24,28},{28,24},{1,5},{5... | collective-permute-start | bytes 786440 | tf_op jit(solution)/shard_map/ppermute | solution.py:286
  1.1 1.4 %copy-start = (f32[4,2,64,128]{3,2,1,0:T(8,128)S(1)}, f32[4,2,64,128]{3,2,1,0:T(8,128)}, u32[]{:S(2)}) copy-start(f32[4,2,64,128]{3,2,1,0:T(8,128)} %fields_ref.3) | copy-start | bytes 786436
  2.5 10.7 %copy-start.1 = (f32[6,8192]{1,0:T(8,128)S(1)}, f32[6,8192]{1,0:T(8,128)}, u32[]{:S(2)}) copy-start(f32[6,8192]{1,0:T(8,128)} %records_ref.1) | copy-start | bytes 589828
  2.5 10.7 %copy-start.4 = (f32[8192]{0:T(1024)S(1)}, f32[8192]{0:T(1024)}, u32[]{:S(2)}) copy-start(f32[8192]{0:T(1024)} %param.15) | copy-start | bytes 98308
  2.5 10.7 %copy-start.5 = (s32[8192]{0:T(1024)S(1)}, s32[8192]{0:T(1024)}, u32[]{:S(2)}) copy-start(s32[8192]{0:T(1024)} %param.18) | copy-start | bytes 98308
  2.5 10.7 %copy-start.6 = (s32[8192]{0:T(1024)S(1)}, s32[8192]{0:T(1024)}, u32[]{:S(2)}) copy-start(s32[8192]{0:T(1024)} %param.19) | copy-start | bytes 98308
  2.5 10.7 %copy-start.7 = (s32[8192]{0:T(1024)S(1)}, s32[8192]{0:T(1024)}, u32[]{:S(2)}) copy-start(s32[8192]{0:T(1024)} %param.16) | copy-start | bytes 98308
  2.6 20.8 %collective-permute-start.1 = (f32[2,4,2,64,128]{4,3,2,1,0:T(8,128)S(1)}, f32[2,4,2,64,128]{4,3,2,1,0:T(8,128)S(1)}, u32[]{:S(2)}, u32[]{:S(2)}) collective-permute-start(f32[2,4,2,64,128]{4,3,2,1,0:T(8,128)S(1)} %pad_maximum_fusion), channel_id=1, source_target_pairs={{0,8},{4,20},{8,0},{12,28},{16,24},{20,4},{24,16},{28,12},{1,9},{5... | collective-permute-start | bytes 1572872 | tf_op jit(solution)/shard_map/ppermute | solution.py:515
  5.5 14.4 %collective-permute-start.2 = (f32[4,2,64,128]{3,2,1,0:T(8,128)S(1)}, f32[4,2,64,128]{3,2,1,0:T(8,128)S(1)}, u32[]{:S(2)}, u32[]{:S(2)}) collective-permute-start(f32[4,2,64,128]{3,2,1,0:T(8,128)S(1)} %copy-done), channel_id=1, source_target_pairs={{0,24},{4,28},{8,16},{12,20},{16,8},{20,12},{24,0},{28,4},{1,25},{... | collective-permute-start | bytes 786440 | tf_op jit(solution)/shard_map/ppermute | solution.py:286
  7.0 9.3 %collective-permute-start.4 = (f32[4,2,16,128]{3,2,1,0:T(8,128)S(1)}, f32[4,2,16,128]{3,2,1,0:T(8,128)S(1)}, u32[]{:S(2)}, u32[]{:S(2)}) collective-permute-start(f32[4,2,16,128]{3,2,1,0:T(8,128)S(1)} %get-tuple-element.43), channel_id=1, source_target_pairs={{0,1},{1,2},{2,3},{3,0},{4,5},{5,6},{6,7},{7,4},{8,9},{9,10},{10,1... | collective-permute-start | bytes 196616 | tf_op jit(solution)/shard_map/ppermute | solution.py:493
  8.6 8.5 %collective-permute-start.5 = (f32[4,2,16,128]{3,2,1,0:T(8,128)S(1)}, f32[4,2,16,128]{3,2,1,0:T(8,128)S(1)}, u32[]{:S(2)}, u32[]{:S(2)}) collective-permute-start(f32[4,2,16,128]{3,2,1,0:T(8,128)S(1)} %get-tuple-element.44), channel_id=1, source_target_pairs={{0,2},{1,3},{2,0},{3,1},{4,6},{5,7},{6,4},{7,5},{8,10},{9,11},{10,... | collective-permute-start | bytes 196616 | tf_op jit(solution)/shard_map/ppermute | solution.py:493
  11.2 5.9 %collective-permute-start.6 = (f32[4,2,16,128]{3,2,1,0:T(8,128)S(1)}, f32[4,2,16,128]{3,2,1,0:T(8,128)S(1)}, u32[]{:S(2)}, u32[]{:S(2)}) collective-permute-start(f32[4,2,16,128]{3,2,1,0:T(8,128)S(1)} %get-tuple-element.45), channel_id=1, source_target_pairs={{0,3},{1,0},{2,1},{3,2},{4,7},{5,4},{6,5},{7,6},{8,11},{9,8},{10,9... | collective-permute-start | bytes 196616 | tf_op jit(solution)/shard_map/ppermute | solution.py:493
  13.2 3.8 %copy-start.2 = (bf16[512,256]{1,0:T(8,128)(2,1)S(1)}, bf16[512,256]{1,0:T(8,128)(2,1)}, u32[]{:S(2)}) copy-start(bf16[512,256]{1,0:T(8,128)(2,1)} %constant.52.clone.high_ref) | copy-start | bytes 786436
  13.3 3.8 %copy-start.3 = (bf16[512,256]{1,0:T(8,128)(2,1)S(1)}, bf16[512,256]{1,0:T(8,128)(2,1)}, u32[]{:S(2)}) copy-start(bf16[512,256]{1,0:T(8,128)(2,1)} %constant.53.clone.low_ref) | copy-start | bytes 786436
  16.4 0.7 %copy-start.8 = (f32[4]{0:T(128)S(1)}, f32[4]{0:T(128)}, u32[]{:S(2)}) copy-start(f32[4]{0:T(128)} %diffusivity_ref.1) | copy-start | bytes 52
  16.4 11.7 %collective-permute-start.3 = (f32[2,8,128]{2,1,0:T(8,128)S(1)}, f32[2,8,128]{2,1,0:T(8,128)S(1)}, u32[]{:S(2)}, u32[]{:S(2)}) collective-permute-start(f32[2,8,128]{2,1,0:T(8,128)S(1)} %get-tuple-element.40), channel_id=1, source_target_pairs={{4,8},{12,16},{20,24},{8,4},{16,12},{24,20},{5,9},{13,17},{21,25},... | collective-permute-start | bytes 24584 | tf_op jit(solution)/shard_map/ppermute | solution.py:522
  17.1 6.3 %copy-start.9 = (bf16[128,192]{1,0:T(8,128)(2,1)S(1)}, bf16[128,192]{1,0:T(8,128)(2,1)}, u32[]{:S(2)}) copy-start(bf16[128,192]{1,0:T(8,128)(2,1)} %constant.54.clone.operator_ref) | copy-start | bytes 147460
  17.8 9.6 %collective-permute-start.7 = (f32[144,128]{1,0:T(8,128)S(1)}, f32[144,128]{1,0:T(8,128)S(1)}, u32[]{:S(2)}, u32[]{:S(2)}) collective-permute-start(f32[144,128]{1,0:T(8,128)S(1)} %get-tuple-element.52), channel_id=1, source_target_pairs={{0,1},{1,2},{2,3},{3,0},{4,5},{5,6},{6,7},{7,4},{8,9},{9,10},{10,1... | collective-permute-start | bytes 221192 | tf_op jit(solution)/shard_map/ppermute | solution.py:493
  18.5 8.8 %collective-permute-start.8 = (f32[128,128]{1,0:T(8,128)S(1)}, f32[128,128]{1,0:T(8,128)S(1)}, u32[]{:S(2)}, u32[]{:S(2)}) collective-permute-start(f32[128,128]{1,0:T(8,128)S(1)} %get-tuple-element.53), channel_id=1, source_target_pairs={{0,2},{1,3},{2,0},{3,1},{4,6},{5,7},{6,4},{7,5},{8,10},{9,11},{10,... | collective-permute-start | bytes 196616 | tf_op jit(solution)/shard_map/ppermute | solution.py:493
  19.9 3.5 %copy-start.10 = (f32[512]{0:T(512)S(1)}, f32[512]{0:T(512)}, u32[]{:S(2)}) copy-start(f32[512]{0:T(512)} %constant.55.clone.refs_1_) | copy-start | bytes 6148
  19.9 7.4 %collective-permute-start.9 = (f32[144,128]{1,0:T(8,128)S(1)}, f32[144,128]{1,0:T(8,128)S(1)}, u32[]{:S(2)}, u32[]{:S(2)}) collective-permute-start(f32[144,128]{1,0:T(8,128)S(1)} %get-tuple-element.54), channel_id=1, source_target_pairs={{0,3},{1,0},{2,1},{3,2},{4,7},{5,4},{6,5},{7,6},{8,11},{9,8},{10,9... | collective-permute-start | bytes 221192 | tf_op jit(solution)/shard_map/ppermute | solution.py:493
  26.6 1.8 %collective-permute-start.10 = (f32[528,128]{1,0:T(8,128)S(1)}, f32[528,128]{1,0:T(8,128)S(1)}, u32[]{:S(2)}, u32[]{:S(2)}) collective-permute-start(f32[528,128]{1,0:T(8,128)S(1)} %get-tuple-element.55), channel_id=1, source_target_pairs={{0,4},{4,0},{8,12},{12,8},{16,20},{20,16},{24,28},{28,24},{1,5},{5... | collective-permute-start | bytes 811016 | tf_op jit(solution)/shard_map/ppermute | solution.py:286

commit v7 on v6

--- a/solution.py
+++ b/solution.py
@@ -199,7 +199,13 @@
     )(row, counts, fields, records, response, cell, destination, slot)
 
 
-def along_xy_kernel(chunk, viscous_ref, fields_ref, operator_ref, cell_ref, force_ref, *refs):
+def along_xy_kernel(chunk, diffusivity_ref, fields_ref, operator_ref, cell_ref, force_ref, *refs):
+    *refs, viscous_ref, weight_ref, sems = refs
+    fetches = [pltpu.make_async_copy(diffusivity_ref, viscous_ref, sems.at[0])]
+    if len(refs) > 2:
+        fetches.append(pltpu.make_async_copy(refs[1], weight_ref, sems.at[1]))
+    for fetch in fetches:
+        fetch.start()
     *y_refs, out_ref, total_ref = refs
     if y_refs:
         *y_refs, out_ref, sibling_ref, total_ref = refs
@@ -233,6 +239,8 @@
             return carry
 
         lax.fori_loop(0, particles // chunk, loop, 0)
+    for fetch in fetches:
+        fetch.wait()
     for component in range(parts):
         viscous = viscous_ref[component]
         for plane in range(planes):
@@ -255,7 +263,7 @@
                 out_ref[component, plane] = value
     if not y_refs:
         return
-    row_ref, weight_ref, near_ref, mate_ref, *others = y_refs
+    row_ref, _, near_ref, mate_ref, *others = y_refs
     both_ref, diagonal_ref = others
     blocks = [fields_ref, diagonal_ref, both_ref.at[0], both_ref.at[1]]
     size = parts * planes * width
@@ -314,14 +322,16 @@
     if y_part:
         row, near, mate, others = y_part
         y_part = (row, along_y_weights(lax.axis_size("row"), planes), near, mate, *others)
-        specs = [SMEM] * 2 + [VMEM] * (2 + len(others))
+        specs = [SMEM, pl.BlockSpec(memory_space=pl.ANY)] + [VMEM] * (2 + len(others))
         outs.append(any_space((fields.size // lanes + MIG // LANES * 8, lanes)))
     return pl.pallas_call(
         functools.partial(along_xy_kernel, chunk_of(particles, 2 * half)),
         out_shape=tuple(outs),
-        in_specs=[SMEM] + [VMEM] * 4 + specs,
+        in_specs=[pl.BlockSpec(memory_space=pl.ANY)] + [VMEM] * 4 + specs,
         out_specs=(VMEM,) * len(outs),
-        scratch_shapes=[pltpu.VMEM((6 * half, 2 * lanes), jnp.float32)],
+        scratch_shapes=[
+            pltpu.VMEM((6 * half, 2 * lanes), jnp.float32), pltpu.SMEM(viscous.shape, jnp.float32),
+            pltpu.SMEM(y_part[1].shape if y_part else (LANES,), jnp.float32), pltpu.SemaphoreType.DMA((2,))],
         compiler_params=params(40),
         cost_estimate=LONG,
         name="along_xy",

time: 29.4 us -> 29.1 us (0.990)
  Pallas kernels: 8.41 us -> 8.09 us
    pallas_call x1, Pallas kernels: 3.23 us -> 2.91 us  [along_xy(): pl.pallas_call(functools.partial(along_xy_kernel, chunk_of(particles, 2 *...]
  transfers between devices with their start and end apart: 11 -> 11, of which waited for: 2 -> 2; matrix products, arithmetic and copies ran while one was open for 3% -> 3% of each run, Pallas kernels for 26% -> 25%
where the time goes in v7:
time: 29.1 us; the launch traced here: 28.9 us
  starting transfers between devices  17.4 us (60%)
  Pallas kernels  8.09 us (28%)
  between operations  1.49 us (5%)
  local copies, waits for them, and re-layouts  1.06 us (4%)
  waiting for transfers between devices  0.83 us (3%)
    ppermute x6, starting transfers between devices, exchange(): lax.ppermute(blocks[s], 'col', [(i, (i + s) % count) for i in range(count)])  11.2 us
    pallas_call x1, Pallas kernels, advance(): pl.pallas_call(functools.partial(advance_kernel, chunk_of(particles, rows...  3.07 us
    ppermute x1, starting transfers between devices, on_device(): both = lax.ppermute(both, 'row', [(i, neighbour(i)) for i in range(rows)])  2.93 us
    pallas_call x1, Pallas kernels, along_xy(): pl.pallas_call(functools.partial(along_xy_kernel, chunk_of(particles, 2 *...  2.91 us
    ppermute x3, starting transfers between devices, same_core(): lax.ppermute(block, 'row', [(i, i ^ s) for i in range(lax.axis_size('row'...  2.67 us
    dynamic_slice x1, local copies, waits for them, and re-layouts, on_device(): lax.dynamic_slice_in_dim(fields, (column + s) % columns * width, width, a...  1 us
    ppermute x3, waiting for transfers between devices, same_core(): lax.ppermute(block, 'row', [(i, i ^ s) for i in range(lax.axis_size('row'...  0.79 us
    pallas_call x1, Pallas kernels, total(): pl.pallas_call(functools.partial(total_kernel, gathered), out_shape=(any_...  0.76 us
  transfers between devices with their start and end apart: 11, of which 2 were waited for; matrix products, arithmetic and copies ran while one was open for 3% of the time, Pallas kernels for 25%

profile of v7, /device:TPU:0, one launch (start us, length us, event | category | flops | bytes accessed | tf_op | source)
XLA Modules:
  0.0 28.9 jit_solution(18109202064347653221)
XLA Ops:
  0.6 0.5 %collective-permute-start = (f32[4,2,64,128]{3,2,1,0:T(8,128)}, f32[4,2,64,128]{3,2,1,0:T(8,128)S(1)}, u32[]{:S(2)}, u32[]{:S(2)}) collective-permute-start(f32[4,2,64,128]{3,2,1,0:T(8,128)} %fields_ref.3), channel_id=1, source_target_pairs={{0,4},{4,0},{8,12},{12,8},{16,20},{20,16},{24,28},{28,24},{1,5},{5... | collective-permute-start | bytes 786440 | tf_op jit(solution)/shard_map/ppermute | solution.py:294
  1.1 0.0 copy-start
  1.1 1.0 %constant_dynamic-slice_fusion = (f32[4,2,16,128]{3,2,1,0:T(8,128)S(1)}, f32[4,2,16,128]{3,2,1,0:T(8,128)S(1)}, f32[4,2,16,128]{3,2,1,0:T(8,128)S(1)}, f32[4,2,16,128]{3,2,1,0:T(8,128)S(1)}) fusion(f32[4,2,64,128]{3,2,1,0:T(8,128)} %fields_ref.3, s32[]{:T(128)S(6)} %select_n.38, s32[]{:T(128)S(6)} %select_n.36, s32[]{:T(128)S(6)} %select_n.34, s32[]{:T(128)S(6)} %select_n.32), kind=kLoop, calls=%fused_computation.1 | loop fusion | bytes 524304 | tf_op jit(solution)/shard_map/dynamic_slice | solution.py:513
  2.2 0.4 %collective-permute-done.refs_3_ = f32[4,2,64,128]{3,2,1,0:T(8,128)S(1)} collective-permute-done((f32[4,2,64,128]{3,2,1,0:T(8,128)}, f32[4,2,64,128]{3,2,1,0:T(8,128)S(1)}, u32[]{:S(2)}, u32[]{:S(2)}) %collective-permute-start) | collective-permute-done | bytes 262176 | tf_op jit(solution)/shard_map/ppermute | solution.py:294
  2.5 0.0 copy-done
  2.5 0.0 copy-start.1
  2.5 0.0 copy-start.4
  2.5 0.0 copy-start.5
  2.5 0.0 copy-start.6
  2.5 0.0 copy-start.7
  2.6 2.9 %collective-permute-start.1 = (f32[2,4,2,64,128]{4,3,2,1,0:T(8,128)S(1)}, f32[2,4,2,64,128]{4,3,2,1,0:T(8,128)S(1)}, u32[]{:S(2)}, u32[]{:S(2)}) collective-permute-start(f32[2,4,2,64,128]{4,3,2,1,0:T(8,128)S(1)} %pad_maximum_fusion), channel_id=1, source_target_pairs={{0,8},{4,20},{8,0},{12,28},{16,24},{20,4},{24,16},{28,12},{1,9},{5... | collective-permute-start | bytes 1572872 | tf_op jit(solution)/shard_map/ppermute | solution.py:525
  5.5 1.5 %collective-permute-start.2 = (f32[4,2,64,128]{3,2,1,0:T(8,128)S(1)}, f32[4,2,64,128]{3,2,1,0:T(8,128)S(1)}, u32[]{:S(2)}, u32[]{:S(2)}) collective-permute-start(f32[4,2,64,128]{3,2,1,0:T(8,128)S(1)} %copy-done), channel_id=1, source_target_pairs={{0,24},{4,28},{8,16},{12,20},{16,8},{20,12},{24,0},{28,4},{1,25},{... | collective-permute-start | bytes 786440 | tf_op jit(solution)/shard_map/ppermute | solution.py:294
  7.0 1.6 %collective-permute-start.4 = (f32[4,2,16,128]{3,2,1,0:T(8,128)S(1)}, f32[4,2,16,128]{3,2,1,0:T(8,128)S(1)}, u32[]{:S(2)}, u32[]{:S(2)}) collective-permute-start(f32[4,2,16,128]{3,2,1,0:T(8,128)S(1)} %get-tuple-element.43), channel_id=1, source_target_pairs={{0,1},{1,2},{2,3},{3,0},{4,5},{5,6},{6,7},{7,4},{8,9},{9,10},{10,1... | collective-permute-start | bytes 196616 | tf_op jit(solution)/shard_map/ppermute | solution.py:503
  8.6 2.6 %collective-permute-start.5 = (f32[4,2,16,128]{3,2,1,0:T(8,128)S(1)}, f32[4,2,16,128]{3,2,1,0:T(8,128)S(1)}, u32[]{:S(2)}, u32[]{:S(2)}) collective-permute-start(f32[4,2,16,128]{3,2,1,0:T(8,128)S(1)} %get-tuple-element.44), channel_id=1, source_target_pairs={{0,2},{1,3},{2,0},{3,1},{4,6},{5,7},{6,4},{7,5},{8,10},{9,11},{10,... | collective-permute-start | bytes 196616 | tf_op jit(solution)/shard_map/ppermute | solution.py:503
  11.2 1.3 %collective-permute-start.6 = (f32[4,2,16,128]{3,2,1,0:T(8,128)S(1)}, f32[4,2,16,128]{3,2,1,0:T(8,128)S(1)}, u32[]{:S(2)}, u32[]{:S(2)}) collective-permute-start(f32[4,2,16,128]{3,2,1,0:T(8,128)S(1)} %get-tuple-element.45), channel_id=1, source_target_pairs={{0,3},{1,0},{2,1},{3,2},{4,7},{5,4},{6,5},{7,6},{8,11},{9,8},{10,9... | collective-permute-start | bytes 196616 | tf_op jit(solution)/shard_map/ppermute | solution.py:503
  13.2 0.0 copy-done.1
  13.2 0.0 copy-done.4
  13.2 0.0 copy-done.5
  13.2 0.0 copy-done.6
  13.2 0.0 copy-done.7
  13.2 0.0 copy-start.2
  13.3 0.0 copy-start.3
  13.3 3.1 %advance.1 = (f32[6,8192]{1,0:T(8,128)S(1)}, f32[3,8192]{1,0:T(4,128)S(1)}, f32[2,8,128]{2,1,0:T(8,128)S(1)}, f32[2,8,128]{2,1,0:T(8,128)S(1)}, f32[2,2,8,128]{3,2,1,0:T(8,128)S(1)}) custom-call(s32[1]{0:T(128)} %bitcast.row_ref.refs_0_, s32[1,1]{1,0:T(1,128)} %bitcast.10.count_ref, f32[4,2,64,128]{3,2,1,0:T(8,128)S(1)} %copy-done, f32[6,8192]{1,0:T(8,128)S(1)} %copy-done.1, ...), custom_call_target="tpu_custom_call" | custom-call | flops 1 | bytes 1 | tf_op jit(solution)/shard_map/advance/pallas_call | solution.py:190
  16.3 0.0 collective-permute-done.4.refs_1_
  16.4 0.0 copy-start.8
  16.4 0.7 %collective-permute-start.3 = (f32[2,8,128]{2,1,0:T(8,128)S(1)}, f32[2,8,128]{2,1,0:T(8,128)S(1)}, u32[]{:S(2)}, u32[]{:S(2)}) collective-permute-start(f32[2,8,128]{2,1,0:T(8,128)S(1)} %get-tuple-element.40), channel_id=1, source_target_pairs={{4,8},{12,16},{20,24},{8,4},{16,12},{24,20},{5,9},{13,17},{21,25},... | collective-permute-start | bytes 24584 | tf_op jit(solution)/shard_map/ppermute | solution.py:532
  17.1 0.0 collective-permute-done.5.refs_2_
  17.1 0.0 collective-permute-done.6.refs_3_
  17.1 0.0 copy-done.2
  17.1 0.0 copy-done.3
  17.1 0.0 copy-done.8
  17.1 0.0 copy-start.9
  17.1 0.6 %along_z.1 = (f32[128,128]{1,0:T(8,128)S(1)}, f32[144,128]{1,0:T(8,128)S(1)}, f32[128,128]{1,0:T(8,128)S(1)}, f32[144,128]{1,0:T(8,128)S(1)}) custom-call(f32[4]{0:T(128)S(1)} %copy-done.8, bf16[512,256]{1,0:T(8,128)(2,1)S(1)} %copy-done.2, bf16[512,256]{1,0:T(8,128)(2,1)S(1)} %copy-done.3, f32[2,2,8,128]{3,2,1,0:T(8,128)S(1)} %get-tuple-element.46.side_ref, ...), custom_call_target="tpu_custom_call" | custom-call | flops 1 | bytes 1 | tf_op jit(solution)/shard_map/along_z/pallas_call | solution.py:410
  17.8 0.7 %collective-permute-start.7 = (f32[144,128]{1,0:T(8,128)S(1)}, f32[144,128]{1,0:T(8,128)S(1)}, u32[]{:S(2)}, u32[]{:S(2)}) collective-permute-start(f32[144,128]{1,0:T(8,128)S(1)} %get-tuple-element.52), channel_id=1, source_target_pairs={{0,1},{1,2},{2,3},{3,0},{4,5},{5,6},{6,7},{7,4},{8,9},{9,10},{10,1... | collective-permute-start | bytes 221192 | tf_op jit(solution)/shard_map/ppermute | solution.py:503
  18.5 1.4 %collective-permute-start.8 = (f32[128,128]{1,0:T(8,128)S(1)}, f32[128,128]{1,0:T(8,128)S(1)}, u32[]{:S(2)}, u32[]{:S(2)}) collective-permute-start(f32[128,128]{1,0:T(8,128)S(1)} %get-tuple-element.53), channel_id=1, source_target_pairs={{0,2},{1,3},{2,0},{3,1},{4,6},{5,7},{6,4},{7,5},{8,10},{9,11},{10,... | collective-permute-start | bytes 196616 | tf_op jit(solution)/shard_map/ppermute | solution.py:503
  19.9 0.0 collective-permute-done.2.refs_5_
  19.9 0.0 copy-start.10
  19.9 3.5 %collective-permute-start.9 = (f32[144,128]{1,0:T(8,128)S(1)}, f32[144,128]{1,0:T(8,128)S(1)}, u32[]{:S(2)}, u32[]{:S(2)}) collective-permute-start(f32[144,128]{1,0:T(8,128)S(1)} %get-tuple-element.54), channel_id=1, source_target_pairs={{0,3},{1,0},{2,1},{3,2},{4,7},{5,4},{6,5},{7,6},{8,11},{9,8},{10,9... | collective-permute-start | bytes 221192 | tf_op jit(solution)/shard_map/ppermute | solution.py:503
  23.4 0.0 collective-permute-done.1.refs_4_
  23.4 0.0 copy-done.9
  23.4 0.0 copy-done.10
  23.4 2.9 %along_xy.1 = (f32[4,2,64,128]{3,2,1,0:T(8,128)S(1)}, f32[528,128]{1,0:T(8,128)S(1)}) custom-call(f32[4]{0:T(128)S(1)} %copy-done.8, f32[4,2,64,128]{3,2,1,0:T(8,128)S(1)} %copy-done, bf16[128,192]{1,0:T(8,128)(2,1)S(1)} %copy-done.9, s32[1,8192]{1,0:T(1,128)S(1)} %bitcast.17, f32[3,8192]{1,0:T(4,128)S(1)} %get-tuple-element.32.force_ref, ...), custom_call_target="tpu_custom_call" | custom-call | flops 20000000000 | bytes 100000000 | tf_op jit(solution)/shard_map/along_xy/pallas_call | solution.py:327
  26.3 0.7 %collective-permute-start.10 = (f32[528,128]{1,0:T(8,128)S(1)}, f32[528,128]{1,0:T(8,128)S(1)}, u32[]{:S(2)}, u32[]{:S(2)}) collective-permute-start(f32[528,128]{1,0:T(8,128)S(1)} %get-tuple-element.55), channel_id=1, source_target_pairs={{0,4},{4,0},{8,12},{12,8},{16,20},{20,16},{24,28},{28,24},{1,5},{5... | collective-permute-start | bytes 811016 | tf_op jit(solution)/shard_map/ppermute | solution.py:294
  27.0 0.0 collective-permute-done.8.refs_2_
  27.0 0.0 collective-permute-done.7.refs_1_
  27.0 0.0 collective-permute-done.9.refs_3_
  27.0 0.7 %stored.1 = f32[6,8192]{1,0:T(8,128)} custom-call(f32[6,8192]{1,0:T(8,128)S(1)} %get-tuple-element.57.source_ref), custom_call_target="tpu_custom_call" | custom-call | flops 1 | bytes 1 | tf_op jit(solution)/shard_map/stored/pallas_call | solution.py:348
  27.7 0.0 collective-permute-done.3.far_ref
  27.7 0.4 %collective-permute-done.10.near_ref = f32[528,128]{1,0:T(8,128)S(1)} collective-permute-done((f32[528,128]{1,0:T(8,128)S(1)}, f32[528,128]{1,0:T(8,128)S(1)}, u32[]{:S(2)}, u32[]{:S(2)}) %collective-permute-start.10) | collective-permute-done | bytes 270368 | tf_op jit(solution)/shard_map/ppermute | solution.py:294
  28.2 0.8 %total.1 = (f32[4,2,64,128]{3,2,1,0:T(8,128)}, f32[6,4,256]{2,1,0:T(4,128)}) custom-call(s32[1]{0:T(128)} %bitcast.row_ref.refs_0_, s32[1]{0:T(128)} %bitcast.1.column_ref, f32[4,2,64,128]{3,2,1,0:T(8,128)S(1)} %get-tuple-element.39.along_x_ref, f32[2,8,128]{2,1,0:T(8,128)S(1)} %collective-permute-done.3.far_ref, ...), custom_call_target="tpu_custom_call" | custom-call | flops 1 | bytes 1 | tf_op jit(solution)/shard_map/total/pallas_call | solution.py:488
  (2 shorter events, 0.0 us)
Async XLA Ops:
  0.6 1.9 %collective-permute-start = (f32[4,2,64,128]{3,2,1,0:T(8,128)}, f32[4,2,64,128]{3,2,1,0:T(8,128)S(1)}, u32[]{:S(2)}, u32[]{:S(2)}) collective-permute-start(f32[4,2,64,128]{3,2,1,0:T(8,128)} %fields_ref.3), channel_id=1, source_target_pairs={{0,4},{4,0},{8,12},{12,8},{16,20},{20,16},{24,28},{28,24},{1,5},{5... | collective-permute-start | bytes 786440 | tf_op jit(solution)/shard_map/ppermute | solution.py:294
  1.1 1.4 %copy-start = (f32[4,2,64,128]{3,2,1,0:T(8,128)S(1)}, f32[4,2,64,128]{3,2,1,0:T(8,128)}, u32[]{:S(2)}) copy-start(f32[4,2,64,128]{3,2,1,0:T(8,128)} %fields_ref.3) | copy-start | bytes 786436
  2.5 10.7 %copy-start.1 = (f32[6,8192]{1,0:T(8,128)S(1)}, f32[6,8192]{1,0:T(8,128)}, u32[]{:S(2)}) copy-start(f32[6,8192]{1,0:T(8,128)} %records_ref.1) | copy-start | bytes 589828
  2.5 10.7 %copy-start.4 = (f32[8192]{0:T(1024)S(1)}, f32[8192]{0:T(1024)}, u32[]{:S(2)}) copy-start(f32[8192]{0:T(1024)} %param.15) | copy-start | bytes 98308
  2.5 10.7 %copy-start.5 = (s32[8192]{0:T(1024)S(1)}, s32[8192]{0:T(1024)}, u32[]{:S(2)}) copy-start(s32[8192]{0:T(1024)} %param.18) | copy-start | bytes 98308
  2.5 10.7 %copy-start.6 = (s32[8192]{0:T(1024)S(1)}, s32[8192]{0:T(1024)}, u32[]{:S(2)}) copy-start(s32[8192]{0:T(1024)} %param.19) | copy-start | bytes 98308
  2.5 10.7 %copy-start.7 = (s32[8192]{0:T(1024)S(1)}, s32[8192]{0:T(1024)}, u32[]{:S(2)}) copy-start(s32[8192]{0:T(1024)} %param.16) | copy-start | bytes 98308
  2.6 20.8 %collective-permute-start.1 = (f32[2,4,2,64,128]{4,3,2,1,0:T(8,128)S(1)}, f32[2,4,2,64,128]{4,3,2,1,0:T(8,128)S(1)}, u32[]{:S(2)}, u32[]{:S(2)}) collective-permute-start(f32[2,4,2,64,128]{4,3,2,1,0:T(8,128)S(1)} %pad_maximum_fusion), channel_id=1, source_target_pairs={{0,8},{4,20},{8,0},{12,28},{16,24},{20,4},{24,16},{28,12},{1,9},{5... | collective-permute-start | bytes 1572872 | tf_op jit(solution)/shard_map/ppermute | solution.py:525
  5.5 14.4 %collective-permute-start.2 = (f32[4,2,64,128]{3,2,1,0:T(8,128)S(1)}, f32[4,2,64,128]{3,2,1,0:T(8,128)S(1)}, u32[]{:S(2)}, u32[]{:S(2)}) collective-permute-start(f32[4,2,64,128]{3,2,1,0:T(8,128)S(1)} %copy-done), channel_id=1, source_target_pairs={{0,24},{4,28},{8,16},{12,20},{16,8},{20,12},{24,0},{28,4},{1,25},{... | collective-permute-start | bytes 786440 | tf_op jit(solution)/shard_map/ppermute | solution.py:294
  7.0 9.3 %collective-permute-start.4 = (f32[4,2,16,128]{3,2,1,0:T(8,128)S(1)}, f32[4,2,16,128]{3,2,1,0:T(8,128)S(1)}, u32[]{:S(2)}, u32[]{:S(2)}) collective-permute-start(f32[4,2,16,128]{3,2,1,0:T(8,128)S(1)} %get-tuple-element.43), channel_id=1, source_target_pairs={{0,1},{1,2},{2,3},{3,0},{4,5},{5,6},{6,7},{7,4},{8,9},{9,10},{10,1... | collective-permute-start | bytes 196616 | tf_op jit(solution)/shard_map/ppermute | solution.py:503
  8.6 8.5 %collective-permute-start.5 = (f32[4,2,16,128]{3,2,1,0:T(8,128)S(1)}, f32[4,2,16,128]{3,2,1,0:T(8,128)S(1)}, u32[]{:S(2)}, u32[]{:S(2)}) collective-permute-start(f32[4,2,16,128]{3,2,1,0:T(8,128)S(1)} %get-tuple-element.44), channel_id=1, source_target_pairs={{0,2},{1,3},{2,0},{3,1},{4,6},{5,7},{6,4},{7,5},{8,10},{9,11},{10,... | collective-permute-start | bytes 196616 | tf_op jit(solution)/shard_map/ppermute | solution.py:503
  11.2 5.9 %collective-permute-start.6 = (f32[4,2,16,128]{3,2,1,0:T(8,128)S(1)}, f32[4,2,16,128]{3,2,1,0:T(8,128)S(1)}, u32[]{:S(2)}, u32[]{:S(2)}) collective-permute-start(f32[4,2,16,128]{3,2,1,0:T(8,128)S(1)} %get-tuple-element.45), channel_id=1, source_target_pairs={{0,3},{1,0},{2,1},{3,2},{4,7},{5,4},{6,5},{7,6},{8,11},{9,8},{10,9... | collective-permute-start | bytes 196616 | tf_op jit(solution)/shard_map/ppermute | solution.py:503
  13.2 3.8 %copy-start.2 = (bf16[512,256]{1,0:T(8,128)(2,1)S(1)}, bf16[512,256]{1,0:T(8,128)(2,1)}, u32[]{:S(2)}) copy-start(bf16[512,256]{1,0:T(8,128)(2,1)} %constant.52.clone.high_ref) | copy-start | bytes 786436
  13.3 3.8 %copy-start.3 = (bf16[512,256]{1,0:T(8,128)(2,1)S(1)}, bf16[512,256]{1,0:T(8,128)(2,1)}, u32[]{:S(2)}) copy-start(bf16[512,256]{1,0:T(8,128)(2,1)} %constant.53.clone.low_ref) | copy-start | bytes 786436
  16.4 0.7 %copy-start.8 = (f32[4]{0:T(128)S(1)}, f32[4]{0:T(128)}, u32[]{:S(2)}) copy-start(f32[4]{0:T(128)} %diffusivity_ref.3) | copy-start | bytes 52
  16.4 11.4 %collective-permute-start.3 = (f32[2,8,128]{2,1,0:T(8,128)S(1)}, f32[2,8,128]{2,1,0:T(8,128)S(1)}, u32[]{:S(2)}, u32[]{:S(2)}) collective-permute-start(f32[2,8,128]{2,1,0:T(8,128)S(1)} %get-tuple-element.40), channel_id=1, source_target_pairs={{4,8},{12,16},{20,24},{8,4},{16,12},{24,20},{5,9},{13,17},{21,25},... | collective-permute-start | bytes 24584 | tf_op jit(solution)/shard_map/ppermute | solution.py:532
  17.1 6.3 %copy-start.9 = (bf16[128,192]{1,0:T(8,128)(2,1)S(1)}, bf16[128,192]{1,0:T(8,128)(2,1)}, u32[]{:S(2)}) copy-start(bf16[128,192]{1,0:T(8,128)(2,1)} %constant.54.clone.operator_ref) | copy-start | bytes 147460
  17.8 9.2 %collective-permute-start.7 = (f32[144,128]{1,0:T(8,128)S(1)}, f32[144,128]{1,0:T(8,128)S(1)}, u32[]{:S(2)}, u32[]{:S(2)}) collective-permute-start(f32[144,128]{1,0:T(8,128)S(1)} %get-tuple-element.52), channel_id=1, source_target_pairs={{0,1},{1,2},{2,3},{3,0},{4,5},{5,6},{6,7},{7,4},{8,9},{9,10},{10,1... | collective-permute-start | bytes 221192 | tf_op jit(solution)/shard_map/ppermute | solution.py:503
  18.5 8.5 %collective-permute-start.8 = (f32[128,128]{1,0:T(8,128)S(1)}, f32[128,128]{1,0:T(8,128)S(1)}, u32[]{:S(2)}, u32[]{:S(2)}) collective-permute-start(f32[128,128]{1,0:T(8,128)S(1)} %get-tuple-element.53), channel_id=1, source_target_pairs={{0,2},{1,3},{2,0},{3,1},{4,6},{5,7},{6,4},{7,5},{8,10},{9,11},{10,... | collective-permute-start | bytes 196616 | tf_op jit(solution)/shard_map/ppermute | solution.py:503
  19.9 3.5 %copy-start.10 = (f32[512]{0:T(512)S(1)}, f32[512]{0:T(512)}, u32[]{:S(2)}) copy-start(f32[512]{0:T(512)} %constant.55.clone.refs_1_) | copy-start | bytes 6148
  19.9 7.1 %collective-permute-start.9 = (f32[144,128]{1,0:T(8,128)S(1)}, f32[144,128]{1,0:T(8,128)S(1)}, u32[]{:S(2)}, u32[]{:S(2)}) collective-permute-start(f32[144,128]{1,0:T(8,128)S(1)} %get-tuple-element.54), channel_id=1, source_target_pairs={{0,3},{1,0},{2,1},{3,2},{4,7},{5,4},{6,5},{7,6},{8,11},{9,8},{10,9... | collective-permute-start | bytes 221192 | tf_op jit(solution)/shard_map/ppermute | solution.py:503
  26.3 1.8 %collective-permute-start.10 = (f32[528,128]{1,0:T(8,128)S(1)}, f32[528,128]{1,0:T(8,128)S(1)}, u32[]{:S(2)}, u32[]{:S(2)}) collective-permute-start(f32[528,128]{1,0:T(8,128)S(1)} %get-tuple-element.55), channel_id=1, source_target_pairs={{0,4},{4,0},{8,12},{12,8},{16,20},{20,16},{24,28},{28,24},{1,5},{5... | collective-permute-start | bytes 811016 | tf_op jit(solution)/shard_map/ppermute | solution.py:294
